TPU v7x, 128 devices: a whole 4x4x4 slice. The times are simulated.
128 devices in a mesh: row: 8 (over y_hi, x), col: 16 (over y_lo, z, core).
Axes of the slice: x: 4, y: 4 (y_hi: 2, y_lo: 2; y = y_hi * 2 + y_lo), z: 4, core: 2. Of those that a mesh axis runs over, the one named last changes fastest.
Arguments:
- trailing_grad: bfloat16 [8, 16, 192, 24576], P(None, 'col', None, 'row'), may hold values from -6 to 6
- panel: bfloat16 [24576, 512], P(('row', 'col')), may hold values from -0.0390625 to 0.0390625
- panel_grad: float32 [24576, 512], P(('row', 'col')), may hold values from -6 to 6
- diag_factor: float32 [512, 512], replicated, may hold values from -2 to 2, as said below
- diag_grad: float32 [512, 512], replicated, may hold values from -6 to 6
Outputs:
- panel_adj: float32 [24576, 512], P(('row', 'col'))
- diag_adj: float32 [512, 512], replicated
Inputs may be any that keep to these rules, and one draw needn't show every extreme that they name: `diag_factor`: lower triangular with zeros above the diagonal; diagonal entries between 1 and 2.
All inputs are finite; a program needn't handle non-finite values.
Results may differ from a plain program's by a relative error of at most 0.0003.
Values may be sent and summed in bfloat16 or wider, within the bound.
No kernel may reach another device: no remote copies, remote signals or barrier semaphores. Data moves between devices by JAX's collectives and lax.ppermute only.
A program may use at most 64 MiB of HBM per device.

v0:
```python
import jax
import jax.numpy as jnp
from jax import lax
from jax.sharding import PartitionSpec as P


def halve_lower(matrix):
    rows = lax.broadcasted_iota(jnp.int32, matrix.shape, 0)
    cols = lax.broadcasted_iota(jnp.int32, matrix.shape, 1)
    keep = jnp.where(rows > cols, 1.0, jnp.where(rows == cols, 0.5, 0.0)).astype(jnp.float32)
    return matrix * keep


def keep_lower(matrix):
    rows = lax.broadcasted_iota(jnp.int32, matrix.shape, 0)
    cols = lax.broadcasted_iota(jnp.int32, matrix.shape, 1)
    return jnp.where(rows >= cols, matrix, 0.0)


def right_solve(left, lower):
    right = jax.scipy.linalg.solve_triangular(lower, left.T, lower=True, trans=1).T
    return 0.5 * (right + right.T)


def on_device(trailing_grad, panel, panel_grad, diag_factor, diag_grad):
    local_flip = trailing_grad.reshape(-1, trailing_grad.shape[3])
    lower = jnp.tril(diag_factor)
    col_panel = lax.all_gather(panel, "row", axis=0, tiled=True)
    row_panel = lax.all_gather(panel, "col", axis=0, tiled=True)
    block = local_flip
    direct = lax.psum_scatter(
        lax.dot_general(
            block, col_panel, (((0,), (0,)), ((), ())), preferred_element_type=jnp.float32
        ),
        "col",
        scatter_dimension=0,
        tiled=True,
    )
    block = local_flip
    transposed = lax.psum_scatter(
        jnp.dot(block, row_panel, preferred_element_type=jnp.float32),
        "row",
        scatter_dimension=0,
        tiled=True,
    )
    reduced = panel_grad - direct - transposed
    panel_adj = jax.scipy.linalg.solve_triangular(lower, reduced.T, lower=True, trans=1).T
    contrib = lax.dot_general(
        panel_adj,
        panel.astype(jnp.float32),
        (((0,), (0,)), ((), ())),
        precision=lax.Precision.HIGHEST,
    )
    diag_new = diag_grad - lax.psum(contrib, ("row", "col"))
    inner = halve_lower(jnp.dot(lower.T, keep_lower(diag_new), precision=lax.Precision.HIGHEST))
    left = jax.scipy.linalg.solve_triangular(lower, inner, lower=True, trans=1)
    return (panel_adj, right_solve(left, lower))


def solution(mesh):
    in_specs = (
        P(None, "col", None, "row"),
        P(("row", "col"), None),
        P(("row", "col"), None),
        P(),
        P(),
    )
    out_specs = (P(("row", "col"), None), P())
    return jax.shard_map(
        on_device, mesh=mesh, in_specs=in_specs, out_specs=out_specs, check_vma=False
    )
```

profile of v0, /device:TPU:8, one launch (start us, length us, event | category | flops | bytes accessed | tf_op | source)
XLA Modules:
  0.0 427.2 jit_solution(13703523502560808614)
XLA Ops:
  7.2 0.7 all-gather.5.cloned.1.call-update
  7.9 0.7 all-gather.3.cloned.1.call-update
  8.7 38.9 %all-gather.5.cloned.1.call-done = bf16[3072,512]{1,0:T(8,128)(2,1)} async-done(((bf16[192,512]{1,0:T(8,128)(2,1)}), bf16[3072,512]{1,0:T(8,128)(2,1)}) %all-gather.5.cloned.1.call-update) | async-done | bytes 3145744 | tf_op jit(solution)/shard_map/all_gather | solution.py:29
  47.6 10.7 %fusion.67 = f32[1536,512]{1,0:T(8,128)} fusion(bf16[1536,3072]{1,0:T(8,128)(2,1)} %bitcast.70, bf16[3072,512]{1,0:T(8,128)(2,1)} %all-gather.5.cloned.1.call-done), kind=kOutput, calls=%fused_computation.91 | convolution fusion | flops 4831838208 | bytes 15728640 | tf_op jit(solution)/shard_map/dot_general | solution.py:41
  58.4 42.3 %all-gather.3.cloned.1.call-done = bf16[1536,512]{1,0:T(8,128)(2,1)} async-done(((bf16[192,512]{1,0:T(8,128)(2,1)}), bf16[1536,512]{1,0:T(8,128)(2,1)}) %all-gather.3.cloned.1.call-update) | async-done | bytes 1572880 | tf_op jit(solution)/shard_map/all_gather | solution.py:28
  100.6 9.8 %fusion.66 = f32[3072,512]{1,0:T(8,128)} fusion(bf16[1536,3072]{1,0:T(8,128)(2,1)} %bitcast.71, bf16[1536,512]{1,0:T(8,128)(2,1)} %all-gather.3.cloned.1.call-done), kind=kOutput, calls=%fused_computation.90 | convolution fusion | flops 4831838208 | bytes 17301504 | tf_op jit(solution)/shard_map/dot_general | solution.py:32
  110.6 1.1 copy-done.1
  111.7 0.1 fusion.2
  111.8 8.3 %while.5 = (s32[]{:T(128)}, f32[512,512]{1,0:T(8,128)S(1)}, s32[4,2]{0,1:T(2,128)S(1)}, f32[4,128,128]{2,1,0:T(8,128)S(1)}, s32[]{:T(128)}) while((s32[]{:T(128)}, f32[512,512]{1,0:T(8,128)S(1)}, s32[4,2]{0,1:T(2,128)S(1)}, f32[4,128,128]{2,1,0:T(8,128)S(1)}, s32[]{:T(128)}) %tuple.31), condition=%wide.while_cond.1, body=%wide.while_body.1.sunk | while | flops 2 | bytes 131189 | solution.py:47
  111.9 0.6 fusion.86
  112.5 1.4 bitcast_dynamic-update-slice_fusion.2
  114.0 0.6 fusion.86
  114.6 1.4 bitcast_dynamic-update-slice_fusion.2
  116.1 0.6 fusion.86
  116.7 1.4 bitcast_dynamic-update-slice_fusion.2
  118.2 0.6 fusion.86
  118.7 1.4 bitcast_dynamic-update-slice_fusion.2
  120.2 39.5 %custom-call.7 = f32[4,128,128]{1,2,0:T(8,128)S(1)} custom-call(f32[4,128,128]{2,1,0:T(8,128)S(1)} %get-tuple-element.18), custom_call_target="InvertDiagBlocksLowerTriangular" | custom-call | tf_op jit(solution)/shard_map/jit(_solve_triangular)/triangular_solve | solution.py:47
  159.7 24.1 %reduce-scatter.5.cloned.1.call-done = f32[192,512]{1,0:T(8,128)} async-done(((f32[1536,512]{1,0:T(8,128)}), f32[192,512]{1,0:T(8,128)}) %reduce-scatter.5.cloned.1.call-update) | async-done | bytes 393232 | tf_op jit(solution)/shard_map/reduce_scatter | solution.py:40
  183.8 72.1 %reduce-scatter.3.cloned.1.call-done = f32[192,512]{1,0:T(8,128)} async-done(((f32[3072,512]{1,0:T(8,128)}), f32[192,512]{1,0:T(8,128)}) %reduce-scatter.3.cloned.1.call-update) | async-done | bytes 393232 | tf_op jit(solution)/shard_map/reduce_scatter | solution.py:31
  255.9 1.2 subtract_bitcast_fusion
  257.1 0.3 fusion.43
  257.4 0.2 convolution_subtract_fusion.6
  257.6 0.3 fusion.53
  257.9 0.3 convolution_subtract_fusion.8
  258.2 0.3 fusion.50
  258.5 0.4 convolution_subtract_fusion.7
  258.9 0.3 fusion.47
  259.2 1.6 fusion.32
  260.9 0.8 fusion.33
  261.6 146.3 %all-reduce.2.cloned.1.call-done = f32[512,512]{1,0:T(8,128)} async-done(((f32[512,512]{1,0:T(8,128)}), f32[512,512]{1,0:T(8,128)}) %all-reduce.2.cloned.1.call-update) | async-done | bytes 1048592 | tf_op jit(solution)/shard_map/psum | solution.py:54
  407.9 3.4 convolution_multiply_fusion
  411.4 0.4 fusion.30
  411.7 0.4 convolution_subtract_fusion.3
  412.2 0.4 fusion.52
  412.5 0.5 convolution_subtract_fusion.2
  413.0 0.4 fusion.49
  413.4 0.7 convolution_subtract_fusion.5
  414.1 0.4 fusion.45
  414.5 0.4 fusion.28
  414.9 0.6 convolution_subtract_fusion.1
  415.5 0.4 fusion.51
  415.9 1.0 convolution_subtract_fusion
  416.9 0.4 fusion.48
  417.3 1.5 convolution_subtract_fusion.4
  418.7 0.4 fusion.46
  419.2 0.3 copy.7
  419.5 1.2 add_multiply_fusion
  (22 shorter events, 0.7 us)
Async XLA Ops:
  7.2 40.5 %all-gather.5.cloned.1.call-start = ((), (), s32[]{:S(2)}) async-start(), calls=%async_computation.4 | async-start | bytes 3342336 | tf_op jit(solution)/shard_map/all_gather | solution.py:29
  7.9 92.7 %all-gather.3.cloned.1.call-start = ((), (), s32[]{:S(2)}) async-start(), calls=%async_computation.2 | async-start | bytes 1769472 | tf_op jit(solution)/shard_map/all_gather | solution.py:28
  8.6 175.1 %reduce-scatter.5.cloned.1.call-start = ((), (), s32[]{:S(2)}) async-start(), calls=%async_computation.5 | async-start | bytes 3538944 | tf_op jit(solution)/shard_map/reduce_scatter | solution.py:40
  58.3 197.6 %reduce-scatter.3.cloned.1.call-start = ((), (), s32[]{:S(2)}) async-start(), calls=%async_computation.3 | async-start | bytes 6684672 | tf_op jit(solution)/shard_map/reduce_scatter | solution.py:31
  110.5 1.2 copy-start.1
  110.5 145.4 %copy-start.2 = (f32[192,512]{1,0:T(8,128)S(1)}, f32[192,512]{1,0:T(8,128)}, u32[]{:S(2)}) copy-start(f32[192,512]{1,0:T(8,128)} %param.9) | copy-start | bytes 1179652
  110.5 297.5 %all-reduce.2.cloned.1.call-start = ((), (), s32[]{:S(2)}) async-start(), calls=%async_computation.6 | async-start | bytes 2097152 | tf_op jit(solution)/shard_map/psum | solution.py:54
  111.7 147.5 %copy-start = (bf16[192,512]{1,0:T(8,128)(2,1)S(1)}, bf16[192,512]{1,0:T(8,128)(2,1)}, u32[]{:S(2)}) copy-start(bf16[192,512]{1,0:T(8,128)(2,1)} %param.8) | copy-start | bytes 589828
Sparse Core Ops, SparseCore 0:
  9.7 37.8 all-gather.4
  49.9 50.6 all-gather.2
  104.5 79.1 reduce-scatter.4
  186.2 69.6 reduce-scatter.2
  261.8 146.0 all-reduce.1
where the time goes:
time: 429 us; the launch traced here: 427 us
  waiting for transfers between devices  325 us (76%)
  other arithmetic  42.9 us (10%)
  matrix products  35.2 us (8%)
  between operations  14 us (3%)
  local copies, waits for them, and re-layouts  9.72 us (2%)
    psum x1, waiting for transfers between devices, on_device(): diag_new = diag_grad - lax.psum(contrib, ('row', 'col'))  146 us
    reduce_scatter x1, waiting for transfers between devices, on_device(): lax.psum_scatter(lax.dot_general(block, col_panel, (((0,), (0,)), ((), ()...  72.1 us
    all_gather x1, waiting for transfers between devices, on_device(): col_panel = lax.all_gather(panel, 'row', axis=0, tiled=True)  42.3 us
    another operation x3, other arithmetic, on_device(): jax.scipy.linalg.solve_triangular(lower, reduced.T, lower=True, trans=1)  39.6 us
    all_gather x1, waiting for transfers between devices, on_device(): row_panel = lax.all_gather(panel, 'col', axis=0, tiled=True)  38.9 us
    reduce_scatter x1, waiting for transfers between devices, on_device(): lax.psum_scatter(jnp.dot(block, row_panel, preferred_element_type=jnp.flo...  24.1 us
    dot_general x1, matrix products, on_device(): jnp.dot(block, row_panel, preferred_element_type=jnp.float32)  10.7 us
    dot_general x1, matrix products, on_device(): lax.dot_general(block, col_panel, (((0,), (0,)), ((), ())), preferred_ele...  9.83 us
  transfers between devices with their start and end apart: 5, of which 5 were waited for; matrix products, arithmetic and copies ran while one was open for 16% of the time, Pallas kernels for 0%

commit v1 on v0

v1 whole, which is shorter than its diff:
```python
import functools

import jax
import jax.numpy as jnp
from jax import lax
from jax.experimental import pallas as pl
from jax.experimental.pallas import tpu as pltpu
from jax.sharding import Mesh, PartitionSpec as P

f32 = jnp.float32
bf16 = jnp.bfloat16
U = 192
B = 512
BLK = 128
NB = B // BLK
LOWER = [(i, j) for i in range(NB) for j in range(i + 1)]
CH = len(LOWER) * BLK // 8
VMEM_LIMIT = 60 * 1024 * 1024


def whole():
    return pl.BlockSpec(memory_space=pltpu.VMEM)


def params(**kw):
    return pltpu.CompilerParams(vmem_limit_bytes=VMEM_LIMIT, **kw)


def hi_dot(a, b, dims):
    return lax.dot_general(
        a, b, (dims, ((), ())), precision=lax.Precision.HIGHEST, preferred_element_type=f32
    )


def shift(x, axis, k, n=4):
    return lax.ppermute(x, axis, [(i, (i + k) % n) for i in range(n)])


def iotas(n):
    return (
        lax.broadcasted_iota(jnp.int32, (n, n), 0),
        lax.broadcasted_iota(jnp.int32, (n, n), 1),
    )


def block(ref, i, j):
    return ref[i * BLK : (i + 1) * BLK, j * BLK : (j + 1) * BLK]


def prep_kernel(l_ref, pg_ref, p_ref, inv_ref, g_ref):
    rows, cols = iotas(BLK)
    blocks = []
    inv = []
    for b in range(NB):
        m = jnp.where(rows >= cols, block(l_ref, b, b), 0.0)
        blocks.append(m)
        inv.append(jnp.where(rows == cols, 1.0 / jnp.where(rows == cols, m, 1.0), 0.0))
    s = 1
    while s < BLK:
        sel = (rows // s != cols // s) & (rows // (2 * s) == cols // (2 * s))
        right = [hi_dot(jnp.where(sel, blocks[b], 0.0), inv[b], ((1,), (0,))) for b in range(NB)]
        inv = [inv[b] - hi_dot(inv[b], right[b], ((1,), (0,))) for b in range(NB)]
        s *= 2
    for b in range(NB):
        inv_ref[b] = inv[b]
    p = p_ref[...]
    g = pg_ref[...]
    total = None
    for _ in range(3):
        part = g.astype(bf16)
        g = g - part.astype(f32)
        term = lax.dot_general(part, p, (((0,), (0,)), ((), ())), preferred_element_type=f32)
        total = term if total is None else total + term
    g_ref[...] = total


def prep(lower, panel_grad, panel):
    return pl.pallas_call(
        prep_kernel,
        out_shape=(
            jax.ShapeDtypeStruct((NB, BLK, BLK), f32),
            jax.ShapeDtypeStruct((B, B), f32),
        ),
        in_specs=[whole()] * 3,
        out_specs=(whole(), whole()),
        compiler_params=params(),
        cost_estimate=pl.CostEstimate(flops=4_000_000_000, bytes_accessed=3_000_000, transcendentals=0),
        name="prep",
    )(lower, panel_grad, panel)


def direct_kernel(s_ref, f_ref, own, swp, r1, r2, r3, *refs):
    mine = refs[:4]
    other, pc = refs[4], refs[5]
    step = pl.program_id(0)
    x, yh, c = s_ref[8], s_ref[9], s_ref[10]

    @pl.when(step == 0)
    def _():
        def put(a, val):
            pc[pl.ds(pl.multiple_of(a * U, U), U), :] = val

        put(yh * 4 + x, own[...])
        put((1 - yh) * 4 + x, swp[...])
        for k, r in ((1, r1), (2, r2), (3, r3)):
            xs = lax.rem(x + 4 - k, 4)
            put(yh * 4 + xs, r[0])
            put((1 - yh) * 4 + xs, r[1])

    d = lax.dot_general(f_ref[...], pc[...], (((0,), (0,)), ((), ())), preferred_element_type=f32)
    lo, hi = d[:U], d[U:]
    first = c == 0
    keep = jnp.where(first, lo, hi)
    give = jnp.where(first, hi, lo)
    for k in range(4):
        for m in range(2):

            @pl.when(step == 2 * k + m)
            def _():
                mine[k][m] = keep
                other[k, m] = give


def direct(scalars, flip, own, swp, recv):
    grid_spec = pltpu.PrefetchScalarGridSpec(
        num_scalar_prefetch=1,
        grid=(8,),
        in_specs=[pl.BlockSpec((8 * U, 2 * U), lambda i, s: (0, s[i]))] + [whole()] * 5,
        out_specs=[whole()] * 5,
        scratch_shapes=[pltpu.VMEM((8 * U, B), bf16)],
    )
    out = pl.pallas_call(
        direct_kernel,
        grid_spec=grid_spec,
        out_shape=[jax.ShapeDtypeStruct((2, U, B), f32)] * 4
        + [jax.ShapeDtypeStruct((4, 2, U, B), f32)],
        compiler_params=params(),
        cost_estimate=pl.CostEstimate(flops=4_831_838_208, bytes_accessed=17_000_000, transcendentals=0),
        name="direct",
    )(scalars, flip, own, swp, *recv)
    return out[:4], out[4]


def transposed_kernel(s_ref, f0, f1, *refs):
    zown, zr, pown, prr = refs[0:2], refs[2:5], refs[5], refs[6:9]
    cown, cswp, c1, c2, c3 = refs[9:14]
    outs = refs[14:18]
    st_ref, pr, pc = refs[18], refs[19], refs[20]
    step = pl.program_id(0)
    z, yl, c = s_ref[8], s_ref[9], s_ref[10]
    x, yh = s_ref[11], s_ref[12]

    @pl.when(step == 0)
    def _():
        def put(yb, zb, cb, val):
            n = ((yb * 4 + zb) * 2 + cb) * U
            pr[pl.ds(pl.multiple_of(n, U), U), :] = val

        put(yl, z, c, zown[0][...])
        put(1 - yl, z, c, zown[1][...])
        put(yl, z, 1 - c, pown[0])
        put(1 - yl, z, 1 - c, pown[1])
        for k in (1, 2, 3):
            zs = lax.rem(z + 4 - k, 4)
            for m, yb in ((0, yl), (1, 1 - yl)):
                put(yb, zs, c, zr[k - 1][m])
                put(yb, zs, 1 - c, prr[k - 1][m])
        pc[0:U, :] = cown[...]
        pc[U : 2 * U, :] = cswp[...]
        for k, r in ((1, c3), (2, c2), (3, c1)):
            pc[2 * k * U : (2 * k + 1) * U, :] = r[0]
            pc[(2 * k + 1) * U : (2 * k + 2) * U, :] = r[1]
        st_ref[...] = jnp.zeros_like(st_ref)

    f = jnp.concatenate([f0[...], f1[...]], axis=0)
    t = jnp.dot(f, pr[...], preferred_element_type=f32)
    for k in range(4):

        @pl.when(step == k)
        def _():
            outs[k][0] = t[:U]
            outs[k][1] = t[U:]

    hi = t.astype(bf16)
    lo = (t - hi.astype(f32)).astype(bf16)
    p = pc[pl.ds(pl.multiple_of(step * 2 * U, 2 * U), 2 * U), :]
    dims = (((0,), (0,)), ((), ()))
    st_ref[...] += lax.dot_general(p, hi, dims, preferred_element_type=f32) + lax.dot_general(
        p, lo, dims, preferred_element_type=f32
    )


def transposed(scalars, flip, zown, zr, pown, prr, cpanel):
    grid_spec = pltpu.PrefetchScalarGridSpec(
        num_scalar_prefetch=1,
        grid=(4,),
        in_specs=[
            pl.BlockSpec((U, 16 * U), lambda i, s: (s[2 * i], 0)),
            pl.BlockSpec((U, 16 * U), lambda i, s: (s[2 * i + 1], 0)),
        ]
        + [whole()] * 14,
        out_specs=[whole()] * 5,
        scratch_shapes=[pltpu.VMEM((16 * U, B), bf16), pltpu.VMEM((8 * U, B), bf16)],
    )
    out = pl.pallas_call(
        transposed_kernel,
        grid_spec=grid_spec,
        out_shape=[jax.ShapeDtypeStruct((2, U, B), f32)] * 4 + [jax.ShapeDtypeStruct((B, B), f32)],
        compiler_params=params(),
        cost_estimate=pl.CostEstimate(flops=6_500_000_000, bytes_accessed=17_000_000, transcendentals=0),
        name="transposed",
    )(scalars, flip, flip, *zown, *zr, pown, *prr, *cpanel)
    return out[:4], out[4]


def pack_kernel(s_ref, g_ref, st_ref, *refs):
    mine, other, flat = refs[:4], refs[4], refs[5]
    c, y = s_ref[0], s_ref[1]
    for n, (i, j) in enumerate(LOWER):
        flat[n * BLK : (n + 1) * BLK, :] = block(g_ref, i, j) - block(st_ref, i, j) - block(st_ref, j, i).T
    for k in range(4):
        q = lax.rem(y + k, 4)
        mine[k][...] = flat[pl.ds(pl.multiple_of((c * 4 + q) * CH, CH), CH), :]
        other[k] = flat[pl.ds(pl.multiple_of(((1 - c) * 4 + q) * CH, CH), CH), :]


def pack(scalars, g, st):
    out = pl.pallas_call(
        pack_kernel,
        out_shape=[jax.ShapeDtypeStruct((CH, BLK), f32)] * 4 + [jax.ShapeDtypeStruct((4, CH, BLK), f32)],
        in_specs=[pl.BlockSpec(memory_space=pltpu.SMEM)] + [whole()] * 2,
        out_specs=[whole()] * 5,
        scratch_shapes=[pltpu.VMEM((8 * CH, BLK), f32)],
        compiler_params=params(),
        cost_estimate=pl.CostEstimate(flops=2_000_000, bytes_accessed=3_000_000, transcendentals=0),
        name="pack",
    )(scalars, g, st)
    return out[:4], out[4]


def tail_kernel(s_ref, mine, other, l_ref, inv_ref, dg_ref, out_ref, flat):
    c, y = s_ref[0], s_ref[1]
    for k in range(4):
        q = lax.rem(y + 4 - k, 4)
        flat[pl.ds(pl.multiple_of((c * 4 + q) * CH, CH), CH), :] = mine[k]
        flat[pl.ds(pl.multiple_of(((1 - c) * 4 + q) * CH, CH), CH), :] = other[k]
    rows, cols = iotas(BLK)
    low = {(i, j): block(l_ref, i, j) for (i, j) in LOWER}
    for i in range(NB):
        low[i, i] = jnp.where(rows >= cols, low[i, i], 0.0)
    q = {ij: flat[n * BLK : (n + 1) * BLK, :] for n, ij in enumerate(LOWER)}
    tdot = functools.partial(hi_dot, dims=((0,), (0,)))
    ndot = functools.partial(hi_dot, dims=((1,), (0,)))
    con = {}
    for j in range(NB):
        for i in reversed(range(j, NB)):
            acc = q[i, j]
            for k in range(i + 1, NB):
                acc = acc - tdot(low[k, i], con[k, j])
            con[i, j] = tdot(inv_ref[i], acc)
    new = {ij: block(dg_ref, *ij) - con[ij] for ij in LOWER}
    for i in range(NB):
        new[i, i] = jnp.where(rows >= cols, new[i, i], 0.0)
    inner = {}
    for i, j in LOWER:
        acc = tdot(low[i, i], new[i, j])
        for k in range(i + 1, NB):
            acc = acc + tdot(low[k, i], new[k, j])
        if i == j:
            acc = acc * jnp.where(rows > cols, 1.0, jnp.where(rows == cols, 0.5, 0.0))
        inner[i, j] = acc
    left = {}
    for i in reversed(range(NB)):
        acc = jnp.concatenate([inner.get((i, j), jnp.zeros((BLK, BLK), f32)) for j in range(NB)], axis=1)
        for k in range(i + 1, NB):
            acc = acc - tdot(low[k, i], left[k])
        left[i] = tdot(inv_ref[i], acc)
    left = jnp.concatenate([left[i] for i in range(NB)], axis=0)
    right = {}
    for j in reversed(range(NB)):
        acc = left[:, j * BLK : (j + 1) * BLK]
        for k in range(j + 1, NB):
            acc = acc - ndot(right[k], low[k, j])
        right[j] = ndot(acc, inv_ref[j])
    for i in range(NB):
        for j in range(i + 1):
            a = right[j][i * BLK : (i + 1) * BLK]
            b = right[i][j * BLK : (j + 1) * BLK]
            v = 0.5 * (a + b.T)
            out_ref[i * BLK : (i + 1) * BLK, j * BLK : (j + 1) * BLK] = v
            if i != j:
                out_ref[j * BLK : (j + 1) * BLK, i * BLK : (i + 1) * BLK] = v.T


def tail(scalars, mine, other, lower, inv, diag_grad):
    return pl.pallas_call(
        tail_kernel,
        out_shape=jax.ShapeDtypeStruct((B, B), f32),
        in_specs=[pl.BlockSpec(memory_space=pltpu.SMEM)] + [whole()] * 5,
        out_specs=whole(),
        scratch_shapes=[pltpu.VMEM((8 * CH, BLK), f32)],
        compiler_params=params(),
        cost_estimate=pl.CostEstimate(flops=6_000_000_000, bytes_accessed=5_000_000, transcendentals=0),
        name="tail",
    )(scalars, mine, other, lower, inv, diag_grad)


def solve_kernel(r_ref, d_ref, t_ref, l_ref, inv_ref, out_ref):
    r = r_ref[...] - d_ref[...] - t_ref[...]
    xs = {}
    for j in reversed(range(NB)):
        acc = r[:, j * BLK : (j + 1) * BLK]
        for k in range(j + 1, NB):
            acc = acc - hi_dot(xs[k], block(l_ref, k, j), ((1,), (0,)))
        xs[j] = hi_dot(acc, inv_ref[j], ((1,), (0,)))
        out_ref[:, j * BLK : (j + 1) * BLK] = xs[j]


def solve(r, d, t, lower, inv):
    return pl.pallas_call(
        solve_kernel,
        out_shape=jax.ShapeDtypeStruct((U, B), f32),
        in_specs=[whole()] * 5,
        out_specs=whole(),
        compiler_params=params(),
        cost_estimate=pl.CostEstimate(flops=1_000_000_000, bytes_accessed=3_000_000, transcendentals=0),
        name="solve",
    )(r, d, t, lower, inv)


def on_device(trailing_grad, panel, panel_grad, diag_factor, diag_grad):
    flip = trailing_grad.reshape(-1, trailing_grad.shape[3])
    x, yh = lax.axis_index("x"), lax.axis_index("yh")
    z, yl, c = lax.axis_index("z"), lax.axis_index("yl"), lax.axis_index("c")
    y = yh * 2 + yl
    ints = lambda *v: jnp.stack([jnp.asarray(e, jnp.int32) for e in v])
    d_scal = ints(*[(yl ^ m) * 4 + (z + k) % 4 for k in range(4) for m in range(2)], x, yh, c)
    t_scal = ints(*[(yh ^ m) * 4 + (x + k) % 4 for k in range(4) for m in range(2)], z, yl, c, x, yh)
    cy = ints(c, y)

    x_swp = shift(panel, "yh", 1, 2)
    z_swp = shift(panel, "yl", 1, 2)
    x_two = jnp.stack([panel, x_swp])
    z_two = jnp.stack([panel, z_swp])
    x_recv = [None] * 4
    z_recv = [None] * 4
    for k in (2, 1, 3):
        x_recv[k] = shift(x_two, "x", k)
    for k in (2, 1, 3):
        z_recv[k] = shift(z_two, "z", k)
    pair_own = shift(z_two, "c", 1, 2)
    pair_recv = [None] + [shift(z_recv[k], "c", 1, 2) for k in (1, 2, 3)]
    inv, g = prep(diag_factor, panel_grad, panel)

    d_mine, d_other = direct(d_scal, flip, panel, x_swp, x_recv[1:])
    d_pair = shift(d_other, "c", 1, 2)
    t_own, st = transposed(
        t_scal, flip, (panel, z_swp), z_recv[1:], pair_own, pair_recv[1:], (panel, x_swp, *x_recv[1:])
    )

    t_in = [None] * 4
    for k in (2, 1, 3):
        t_in[k] = shift(t_own[k], "x", k)
    d_sum = [d_mine[k] + d_pair[k] for k in range(4)]
    d_in = [None] * 4
    for k in (2, 1, 3):
        d_in[k] = shift(d_sum[k], "z", k)
    t_far = t_own[0][1] + t_in[1][1] + t_in[2][1] + t_in[3][1]
    d_far = d_sum[0][1] + d_in[1][1] + d_in[2][1] + d_in[3][1]
    t_last = shift(t_far, "yh", 1, 2)
    d_last = shift(d_far, "yl", 1, 2)
    near = (
        panel_grad
        - (t_own[0][0] + t_in[1][0] + t_in[2][0] + t_in[3][0])
        - (d_sum[0][0] + d_in[1][0] + d_in[2][0] + d_in[3][0])
    )
    panel_adj = solve(near, d_last, t_last, diag_factor, inv)

    q_mine, q_other = pack(cy, g, st)
    q_pair = shift(q_other, "c", 1, 2)
    q = [q_mine[k] + q_pair[k] for k in range(4)]
    q_in = [shift(q[k], ("yh", "yl"), k) for k in (1, 2, 3)]
    part = q[0] + q_in[0] + q_in[1] + q_in[2]
    for axis in ("z", "x"):
        got = [shift(part, axis, k) for k in (1, 2, 3)]
        part = (part + got[1]) + (got[0] + got[2])
    q_all = jnp.stack([part] + [shift(part, ("yh", "yl"), k) for k in (1, 2, 3)])
    diag_adj = tail(cy, q_all, shift(q_all, "c", 1, 2), diag_factor, inv, diag_grad)
    return panel_adj, diag_adj


def solution(mesh):
    fine = Mesh(mesh.devices.reshape(2, 4, 2, 4, 2), ("yh", "x", "yl", "z", "c"))
    row, col = ("yh", "x"), ("yl", "z", "c")
    return jax.shard_map(
        on_device,
        mesh=fine,
        in_specs=(P(None, col, None, row), P(row + col, None), P(row + col, None), P(), P()),
        out_specs=(P(row + col, None), P()),
        check_vma=False,
    )
```

time: 429 us -> 198 us (0.46)
  waiting for transfers between devices: 325 us -> 85.6 us
  Pallas kernels: 0 us -> 55.2 us
  starting transfers between devices: 0.2 us -> 41 us
  matrix products: 35.2 us -> 0 us
  other arithmetic: 42.9 us -> 10.9 us
  between operations: 14 us -> 0.84 us
  local copies, waits for them, and re-layouts: 9.72 us -> 2.91 us
    psum x1 -> x0, waiting for transfers between devices: 146 us -> none  [on_device(): diag_new = diag_grad - lax.psum(contrib, ('row', 'col'))]
    reduce_scatter x2 -> x0, waiting for transfers between devices: 96.2 us -> none  [the longest x1 72.1 us: on_device(): lax.psum_scatter(lax.dot_general(block, col_panel, (((0,), (0,)), ((), ()...]
    ppermute x0 -> x35, waiting for transfers between devices: none -> 85.6 us  [shift(): return lax.ppermute(x, axis, [(i, (i + k) % n) for i in range(n)])]
    all_gather x2 -> x0, waiting for transfers between devices: 81.2 us -> none  [the longest x1 42.3 us: on_device(): col_panel = lax.all_gather(panel, 'row', axis=0, tiled=True)]
    pallas_call x0 -> x6, Pallas kernels: none -> 55.2 us  [the longest x1 14.6 us: transposed(): pl.pallas_call(transposed_kernel, grid_spec=grid_spec, out_shape=[jax.Sha...]
    ppermute x0 -> x35, starting transfers between devices: none -> 41 us  [shift(): return lax.ppermute(x, axis, [(i, (i + k) % n) for i in range(n)])]
    another operation x3, other arithmetic: 39.6 us -> 1.72 us  [the longest x1 1.06 us: on_device(): z_two = jnp.stack([panel, z_swp])]
    dot_general x4 -> x0, matrix products: 25.6 us -> none  [the longest x1 10.7 us: on_device(): jnp.dot(block, row_panel, preferred_element_type=jnp.float32)]
  transfers between devices with their start and end apart: 5 -> 35, of which waited for: 5 -> 20; matrix products, arithmetic and copies ran while one was open for 16% -> 6% of each run, Pallas kernels for 0% -> 19%
where the time goes in v1:
time: 198 us; the launch traced here: 197 us
  waiting for transfers between devices  85.6 us (43%)
  Pallas kernels  55.2 us (28%)
  starting transfers between devices  41 us (21%)
  other arithmetic  10.9 us (6%)
  local copies, waits for them, and re-layouts  2.91 us (1%)
    ppermute x35, waiting for transfers between devices, shift(): return lax.ppermute(x, axis, [(i, (i + k) % n) for i in range(n)])  85.6 us
    ppermute x35, starting transfers between devices, shift(): return lax.ppermute(x, axis, [(i, (i + k) % n) for i in range(n)])  41 us
    pallas_call x1, Pallas kernels, transposed(): pl.pallas_call(transposed_kernel, grid_spec=grid_spec, out_shape=[jax.Sha...  14.6 us
    pallas_call x1, Pallas kernels, direct(): pl.pallas_call(direct_kernel, grid_spec=grid_spec, out_shape=[jax.ShapeDt...  13.7 us
    pallas_call x1, Pallas kernels, tail(): pl.pallas_call(tail_kernel, out_shape=jax.ShapeDtypeStruct((B, B), f32),...  13.5 us
    pallas_call x1, Pallas kernels, prep(): pl.pallas_call(prep_kernel, out_shape=(jax.ShapeDtypeStruct((NB, BLK, BLK...  6.59 us
    pallas_call x1, Pallas kernels, solve(): pl.pallas_call(solve_kernel, out_shape=jax.ShapeDtypeStruct((U, B), f32),...  4.3 us
  transfers between devices with their start and end apart: 35, of which 20 were waited for; matrix products, arithmetic and copies ran while one was open for 6% of the time, Pallas kernels for 19%

profile of v1, /device:TPU:8, one launch (start us, length us, event | category | flops | bytes accessed | tf_op | source)
XLA Modules:
  0.0 196.5 jit_solution(11386012695170614413)
XLA Ops:
  0.6 2.4 %collective-permute-start.8 = (bf16[192,512]{1,0:T(8,128)(2,1)}, bf16[192,512]{1,0:T(8,128)(2,1)S(1)}, u32[]{:S(2)}, u32[]{:S(2)}) collective-permute-start(bf16[192,512]{1,0:T(8,128)(2,1)} %p_ref.1), channel_id=1, source_target_pairs={{0,64},{64,0},{1,65},{65,1},{2,66},{66,2},{3,67},{67,3},{4,68},{68... | collective-permute-start | bytes 589832 | tf_op jit(solution)/shard_map/ppermute | solution.py:36
  3.0 1.3 collective-permute-start
  4.4 5.9 %collective-permute-done.8.refs_10_.swp = bf16[192,512]{1,0:T(8,128)(2,1)S(1)} collective-permute-done((bf16[192,512]{1,0:T(8,128)(2,1)}, bf16[192,512]{1,0:T(8,128)(2,1)S(1)}, u32[]{:S(2)}, u32[]{:S(2)}) %collective-permute-start.8) | collective-permute-done | bytes 196640 | tf_op jit(solution)/shard_map/ppermute | solution.py:36
  10.2 3.2 %collective-permute-done.refs_1_ = bf16[192,512]{1,0:T(8,128)(2,1)S(1)} collective-permute-done((bf16[192,512]{1,0:T(8,128)(2,1)}, bf16[192,512]{1,0:T(8,128)(2,1)S(1)}, u32[]{:S(2)}, u32[]{:S(2)}) %collective-permute-start) | collective-permute-done | bytes 196640 | tf_op jit(solution)/shard_map/ppermute | solution.py:36
  13.4 1.1 pad_maximum_fusion.1
  14.5 1.6 collective-permute-start.9
  16.0 2.7 %collective-permute-start.10 = (bf16[2,192,512]{2,1,0:T(8,128)(2,1)S(1)}, bf16[2,192,512]{2,1,0:T(8,128)(2,1)S(1)}, u32[]{:S(2)}, u32[]{:S(2)}) collective-permute-start(bf16[2,192,512]{2,1,0:T(8,128)(2,1)S(1)} %get-tuple-element.44), channel_id=1, source_target_pairs={{0,32},{16,48},{32,0},{48,16},{1,33},{17,49},{33,1},{49,17},{2,34}... | collective-permute-start | bytes 1179656 | tf_op jit(solution)/shard_map/ppermute | solution.py:36
  18.7 1.4 collective-permute-start.11
  20.8 6.0 %collective-permute-done.9.refs_11_.r1 = bf16[2,192,512]{2,1,0:T(8,128)(2,1)S(1)} collective-permute-done((bf16[2,192,512]{2,1,0:T(8,128)(2,1)S(1)}, bf16[2,192,512]{2,1,0:T(8,128)(2,1)S(1)}, u32[]{:S(2)}, u32[]{:S(2)}) %collective-permute-start.9) | collective-permute-done | bytes 393248 | tf_op jit(solution)/shard_map/ppermute | solution.py:36
  26.8 8.3 %collective-permute-done.10.refs_12_.r2 = bf16[2,192,512]{2,1,0:T(8,128)(2,1)S(1)} collective-permute-done((bf16[2,192,512]{2,1,0:T(8,128)(2,1)S(1)}, bf16[2,192,512]{2,1,0:T(8,128)(2,1)S(1)}, u32[]{:S(2)}, u32[]{:S(2)}) %collective-permute-start.10) | collective-permute-done | bytes 393248 | tf_op jit(solution)/shard_map/ppermute | solution.py:36
  36.0 13.7 %direct.1 = (f32[2,192,512]{2,1,0:T(8,128)}, f32[2,192,512]{2,1,0:T(8,128)}, f32[2,192,512]{2,1,0:T(8,128)}, f32[2,192,512]{2,1,0:T(8,128)}, f32[4,2,192,512]{3,2,1,0:T(8,128)}) custom-call(s32[11]{0:T(128)} %stack.137.s_ref, bf16[1536,3072]{1,0:T(8,128)(2,1)} %bitcast.89, bf16[192,512]{1,0:T(8,128)(2,1)} %p_ref.1, bf16[192,512]{1,0:T(8,128)(2,1)} %copy-done.14, ...), custom_call_target="tpu_custom_call" | custom-call | flops 4831838208 | bytes 17000000 | tf_op jit(solution)/shard_map/direct/pallas_call | solution.py:132
  49.7 2.0 collective-permute-start.1
  51.6 3.6 %collective-permute-start.2 = (bf16[2,192,512]{2,1,0:T(8,128)(2,1)S(1)}, bf16[2,192,512]{2,1,0:T(8,128)(2,1)}, u32[]{:S(2)}, u32[]{:S(2)}) collective-permute-start(bf16[2,192,512]{2,1,0:T(8,128)(2,1)S(1)} %get-tuple-element.43), channel_id=1, source_target_pairs={{0,4},{2,6},{4,0},{6,2},{1,5},{3,7},{5,1},{7,3},{8,12},{10,14},{12... | collective-permute-start | bytes 1179656 | tf_op jit(solution)/shard_map/ppermute | solution.py:36
  56.2 7.3 %collective-permute-done.1.refs_2_ = bf16[2,192,512]{2,1,0:T(8,128)(2,1)} collective-permute-done((bf16[2,192,512]{2,1,0:T(8,128)(2,1)S(1)}, bf16[2,192,512]{2,1,0:T(8,128)(2,1)}, u32[]{:S(2)}, u32[]{:S(2)}) %collective-permute-start.1) | collective-permute-done | bytes 393248 | tf_op jit(solution)/shard_map/ppermute | solution.py:36
  63.6 9.6 %collective-permute-done.2.refs_3_ = bf16[2,192,512]{2,1,0:T(8,128)(2,1)} collective-permute-done((bf16[2,192,512]{2,1,0:T(8,128)(2,1)S(1)}, bf16[2,192,512]{2,1,0:T(8,128)(2,1)}, u32[]{:S(2)}, u32[]{:S(2)}) %collective-permute-start.2) | collective-permute-done | bytes 393248 | tf_op jit(solution)/shard_map/ppermute | solution.py:36
  75.0 6.6 %prep.1 = (f32[4,128,128]{2,1,0:T(8,128)}, f32[512,512]{1,0:T(8,128)}) custom-call(f32[512,512]{1,0:T(8,128)} %l_ref.5, f32[192,512]{1,0:T(8,128)} %pg_ref.1, bf16[192,512]{1,0:T(8,128)(2,1)} %p_ref.1), custom_call_target="tpu_custom_call" | custom-call | flops 4000000000 | bytes 3000000 | tf_op jit(solution)/shard_map/prep/pallas_call | solution.py:78
  81.6 14.6 %transposed.1 = (f32[2,192,512]{2,1,0:T(8,128)}, f32[2,192,512]{2,1,0:T(8,128)}, f32[2,192,512]{2,1,0:T(8,128)}, f32[2,192,512]{2,1,0:T(8,128)}, f32[512,512]{1,0:T(8,128)}) custom-call(s32[13]{0:T(128)} %stack.123.s_ref, bf16[1536,3072]{1,0:T(8,128)(2,1)} %bitcast.90, bf16[1536,3072]{1,0:T(8,128)(2,1)} %bitcast.91, bf16[192,512]{1,0:T(8,128)(2,1)} %p_ref.1, ...), custom_call_target="tpu_custom_call" | custom-call | flops 6499999744 | bytes 17000000 | tf_op jit(solution)/shard_map/transposed/pallas_call | solution.py:205
  96.2 2.6 %pack.1 = (f32[160,128]{1,0:T(8,128)}, f32[160,128]{1,0:T(8,128)}, f32[160,128]{1,0:T(8,128)}, f32[160,128]{1,0:T(8,128)}, f32[4,160,128]{2,1,0:T(8,128)}) custom-call(s32[2]{0:T(128)} %pad_add_fusion.s_ref, f32[512,512]{1,0:T(8,128)} %get-tuple-element.29.g_ref, f32[512,512]{1,0:T(8,128)} %get-tuple-element.30.st_ref), custom_call_target="tpu_custom_call" | custom-call | flops 2000000 | bytes 3000000 | tf_op jit(solution)/shard_map/pack/pallas_call | solution.py:228
  98.8 1.8 collective-permute-done.21
  102.6 1.2 collective-permute-start.23
  104.3 2.1 %collective-permute-done.24 = f32[160,128]{1,0:T(8,128)S(1)} collective-permute-done((f32[160,128]{1,0:T(8,128)S(1)}, f32[160,128]{1,0:T(8,128)S(1)}, u32[]{:S(2)}, u32[]{:S(2)}) %collective-permute-start.24) | collective-permute-done | bytes 81952 | tf_op jit(solution)/shard_map/ppermute | solution.py:36
  106.4 2.1 %collective-permute-done.23 = f32[160,128]{1,0:T(8,128)S(1)} collective-permute-done((f32[160,128]{1,0:T(8,128)S(1)}, f32[160,128]{1,0:T(8,128)S(1)}, u32[]{:S(2)}, u32[]{:S(2)}) %collective-permute-start.23) | collective-permute-done | bytes 81952 | tf_op jit(solution)/shard_map/ppermute | solution.py:36
  108.5 1.4 collective-permute-done.22
  110.9 1.0 collective-permute-start.26
  111.9 2.3 %collective-permute-start.27 = (f32[160,128]{1,0:T(8,128)S(1)}, f32[160,128]{1,0:T(8,128)S(1)}, u32[]{:S(2)}, u32[]{:S(2)}) collective-permute-start(f32[160,128]{1,0:T(8,128)S(1)} %fusion.16), channel_id=1, source_target_pairs={{0,6},{2,0},{4,2},{6,4},{1,7},{3,1},{5,3},{7,5},{8,14},{10,8},{12,... | collective-permute-start | bytes 245768 | tf_op jit(solution)/shard_map/ppermute | solution.py:36
  115.1 1.8 collective-permute-done.26
  116.8 3.3 %collective-permute-done.25 = f32[160,128]{1,0:T(8,128)S(1)} collective-permute-done((f32[160,128]{1,0:T(8,128)S(1)}, f32[160,128]{1,0:T(8,128)S(1)}, u32[]{:S(2)}, u32[]{:S(2)}) %collective-permute-start.25) | collective-permute-done | bytes 81952 | tf_op jit(solution)/shard_map/ppermute | solution.py:36
  120.1 1.5 collective-permute-start.29
  121.7 1.8 collective-permute-start.30
  123.4 1.4 collective-permute-start.28
  124.9 1.5 collective-permute-start.14
  127.0 2.4 %collective-permute-done.28 = f32[160,128]{1,0:T(8,128)S(1)} collective-permute-done((f32[160,128]{1,0:T(8,128)S(1)}, f32[160,128]{1,0:T(8,128)S(1)}, u32[]{:S(2)}, u32[]{:S(2)}) %collective-permute-start.28) | collective-permute-done | bytes 81952 | tf_op jit(solution)/shard_map/ppermute | solution.py:36
  129.4 1.9 collective-permute-start.33
  131.3 1.4 collective-permute-start.13
  132.8 1.3 collective-permute-start.12
  134.5 1.6 collective-permute-start.32
  136.2 1.1 collective-permute-start.31
  137.2 2.7 %fusion.3 = (f32[2,192,512]{2,1,0:T(8,128)S(1)}, f32[2,192,512]{2,1,0:T(8,128)S(1)}, f32[2,192,512]{2,1,0:T(8,128)S(1)}, f32[2,192,512]{2,1,0:T(8,128)S(1)}) fusion(f32[2,192,512]{2,1,0:T(8,128)} %get-tuple-element.23, f32[4,2,192,512]{3,2,1,0:T(8,128)S(1)} %collective-permute-done.15, f32[2,192,512]{2,1,0:T(8,128)} %get-tuple-element.27, ...), kind=kLoop, calls=%fused_computation.7 | loop fusion | flops 786432 | bytes 9437184 | tf_op jit(solution)/shard_map/add | solution.py:364
  141.2 1.1 collective-permute-start.17
  142.4 3.2 %collective-permute-done.14 = f32[2,192,512]{2,1,0:T(8,128)S(1)} collective-permute-done((f32[2,192,512]{2,1,0:T(8,128)}, f32[2,192,512]{2,1,0:T(8,128)S(1)}, u32[]{:S(2)}, u32[]{:S(2)}) %collective-permute-start.14) | collective-permute-done | bytes 786464 | tf_op jit(solution)/shard_map/ppermute | solution.py:36
  145.6 7.9 %collective-permute-done.13 = f32[2,192,512]{2,1,0:T(8,128)S(1)} collective-permute-done((f32[2,192,512]{2,1,0:T(8,128)}, f32[2,192,512]{2,1,0:T(8,128)S(1)}, u32[]{:S(2)}, u32[]{:S(2)}) %collective-permute-start.13) | collective-permute-done | bytes 786464 | tf_op jit(solution)/shard_map/ppermute | solution.py:36
  153.5 10.8 %collective-permute-done.12 = f32[2,192,512]{2,1,0:T(8,128)S(1)} collective-permute-done((f32[2,192,512]{2,1,0:T(8,128)}, f32[2,192,512]{2,1,0:T(8,128)S(1)}, u32[]{:S(2)}, u32[]{:S(2)}) %collective-permute-start.12) | collective-permute-done | bytes 786464 | tf_op jit(solution)/shard_map/ppermute | solution.py:36
  164.4 1.1 fusion.4
  166.0 6.7 %collective-permute-done.16 = f32[2,192,512]{2,1,0:T(8,128)S(1)} collective-permute-done((f32[2,192,512]{2,1,0:T(8,128)S(1)}, f32[2,192,512]{2,1,0:T(8,128)S(1)}, u32[]{:S(2)}, u32[]{:S(2)}) %collective-permute-start.16) | collective-permute-done | bytes 786464 | tf_op jit(solution)/shard_map/ppermute | solution.py:36
  173.7 1.7 collective-permute-start.19
  176.2 13.5 %tail.1 = f32[512,512]{1,0:T(8,128)} custom-call(s32[2]{0:T(128)} %pad_add_fusion.s_ref, f32[4,160,128]{2,1,0:T(8,128)} %copy-done.13, f32[4,160,128]{2,1,0:T(8,128)} %copy-done.19, f32[512,512]{1,0:T(8,128)} %l_ref.5, f32[4,128,128]{2,1,0:T(8,128)} %get-tuple-element.28.inv_ref, f32[512,512]{1,0:T(8,128)} %dg_ref.1), custom_call_target="tpu_custom_call" | custom-call | flops 6000000000 | bytes 5000000 | tf_op jit(solution)/shard_map/tail/pallas_call | solution.py:296
  189.7 2.5 %fusion.7.r_ref = f32[192,512]{1,0:T(8,128)} fusion(f32[2,192,512]{2,1,0:T(8,128)} %copy-done.10, f32[2,192,512]{2,1,0:T(8,128)} %copy-done.11, f32[2,192,512]{2,1,0:T(8,128)} %copy-done.12, f32[2,192,512]{2,1,0:T(8,128)S(1)} %copy-done.1, f32[192,512]{1,0:T(8,128)} %pg_ref.1, f32[2,192,512]{2,1,0:T(8,128)S(1)} %copy-done.5, ...), kind=kLoop, calls=%fused_computation.20 | loop fusion | flops 786432 | bytes 3932160 | tf_op jit(solution)/shard_map/sub | solution.py:373
  192.2 4.3 %solve.1 = f32[192,512]{1,0:T(8,128)} custom-call(f32[192,512]{1,0:T(8,128)} %fusion.7.r_ref, f32[192,512]{1,0:T(8,128)} %collective-permute-done.19.d_ref, f32[192,512]{1,0:T(8,128)} %collective-permute-done.20.t_ref, f32[512,512]{1,0:T(8,128)} %l_ref.5, f32[4,128,128]{2,1,0:T(8,128)} %get-tuple-element.28.inv_ref), custom_call_target="tpu_custom_call" | custom-call | flops 1000000000 | bytes 3000000 | tf_op jit(solution)/shard_map/solve/pallas_call | solution.py:320
  (81 shorter events, 13.2 us)
Async XLA Ops:
  0.6 9.6 %collective-permute-start.8 = (bf16[192,512]{1,0:T(8,128)(2,1)}, bf16[192,512]{1,0:T(8,128)(2,1)S(1)}, u32[]{:S(2)}, u32[]{:S(2)}) collective-permute-start(bf16[192,512]{1,0:T(8,128)(2,1)} %p_ref.1), channel_id=1, source_target_pairs={{0,64},{64,0},{1,65},{65,1},{2,66},{66,2},{3,67},{67,3},{4,68},{68... | collective-permute-start | bytes 589832 | tf_op jit(solution)/shard_map/ppermute | solution.py:36
  3.0 10.4 %collective-permute-start = (bf16[192,512]{1,0:T(8,128)(2,1)}, bf16[192,512]{1,0:T(8,128)(2,1)S(1)}, u32[]{:S(2)}, u32[]{:S(2)}) collective-permute-start(bf16[192,512]{1,0:T(8,128)(2,1)} %p_ref.1), channel_id=1, source_target_pairs={{0,8},{8,0},{1,9},{9,1},{2,10},{10,2},{3,11},{11,3},{4,12},{12,4},... | collective-permute-start | bytes 589832 | tf_op jit(solution)/shard_map/ppermute | solution.py:36
  10.2 24.9 %copy-start.14 = (bf16[192,512]{1,0:T(8,128)(2,1)}, bf16[192,512]{1,0:T(8,128)(2,1)S(1)}, u32[]{:S(2)}) copy-start(bf16[192,512]{1,0:T(8,128)(2,1)S(1)} %collective-permute-done.8.refs_10_.swp) | copy-start | bytes 589828
  13.4 36.3 %copy-start.15 = (bf16[192,512]{1,0:T(8,128)(2,1)}, bf16[192,512]{1,0:T(8,128)(2,1)S(1)}, u32[]{:S(2)}) copy-start(bf16[192,512]{1,0:T(8,128)(2,1)S(1)} %collective-permute-done.refs_1_) | copy-start | bytes 589828
  14.5 12.3 %collective-permute-start.9 = (bf16[2,192,512]{2,1,0:T(8,128)(2,1)S(1)}, bf16[2,192,512]{2,1,0:T(8,128)(2,1)S(1)}, u32[]{:S(2)}, u32[]{:S(2)}) collective-permute-start(bf16[2,192,512]{2,1,0:T(8,128)(2,1)S(1)} %get-tuple-element.44), channel_id=1, source_target_pairs={{0,16},{16,32},{32,48},{48,0},{1,17},{17,33},{33,49},{49,1},{2,18}... | collective-permute-start | bytes 1179656 | tf_op jit(solution)/shard_map/ppermute | solution.py:36
  16.0 19.1 %collective-permute-start.10 = (bf16[2,192,512]{2,1,0:T(8,128)(2,1)S(1)}, bf16[2,192,512]{2,1,0:T(8,128)(2,1)S(1)}, u32[]{:S(2)}, u32[]{:S(2)}) collective-permute-start(bf16[2,192,512]{2,1,0:T(8,128)(2,1)S(1)} %get-tuple-element.44), channel_id=1, source_target_pairs={{0,32},{16,48},{32,0},{48,16},{1,33},{17,49},{33,1},{49,17},{2,34}... | collective-permute-start | bytes 1179656 | tf_op jit(solution)/shard_map/ppermute | solution.py:36
  18.7 16.4 %collective-permute-start.11 = (bf16[2,192,512]{2,1,0:T(8,128)(2,1)S(1)}, bf16[2,192,512]{2,1,0:T(8,128)(2,1)S(1)}, u32[]{:S(2)}, u32[]{:S(2)}) collective-permute-start(bf16[2,192,512]{2,1,0:T(8,128)(2,1)S(1)} %get-tuple-element.44), channel_id=1, source_target_pairs={{0,48},{16,0},{32,16},{48,32},{1,49},{17,1},{33,17},{49,33},{2,50}... | collective-permute-start | bytes 1179656 | tf_op jit(solution)/shard_map/ppermute | solution.py:36
  49.7 86.5 %collective-permute-start.15 = (f32[4,2,192,512]{3,2,1,0:T(8,128)}, f32[4,2,192,512]{3,2,1,0:T(8,128)S(1)}, u32[]{:S(2)}, u32[]{:S(2)}) collective-permute-start(f32[4,2,192,512]{3,2,1,0:T(8,128)} %get-tuple-element.24), channel_id=1, source_target_pairs={{0,1},{1,0},{2,3},{3,2},{4,5},{5,4},{6,7},{7,6},{8,9},{9,8},{10,11... | collective-permute-start | bytes 9437192 | tf_op jit(solution)/shard_map/ppermute | solution.py:36
  49.7 13.9 %collective-permute-start.1 = (bf16[2,192,512]{2,1,0:T(8,128)(2,1)S(1)}, bf16[2,192,512]{2,1,0:T(8,128)(2,1)}, u32[]{:S(2)}, u32[]{:S(2)}) collective-permute-start(bf16[2,192,512]{2,1,0:T(8,128)(2,1)S(1)} %get-tuple-element.43), channel_id=1, source_target_pairs={{0,2},{2,4},{4,6},{6,0},{1,3},{3,5},{5,7},{7,1},{8,10},{10,12},{12... | collective-permute-start | bytes 1179656 | tf_op jit(solution)/shard_map/ppermute | solution.py:36
  51.6 21.6 %collective-permute-start.2 = (bf16[2,192,512]{2,1,0:T(8,128)(2,1)S(1)}, bf16[2,192,512]{2,1,0:T(8,128)(2,1)}, u32[]{:S(2)}, u32[]{:S(2)}) collective-permute-start(bf16[2,192,512]{2,1,0:T(8,128)(2,1)S(1)} %get-tuple-element.43), channel_id=1, source_target_pairs={{0,4},{2,6},{4,0},{6,2},{1,5},{3,7},{5,1},{7,3},{8,12},{10,14},{12... | collective-permute-start | bytes 1179656 | tf_op jit(solution)/shard_map/ppermute | solution.py:36
  55.2 18.0 %collective-permute-start.3 = (bf16[2,192,512]{2,1,0:T(8,128)(2,1)S(1)}, bf16[2,192,512]{2,1,0:T(8,128)(2,1)}, u32[]{:S(2)}, u32[]{:S(2)}) collective-permute-start(bf16[2,192,512]{2,1,0:T(8,128)(2,1)S(1)} %get-tuple-element.43), channel_id=1, source_target_pairs={{0,6},{2,0},{4,2},{6,4},{1,7},{3,1},{5,3},{7,5},{8,14},{10,8},{12,... | collective-permute-start | bytes 1179656 | tf_op jit(solution)/shard_map/ppermute | solution.py:36
  56.2 25.4 %collective-permute-start.4 = (bf16[2,192,512]{2,1,0:T(8,128)(2,1)S(1)}, bf16[2,192,512]{2,1,0:T(8,128)(2,1)}, u32[]{:S(2)}, u32[]{:S(2)}) collective-permute-start(bf16[2,192,512]{2,1,0:T(8,128)(2,1)S(1)} %get-tuple-element.43), channel_id=1, source_target_pairs={{0,1},{1,0},{2,3},{3,2},{4,5},{5,4},{6,7},{7,6},{8,9},{9,8},{10,11... | collective-permute-start | bytes 1179656 | tf_op jit(solution)/shard_map/ppermute | solution.py:36
  63.6 18.0 %collective-permute-start.5 = (bf16[2,192,512]{2,1,0:T(8,128)(2,1)}, bf16[2,192,512]{2,1,0:T(8,128)(2,1)}, u32[]{:S(2)}, u32[]{:S(2)}) collective-permute-start(bf16[2,192,512]{2,1,0:T(8,128)(2,1)} %collective-permute-done.1.refs_2_), channel_id=1, source_target_pairs={{0,1},{1,0},{2,3},{3,2},{4,5},{5,4},{6,7},{7,6},{8,9},{9,8},{10,11... | collective-permute-start | bytes 1179656 | tf_op jit(solution)/shard_map/ppermute | solution.py:36
  73.2 8.4 %collective-permute-start.6 = (bf16[2,192,512]{2,1,0:T(8,128)(2,1)}, bf16[2,192,512]{2,1,0:T(8,128)(2,1)}, u32[]{:S(2)}, u32[]{:S(2)}) collective-permute-start(bf16[2,192,512]{2,1,0:T(8,128)(2,1)} %collective-permute-done.2.refs_3_), channel_id=1, source_target_pairs={{0,1},{1,0},{2,3},{3,2},{4,5},{5,4},{6,7},{7,6},{8,9},{9,8},{10,11... | collective-permute-start | bytes 1179656 | tf_op jit(solution)/shard_map/ppermute | solution.py:36
  73.2 8.4 %collective-permute-start.7 = (bf16[2,192,512]{2,1,0:T(8,128)(2,1)}, bf16[2,192,512]{2,1,0:T(8,128)(2,1)}, u32[]{:S(2)}, u32[]{:S(2)}) collective-permute-start(bf16[2,192,512]{2,1,0:T(8,128)(2,1)} %collective-permute-done.3.refs_4_), channel_id=1, source_target_pairs={{0,1},{1,0},{2,3},{3,2},{4,5},{5,4},{6,7},{7,6},{8,9},{9,8},{10,11... | collective-permute-start | bytes 1179656 | tf_op jit(solution)/shard_map/ppermute | solution.py:36
  98.8 1.8 collective-permute-start.21
  101.7 4.7 %collective-permute-start.24 = (f32[160,128]{1,0:T(8,128)S(1)}, f32[160,128]{1,0:T(8,128)S(1)}, u32[]{:S(2)}, u32[]{:S(2)}) collective-permute-start(f32[160,128]{1,0:T(8,128)S(1)} %get-tuple-element.41), channel_id=1, source_target_pairs={{0,72},{8,0},{64,8},{72,64},{1,73},{9,1},{65,9},{73,65},{2,74},{10... | collective-permute-start | bytes 245768 | tf_op jit(solution)/shard_map/ppermute | solution.py:36
  102.6 5.9 %collective-permute-start.23 = (f32[160,128]{1,0:T(8,128)S(1)}, f32[160,128]{1,0:T(8,128)S(1)}, u32[]{:S(2)}, u32[]{:S(2)}) collective-permute-start(f32[160,128]{1,0:T(8,128)S(1)} %get-tuple-element.42), channel_id=1, source_target_pairs={{0,64},{8,72},{64,0},{72,8},{1,65},{9,73},{65,1},{73,9},{2,66},{10... | collective-permute-start | bytes 245768 | tf_op jit(solution)/shard_map/ppermute | solution.py:36
  103.8 6.1 %collective-permute-start.22 = (f32[160,128]{1,0:T(8,128)S(1)}, f32[160,128]{1,0:T(8,128)S(1)}, u32[]{:S(2)}, u32[]{:S(2)}) collective-permute-start(f32[160,128]{1,0:T(8,128)S(1)} %get-tuple-element.40), channel_id=1, source_target_pairs={{0,8},{8,64},{64,72},{72,0},{1,9},{9,65},{65,73},{73,1},{2,10},{10... | collective-permute-start | bytes 245768 | tf_op jit(solution)/shard_map/ppermute | solution.py:36
  110.9 6.0 %collective-permute-start.26 = (f32[160,128]{1,0:T(8,128)S(1)}, f32[160,128]{1,0:T(8,128)S(1)}, u32[]{:S(2)}, u32[]{:S(2)}) collective-permute-start(f32[160,128]{1,0:T(8,128)S(1)} %fusion.16), channel_id=1, source_target_pairs={{0,2},{2,4},{4,6},{6,0},{1,3},{3,5},{5,7},{7,1},{8,10},{10,12},{12... | collective-permute-start | bytes 245768 | tf_op jit(solution)/shard_map/ppermute | solution.py:36
  111.9 4.9 %collective-permute-start.27 = (f32[160,128]{1,0:T(8,128)S(1)}, f32[160,128]{1,0:T(8,128)S(1)}, u32[]{:S(2)}, u32[]{:S(2)}) collective-permute-start(f32[160,128]{1,0:T(8,128)S(1)} %fusion.16), channel_id=1, source_target_pairs={{0,6},{2,0},{4,2},{6,4},{1,7},{3,1},{5,3},{7,5},{8,14},{10,8},{12,... | collective-permute-start | bytes 245768 | tf_op jit(solution)/shard_map/ppermute | solution.py:36
  114.2 5.9 %collective-permute-start.25 = (f32[160,128]{1,0:T(8,128)S(1)}, f32[160,128]{1,0:T(8,128)S(1)}, u32[]{:S(2)}, u32[]{:S(2)}) collective-permute-start(f32[160,128]{1,0:T(8,128)S(1)} %fusion.16), channel_id=1, source_target_pairs={{0,4},{2,6},{4,0},{6,2},{1,5},{3,7},{5,1},{7,3},{8,12},{10,14},{12... | collective-permute-start | bytes 245768 | tf_op jit(solution)/shard_map/ppermute | solution.py:36
  120.1 6.2 %collective-permute-start.29 = (f32[160,128]{1,0:T(8,128)S(1)}, f32[160,128]{1,0:T(8,128)S(1)}, u32[]{:S(2)}, u32[]{:S(2)}) collective-permute-start(f32[160,128]{1,0:T(8,128)S(1)} %add_add_fusion.1), channel_id=1, source_target_pairs={{0,16},{16,32},{32,48},{48,0},{1,17},{17,33},{33,49},{49,1},{2,18}... | collective-permute-start | bytes 245768 | tf_op jit(solution)/shard_map/ppermute | solution.py:36
  121.7 5.3 %collective-permute-start.30 = (f32[160,128]{1,0:T(8,128)S(1)}, f32[160,128]{1,0:T(8,128)S(1)}, u32[]{:S(2)}, u32[]{:S(2)}) collective-permute-start(f32[160,128]{1,0:T(8,128)S(1)} %add_add_fusion.1), channel_id=1, source_target_pairs={{0,48},{16,0},{32,16},{48,32},{1,49},{17,1},{33,17},{49,33},{2,50}... | collective-permute-start | bytes 245768 | tf_op jit(solution)/shard_map/ppermute | solution.py:36
  123.4 5.9 %collective-permute-start.28 = (f32[160,128]{1,0:T(8,128)S(1)}, f32[160,128]{1,0:T(8,128)S(1)}, u32[]{:S(2)}, u32[]{:S(2)}) collective-permute-start(f32[160,128]{1,0:T(8,128)S(1)} %add_add_fusion.1), channel_id=1, source_target_pairs={{0,32},{16,48},{32,0},{48,16},{1,33},{17,49},{33,1},{49,17},{2,34}... | collective-permute-start | bytes 245768 | tf_op jit(solution)/shard_map/ppermute | solution.py:36
  124.9 20.7 %collective-permute-start.14 = (f32[2,192,512]{2,1,0:T(8,128)}, f32[2,192,512]{2,1,0:T(8,128)S(1)}, u32[]{:S(2)}, u32[]{:S(2)}) collective-permute-start(f32[2,192,512]{2,1,0:T(8,128)} %get-tuple-element.22), channel_id=1, source_target_pairs={{0,48},{16,0},{32,16},{48,32},{1,49},{17,1},{33,17},{49,33},{2,50}... | collective-permute-start | bytes 2359304 | tf_op jit(solution)/shard_map/ppermute | solution.py:36
  129.4 5.1 %collective-permute-start.33 = (f32[160,128]{1,0:T(8,128)S(1)}, f32[160,128]{1,0:T(8,128)S(1)}, u32[]{:S(2)}, u32[]{:S(2)}) collective-permute-start(f32[160,128]{1,0:T(8,128)S(1)} %add_add_fusion), channel_id=1, source_target_pairs={{0,72},{8,0},{64,8},{72,64},{1,73},{9,1},{65,9},{73,65},{2,74},{10... | collective-permute-start | bytes 245768 | tf_op jit(solution)/shard_map/ppermute | solution.py:36
  131.3 22.2 %collective-permute-start.13 = (f32[2,192,512]{2,1,0:T(8,128)}, f32[2,192,512]{2,1,0:T(8,128)S(1)}, u32[]{:S(2)}, u32[]{:S(2)}) collective-permute-start(f32[2,192,512]{2,1,0:T(8,128)} %get-tuple-element.21), channel_id=1, source_target_pairs={{0,32},{16,48},{32,0},{48,16},{1,33},{17,49},{33,1},{49,17},{2,34}... | collective-permute-start | bytes 2359304 | tf_op jit(solution)/shard_map/ppermute | solution.py:36
  132.8 31.6 %collective-permute-start.12 = (f32[2,192,512]{2,1,0:T(8,128)}, f32[2,192,512]{2,1,0:T(8,128)S(1)}, u32[]{:S(2)}, u32[]{:S(2)}) collective-permute-start(f32[2,192,512]{2,1,0:T(8,128)} %get-tuple-element.20), channel_id=1, source_target_pairs={{0,16},{16,32},{32,48},{48,0},{1,17},{17,33},{33,49},{49,1},{2,18}... | collective-permute-start | bytes 2359304 | tf_op jit(solution)/shard_map/ppermute | solution.py:36
  134.5 5.9 %collective-permute-start.32 = (f32[160,128]{1,0:T(8,128)S(1)}, f32[160,128]{1,0:T(8,128)S(1)}, u32[]{:S(2)}, u32[]{:S(2)}) collective-permute-start(f32[160,128]{1,0:T(8,128)S(1)} %add_add_fusion), channel_id=1, source_target_pairs={{0,64},{8,72},{64,0},{72,8},{1,65},{9,73},{65,1},{73,9},{2,66},{10... | collective-permute-start | bytes 245768 | tf_op jit(solution)/shard_map/ppermute | solution.py:36
  136.2 5.1 %collective-permute-start.31 = (f32[160,128]{1,0:T(8,128)S(1)}, f32[160,128]{1,0:T(8,128)S(1)}, u32[]{:S(2)}, u32[]{:S(2)}) collective-permute-start(f32[160,128]{1,0:T(8,128)S(1)} %add_add_fusion), channel_id=1, source_target_pairs={{0,8},{8,64},{64,72},{72,0},{1,9},{9,65},{65,73},{73,1},{2,10},{10... | collective-permute-start | bytes 245768 | tf_op jit(solution)/shard_map/ppermute | solution.py:36
  137.2 27.1 %copy-start.2 = (f32[2,192,512]{2,1,0:T(8,128)S(1)}, f32[2,192,512]{2,1,0:T(8,128)}, u32[]{:S(2)}) copy-start(f32[2,192,512]{2,1,0:T(8,128)} %get-tuple-element.19) | copy-start | bytes 2359300
  139.9 32.8 %copy-start = (f32[2,192,512]{2,1,0:T(8,128)}, f32[2,192,512]{2,1,0:T(8,128)S(1)}, u32[]{:S(2)}) copy-start(f32[2,192,512]{2,1,0:T(8,128)S(1)} %get-tuple-element.36) | copy-start | bytes 2359300
  140.5 25.5 %collective-permute-start.18 = (f32[2,192,512]{2,1,0:T(8,128)S(1)}, f32[2,192,512]{2,1,0:T(8,128)S(1)}, u32[]{:S(2)}, u32[]{:S(2)}) collective-permute-start(f32[2,192,512]{2,1,0:T(8,128)S(1)} %get-tuple-element.37), channel_id=1, source_target_pairs={{0,6},{2,0},{4,2},{6,4},{1,7},{3,1},{5,3},{7,5},{8,14},{10,8},{12,... | collective-permute-start | bytes 2359304 | tf_op jit(solution)/shard_map/ppermute | solution.py:36
  141.2 24.7 %collective-permute-start.17 = (f32[2,192,512]{2,1,0:T(8,128)S(1)}, f32[2,192,512]{2,1,0:T(8,128)S(1)}, u32[]{:S(2)}, u32[]{:S(2)}) collective-permute-start(f32[2,192,512]{2,1,0:T(8,128)S(1)} %get-tuple-element.38), channel_id=1, source_target_pairs={{0,4},{2,6},{4,0},{6,2},{1,5},{3,7},{5,1},{7,3},{8,12},{10,14},{12... | collective-permute-start | bytes 2359304 | tf_op jit(solution)/shard_map/ppermute | solution.py:36
  145.6 29.8 %copy-start.4 = (f32[2,192,512]{2,1,0:T(8,128)}, f32[2,192,512]{2,1,0:T(8,128)S(1)}, u32[]{:S(2)}) copy-start(f32[2,192,512]{2,1,0:T(8,128)S(1)} %collective-permute-done.14) | copy-start | bytes 2359300
  145.6 27.1 %collective-permute-start.16 = (f32[2,192,512]{2,1,0:T(8,128)S(1)}, f32[2,192,512]{2,1,0:T(8,128)S(1)}, u32[]{:S(2)}, u32[]{:S(2)}) collective-permute-start(f32[2,192,512]{2,1,0:T(8,128)S(1)} %get-tuple-element.39), channel_id=1, source_target_pairs={{0,2},{2,4},{4,6},{6,0},{1,3},{3,5},{5,7},{7,1},{8,10},{10,12},{12... | collective-permute-start | bytes 2359304 | tf_op jit(solution)/shard_map/ppermute | solution.py:36
  145.6 29.8 %copy-start.13 = (f32[4,160,128]{2,1,0:T(8,128)}, f32[4,160,128]{2,1,0:T(8,128)S(1)}, u32[]{:S(2)}) copy-start(f32[4,160,128]{2,1,0:T(8,128)S(1)} %pad_maximum_fusion.2.mine) | copy-start | bytes 983044
  153.5 21.9 %copy-start.6 = (f32[2,192,512]{2,1,0:T(8,128)}, f32[2,192,512]{2,1,0:T(8,128)S(1)}, u32[]{:S(2)}) copy-start(f32[2,192,512]{2,1,0:T(8,128)S(1)} %collective-permute-done.13) | copy-start | bytes 2359300
  153.5 21.9 %collective-permute-start.34 = (f32[4,160,128]{2,1,0:T(8,128)S(1)}, f32[4,160,128]{2,1,0:T(8,128)S(1)}, u32[]{:S(2)}, u32[]{:S(2)}) collective-permute-start(f32[4,160,128]{2,1,0:T(8,128)S(1)} %pad_maximum_fusion.2.mine), channel_id=1, source_target_pairs={{0,1},{1,0},{2,3},{3,2},{4,5},{5,4},{6,7},{7,6},{8,9},{9,8},{10,11... | collective-permute-start | bytes 983048 | tf_op jit(solution)/shard_map/ppermute | solution.py:36
  164.4 11.1 %copy-start.8 = (f32[2,192,512]{2,1,0:T(8,128)}, f32[2,192,512]{2,1,0:T(8,128)S(1)}, u32[]{:S(2)}) copy-start(f32[2,192,512]{2,1,0:T(8,128)S(1)} %collective-permute-done.12) | copy-start | bytes 2359300
  165.4 26.8 %collective-permute-start.20 = (f32[192,512]{1,0:T(8,128)}, f32[192,512]{1,0:T(8,128)}, u32[]{:S(2)}, u32[]{:S(2)}) collective-permute-start(f32[192,512]{1,0:T(8,128)} %fusion.4), channel_id=1, source_target_pairs={{0,64},{64,0},{1,65},{65,1},{2,66},{66,2},{3,67},{67,3},{4,68},{68... | collective-permute-start | bytes 1179656 | tf_op jit(solution)/shard_map/ppermute | solution.py:36
  173.7 18.6 %collective-permute-start.19 = (f32[192,512]{1,0:T(8,128)}, f32[192,512]{1,0:T(8,128)}, u32[]{:S(2)}, u32[]{:S(2)}) collective-permute-start(f32[192,512]{1,0:T(8,128)} %fusion.5), channel_id=1, source_target_pairs={{0,8},{8,0},{1,9},{9,1},{2,10},{10,2},{3,11},{11,3},{4,12},{12,4},... | collective-permute-start | bytes 1179656 | tf_op jit(solution)/shard_map/ppermute | solution.py:36
  176.2 13.5 %copy-start.1 = (f32[2,192,512]{2,1,0:T(8,128)S(1)}, f32[2,192,512]{2,1,0:T(8,128)}, u32[]{:S(2)}) copy-start(f32[2,192,512]{2,1,0:T(8,128)} %copy-done) | copy-start | bytes 2359300
  176.2 13.5 %copy-start.3 = (f32[2,192,512]{2,1,0:T(8,128)S(1)}, f32[2,192,512]{2,1,0:T(8,128)}, u32[]{:S(2)}) copy-start(f32[2,192,512]{2,1,0:T(8,128)} %get-tuple-element.19) | copy-start | bytes 2359300
  176.2 13.5 %copy-start.5 = (f32[2,192,512]{2,1,0:T(8,128)S(1)}, f32[2,192,512]{2,1,0:T(8,128)}, u32[]{:S(2)}) copy-start(f32[2,192,512]{2,1,0:T(8,128)} %copy-done.4) | copy-start | bytes 2359300
  176.2 13.5 %copy-start.7 = (f32[2,192,512]{2,1,0:T(8,128)S(1)}, f32[2,192,512]{2,1,0:T(8,128)}, u32[]{:S(2)}) copy-start(f32[2,192,512]{2,1,0:T(8,128)} %copy-done.6) | copy-start | bytes 2359300
  176.2 13.5 %copy-start.9 = (f32[2,192,512]{2,1,0:T(8,128)S(1)}, f32[2,192,512]{2,1,0:T(8,128)}, u32[]{:S(2)}) copy-start(f32[2,192,512]{2,1,0:T(8,128)} %copy-done.8) | copy-start | bytes 2359300
  (7 other events, 32.5 us)

commit v2 on v1

v2 whole, which is shorter than its diff:
```python
import functools

import jax
import jax.numpy as jnp
from jax import lax
from jax.experimental import pallas as pl
from jax.experimental.pallas import tpu as pltpu
from jax.sharding import Mesh, PartitionSpec as P

f32 = jnp.float32
bf16 = jnp.bfloat16
f16 = jnp.float16
U = 192
B = 512
BLK = 128
NB = B // BLK
LOWER = [(i, j) for i in range(NB) for j in range(i + 1)]
CH = len(LOWER) * BLK // 8
VMEM_LIMIT = 60 * 1024 * 1024


def whole():
    return pl.BlockSpec(memory_space=pltpu.VMEM)


def params(**kw):
    return pltpu.CompilerParams(vmem_limit_bytes=VMEM_LIMIT, **kw)


def hi_dot(a, b, dims):
    return lax.dot_general(
        a, b, (dims, ((), ())), precision=lax.Precision.HIGHEST, preferred_element_type=f32
    )


def shift(x, axis, k, n=4):
    return lax.ppermute(x, axis, [(i, (i + k) % n) for i in range(n)])


def iotas(n):
    return (
        lax.broadcasted_iota(jnp.int32, (n, n), 0),
        lax.broadcasted_iota(jnp.int32, (n, n), 1),
    )


def block(ref, i, j):
    return ref[i * BLK : (i + 1) * BLK, j * BLK : (j + 1) * BLK]


def prep_kernel(l_ref, pg_ref, p_ref, inv_ref, g_ref):
    rows, cols = iotas(BLK)
    blocks = []
    inv = []
    for b in range(NB):
        m = jnp.where(rows >= cols, block(l_ref, b, b), 0.0)
        blocks.append(m)
        inv.append(jnp.where(rows == cols, 1.0 / jnp.where(rows == cols, m, 1.0), 0.0))
    s = 1
    while s < BLK:
        sel = (rows // s != cols // s) & (rows // (2 * s) == cols // (2 * s))
        right = [hi_dot(jnp.where(sel, blocks[b], 0.0), inv[b], ((1,), (0,))) for b in range(NB)]
        inv = [inv[b] - hi_dot(inv[b], right[b], ((1,), (0,))) for b in range(NB)]
        s *= 2
    for b in range(NB):
        inv_ref[b] = inv[b]
    p = p_ref[...]
    g = pg_ref[...]
    total = None
    for _ in range(3):
        part = g.astype(bf16)
        g = g - part.astype(f32)
        term = lax.dot_general(part, p, (((0,), (0,)), ((), ())), preferred_element_type=f32)
        total = term if total is None else total + term
    g_ref[...] = total


def prep(lower, panel_grad, panel):
    return pl.pallas_call(
        prep_kernel,
        out_shape=(
            jax.ShapeDtypeStruct((NB, BLK, BLK), f32),
            jax.ShapeDtypeStruct((B, B), f32),
        ),
        in_specs=[whole()] * 3,
        out_specs=(whole(), whole()),
        compiler_params=params(),
        cost_estimate=pl.CostEstimate(flops=4_000_000_000, bytes_accessed=3_000_000, transcendentals=0),
        name="prep",
    )(lower, panel_grad, panel)


DIM0 = (((0,), (0,)), ((), ()))
ANY = pl.BlockSpec(memory_space=pl.ANY)


def band(ref, i):
    return ref.at[pl.ds(pl.multiple_of(i * U, U), U), :]


def pair_kernel(p, xs, zs, *refs):
    x_two, z_two, sem = refs[-3:]
    jobs = [(p, x_two.at[0]), (p, z_two.at[0]), (xs, x_two.at[1]), (zs, z_two.at[1])]
    copies = [pltpu.make_async_copy(a, b, sem.at[i]) for i, (a, b) in enumerate(jobs)]
    for cp in copies:
        cp.start()
    for cp in copies:
        cp.wait()


def pair(p, xs, zs, *after):
    return pl.pallas_call(
        pair_kernel,
        out_shape=[jax.ShapeDtypeStruct((2, U, B), bf16)] * 2,
        in_specs=[ANY] * (3 + len(after)),
        out_specs=[ANY] * 2,
        scratch_shapes=[pltpu.SemaphoreType.DMA((4,))],
        compiler_params=params(),
        cost_estimate=pl.CostEstimate(flops=0, bytes_accessed=1_600_000, transcendentals=0),
        name="pair",
    )(p, xs, zs, *after)


def direct_kernel(s_ref, f_ref, own, swp, r1, r2, r3, *refs):
    refs = refs[-10:]
    mine, other, pc, keep, give, s_in, s_out = refs[:4], *refs[4:]
    step = pl.program_id(0)
    x, yh, c = s_ref[8], s_ref[9], s_ref[10]
    copies = []
    for k in range(4):
        copies.append(
            (
                pltpu.make_async_copy(keep.at[k], mine[k], s_out.at[k]),
                pltpu.make_async_copy(give.at[k], other.at[k], s_out.at[4 + k]),
            )
        )

    @pl.when(step == 0)
    def _():
        jobs = [(yh * 4 + x, own), ((1 - yh) * 4 + x, swp)]
        for k, r in ((1, r1), (2, r2), (3, r3)):
            xs = lax.rem(x + 4 - k, 4)
            jobs += [(yh * 4 + xs, r.at[0]), ((1 - yh) * 4 + xs, r.at[1])]
        ins = [pltpu.make_async_copy(src, band(pc, a), s_in.at[i]) for i, (a, src) in enumerate(jobs)]
        for cp in ins:
            cp.start()
        for cp in ins:
            cp.wait()

    d = lax.dot_general(f_ref[...], pc[...], DIM0, preferred_element_type=f32)
    lo, hi = d[:U], d[U:]
    first = c == 0
    keep[step // 2, step % 2] = jnp.where(first, lo, hi)
    give[step // 2, step % 2] = jnp.where(first, hi, lo)
    for k in range(4):

        @pl.when(step == 2 * k + 1)
        def _():
            for cp in copies[k]:
                cp.start()

    @pl.when(step == 7)
    def _():
        for two in copies:
            for cp in two:
                cp.wait()


def direct(scalars, flip, own, swp, recv, *after):
    grid_spec = pltpu.PrefetchScalarGridSpec(
        num_scalar_prefetch=1,
        grid=(8,),
        in_specs=[pl.BlockSpec((8 * U, 2 * U), lambda i, s: (0, s[i]))] + [ANY] * (5 + len(after)),
        out_specs=[ANY] * 5,
        scratch_shapes=[
            pltpu.VMEM((8 * U, B), bf16),
            pltpu.VMEM((4, 2, U, B), f32),
            pltpu.VMEM((4, 2, U, B), f32),
            pltpu.SemaphoreType.DMA((8,)),
            pltpu.SemaphoreType.DMA((8,)),
        ],
    )
    out = pl.pallas_call(
        direct_kernel,
        grid_spec=grid_spec,
        out_shape=[jax.ShapeDtypeStruct((2, U, B), f32)] * 4
        + [jax.ShapeDtypeStruct((4, 2, U, B), f32)],
        compiler_params=params(),
        cost_estimate=pl.CostEstimate(flops=14_000_000_000, bytes_accessed=17_000_000, transcendentals=0),
        name="direct",
    )(scalars, flip, own, swp, *recv, *after)
    return out[:4], out[4]


def transposed_kernel(s_ref, f0, f1, *refs):
    zown, zr, pown, prr = refs[0:2], refs[2:5], refs[5], refs[6:9]
    xown, xr = refs[9:11], refs[11:14]
    refs = refs[-11:]
    outs, st_ref, pr, pc, acc, tbuf, s_in, s_out = refs[:4], *refs[4:]
    step = pl.program_id(0)
    z, yl, c = s_ref[8], s_ref[9], s_ref[10]
    copies = [pltpu.make_async_copy(tbuf.at[k], outs[k], s_out.at[k]) for k in range(4)]
    copies.append(pltpu.make_async_copy(acc, st_ref, s_out.at[4]))

    def place(zb, yb, cb):
        return (yb * 4 + zb) * 2 + cb

    rows_in = [
        (place(z, yl, c), zown[0]),
        (place(z, 1 - yl, c), zown[1]),
        (place(z, yl, 1 - c), pown.at[0]),
        (place(z, 1 - yl, 1 - c), pown.at[1]),
    ]
    for k in (1, 2, 3):
        zs = lax.rem(z + 4 - k, 4)
        for m, yb in ((0, yl), (1, 1 - yl)):
            rows_in += [(place(zs, yb, c), zr[k - 1].at[m]), (place(zs, yb, 1 - c), prr[k - 1].at[m])]
    ins = [pltpu.make_async_copy(src, band(pr, a), s_in.at[i]) for i, (a, src) in enumerate(rows_in)]
    locals_ = [xown[0], xown[1]] + [xr[3 - k].at[m] for k in (1, 2, 3) for m in (0, 1)]
    ins_c = [pltpu.make_async_copy(src, band(pc, i), s_in.at[16 + i]) for i, src in enumerate(locals_)]

    @pl.when(step == 0)
    def _():
        for cp in ins + ins_c:
            cp.start()
        acc[...] = jnp.zeros_like(acc)
        for cp in ins:
            cp.wait()

    f = jnp.concatenate([f0[...], f1[...]], axis=0)
    t = jnp.dot(f, pr[...], preferred_element_type=f32)
    tbuf[step, 0] = t[:U]
    tbuf[step, 1] = t[U:]
    for k in range(4):

        @pl.when(step == k)
        def _():
            copies[k].start()

    @pl.when(step == 0)
    def _():
        for cp in ins_c:
            cp.wait()

    hi = t.astype(bf16)
    lo = (t - hi.astype(f32)).astype(bf16)
    p = pc[pl.ds(pl.multiple_of(step * 2 * U, 2 * U), 2 * U), :]
    acc[...] += lax.dot_general(p, hi, DIM0, preferred_element_type=f32) + lax.dot_general(
        p, lo, DIM0, preferred_element_type=f32
    )

    @pl.when(step == 3)
    def _():
        copies[4].start()
        for cp in copies:
            cp.wait()


def transposed(scalars, flip, zown, zr, pown, prr, xown, xr, *after):
    grid_spec = pltpu.PrefetchScalarGridSpec(
        num_scalar_prefetch=1,
        grid=(4,),
        in_specs=[
            pl.BlockSpec((U, 16 * U), lambda i, s: (s[2 * i], 0)),
            pl.BlockSpec((U, 16 * U), lambda i, s: (s[2 * i + 1], 0)),
        ]
        + [ANY] * (14 + len(after)),
        out_specs=[ANY] * 5,
        scratch_shapes=[
            pltpu.VMEM((16 * U, B), bf16),
            pltpu.VMEM((8 * U, B), bf16),
            pltpu.VMEM((B, B), f32),
            pltpu.VMEM((4, 2, U, B), f32),
            pltpu.SemaphoreType.DMA((24,)),
            pltpu.SemaphoreType.DMA((5,)),
        ],
    )
    out = pl.pallas_call(
        transposed_kernel,
        grid_spec=grid_spec,
        out_shape=[jax.ShapeDtypeStruct((2, U, B), f32)] * 4 + [jax.ShapeDtypeStruct((B, B), f32)],
        compiler_params=params(),
        cost_estimate=pl.CostEstimate(flops=15_000_000_000, bytes_accessed=17_000_000, transcendentals=0),
        name="transposed",
    )(scalars, flip, flip, *zown, *zr, pown, *prr, *xown, *xr, *after)
    return out[:4], out[4]


def ring_kernel(a, b, c, d, *refs):
    refs[-1][...] = (a[...] + c[...]) + (b[...] + d[...])


def ring_sum(a, b, c, d, *after):
    return pl.pallas_call(
        ring_kernel,
        out_shape=jax.ShapeDtypeStruct((CH, BLK), f32),
        in_specs=[whole()] * 4 + [ANY] * len(after),
        out_specs=whole(),
        compiler_params=params(),
        cost_estimate=pl.CostEstimate(flops=100_000, bytes_accessed=500_000, transcendentals=0),
        name="ring_sum",
    )(a, b, c, d, *after)


def pack_kernel(s_ref, g_ref, st_ref, *refs):
    mine, other, flat = refs[:4], refs[4], refs[5]
    c, y = s_ref[0], s_ref[1]
    for n, (i, j) in enumerate(LOWER):
        flat[n * BLK : (n + 1) * BLK, :] = block(g_ref, i, j) - block(st_ref, i, j) - block(st_ref, j, i).T
    for k in range(4):
        q = lax.rem(y + k, 4)
        mine[k][...] = flat[pl.ds(pl.multiple_of((c * 4 + q) * CH, CH), CH), :]
        other[k] = flat[pl.ds(pl.multiple_of(((1 - c) * 4 + q) * CH, CH), CH), :]


def pack(scalars, g, st):
    out = pl.pallas_call(
        pack_kernel,
        out_shape=[jax.ShapeDtypeStruct((CH, BLK), f32)] * 4 + [jax.ShapeDtypeStruct((4, CH, BLK), f32)],
        in_specs=[pl.BlockSpec(memory_space=pltpu.SMEM)] + [whole()] * 2,
        out_specs=[whole()] * 5,
        scratch_shapes=[pltpu.VMEM((8 * CH, BLK), f32)],
        compiler_params=params(),
        cost_estimate=pl.CostEstimate(flops=2_000_000, bytes_accessed=3_000_000, transcendentals=0),
        name="pack",
    )(scalars, g, st)
    return out[:4], out[4]


def split(a):
    hi = a.astype(bf16)
    return hi, (a - hi.astype(f32)).astype(bf16)


def cat(parts, axis):
    return parts[0] if len(parts) == 1 else jnp.concatenate(parts, axis=axis)


def cat2(pairs, axis):
    return cat([p[0] for p in pairs], axis), cat([p[1] for p in pairs], axis)


def dot3(a, b):
    return jnp.dot(cat([a[0], a[0], a[1]], 1), cat([b[0], b[1], b[0]], 0), preferred_element_type=f32)


def tail_kernel(s_ref, mine, other, l_ref, inv_ref, dg_ref, *refs):
    out_ref, flat = refs[-2:]
    c, y = s_ref[0], s_ref[1]
    for k in range(4):
        q = lax.rem(y + 4 - k, 4)
        flat[pl.ds(pl.multiple_of((c * 4 + q) * CH, CH), CH), :] = mine[k]
        flat[pl.ds(pl.multiple_of(((1 - c) * 4 + q) * CH, CH), CH), :] = other[k]
    rows, cols = iotas(BLK)
    tri = rows >= cols
    low = {ij: block(l_ref, *ij) for ij in LOWER}
    for i in range(NB):
        low[i, i] = jnp.where(tri, low[i, i], 0.0)
    low_t = {ij: split(v.T) for ij, v in low.items()}
    low_n = {ij: split(v) for ij, v in low.items()}
    inv_n = [split(inv_ref[i]) for i in range(NB)]
    inv_t = [split(inv_ref[i].T) for i in range(NB)]
    q = {ij: flat[n * BLK : (n + 1) * BLK, :] for n, ij in enumerate(LOWER)}
    acc = {i: cat([q[i, j] for j in range(i + 1)], 1) for i in range(NB)}
    new = {}
    for i in reversed(range(NB)):
        con = dot3(inv_t[i], split(acc[i]))
        if i:
            part = tuple(v[:, : i * BLK] for v in split(con))
            upd = dot3(cat2([low_t[i, r] for r in range(i)], 0), part)
            for r in range(i):
                acc[r] = acc[r] - upd[r * BLK : (r + 1) * BLK, : (r + 1) * BLK]
        n = dg_ref[i * BLK : (i + 1) * BLK, : (i + 1) * BLK] - con
        corner = jnp.where(tri, n[:, i * BLK :], 0.0)
        new[i] = split(corner if i == 0 else cat([n[:, : i * BLK], corner], 1))
    keep = jnp.where(rows > cols, 1.0, jnp.where(rows == cols, 0.5, 0.0))
    inner = {}
    for i in range(NB):
        width = (i + 1) * BLK
        r = dot3(
            cat2([low_t[k, i] for k in range(i, NB)], 1),
            cat2([tuple(v[:, :width] for v in new[k]) for k in range(i, NB)], 0),
        )
        parts = [] if i == 0 else [r[:, : i * BLK]]
        parts.append(r[:, i * BLK :] * keep)
        if width < B:
            parts.append(jnp.zeros((BLK, B - width), f32))
        inner[i] = cat(parts, 1)
    left = {}
    for i in reversed(range(NB)):
        left[i] = dot3(inv_t[i], split(inner[i]))
        if i:
            upd = dot3(cat2([low_t[i, r] for r in range(i)], 0), split(left[i]))
            for r in range(i):
                inner[r] = inner[r] - upd[r * BLK : (r + 1) * BLK]
    acc = cat([left[i] for i in range(NB)], 0)
    right = {}
    for j in reversed(range(NB)):
        right[j] = dot3(split(acc[:, j * BLK : (j + 1) * BLK]), inv_n[j])
        if j:
            upd = dot3(split(right[j]), cat2([low_n[j, r] for r in range(j)], 1))
            acc = acc[:, : j * BLK] - upd
    for i in range(NB):
        for j in range(i + 1):
            v = 0.5 * (right[j][i * BLK : (i + 1) * BLK] + right[i][j * BLK : (j + 1) * BLK].T)
            out_ref[i * BLK : (i + 1) * BLK, j * BLK : (j + 1) * BLK] = v
            if i != j:
                out_ref[j * BLK : (j + 1) * BLK, i * BLK : (i + 1) * BLK] = v.T


def tail(scalars, mine, other, lower, inv, diag_grad, *after):
    return pl.pallas_call(
        tail_kernel,
        out_shape=jax.ShapeDtypeStruct((B, B), f32),
        in_specs=[pl.BlockSpec(memory_space=pltpu.SMEM)] + [whole()] * 5 + [ANY] * len(after),
        out_specs=whole(),
        scratch_shapes=[pltpu.VMEM((8 * CH, BLK), f32)],
        compiler_params=params(),
        cost_estimate=pl.CostEstimate(flops=8_000_000_000, bytes_accessed=5_000_000, transcendentals=0),
        name="tail",
    )(scalars, mine, other, lower, inv, diag_grad, *after)


def solve_kernel(r_ref, d_ref, t_ref, l_ref, inv_ref, out_ref):
    r = r_ref[...] - d_ref[...] - t_ref[...]
    xs = {}
    for j in reversed(range(NB)):
        acc = r[:, j * BLK : (j + 1) * BLK]
        for k in range(j + 1, NB):
            acc = acc - hi_dot(xs[k], block(l_ref, k, j), ((1,), (0,)))
        xs[j] = hi_dot(acc, inv_ref[j], ((1,), (0,)))
        out_ref[:, j * BLK : (j + 1) * BLK] = xs[j]


def solve(r, d, t, lower, inv):
    return pl.pallas_call(
        solve_kernel,
        out_shape=jax.ShapeDtypeStruct((U, B), f32),
        in_specs=[whole()] * 5,
        out_specs=whole(),
        compiler_params=params(),
        cost_estimate=pl.CostEstimate(flops=1_000_000_000, bytes_accessed=3_000_000, transcendentals=0),
        name="solve",
    )(r, d, t, lower, inv)


def on_device(trailing_grad, panel, panel_grad, diag_factor, diag_grad):
    flip = trailing_grad.reshape(-1, trailing_grad.shape[3])
    x, yh = lax.axis_index("x"), lax.axis_index("yh")
    z, yl, c = lax.axis_index("z"), lax.axis_index("yl"), lax.axis_index("c")
    y = yh * 2 + yl
    ints = lambda *v: jnp.stack([jnp.asarray(e, jnp.int32) for e in v])
    d_scal = ints(*[(yl ^ m) * 4 + (z + k) % 4 for k in range(4) for m in range(2)], x, yh, c)
    t_scal = ints(*[(yh ^ m) * 4 + (x + k) % 4 for k in range(4) for m in range(2)], z, yl, c, x, yh)
    cy = ints(c, y)

    x_swp = shift(panel, "yh", 1, 2)
    z_swp = shift(panel, "yl", 1, 2)
    inv, g = prep(diag_factor, panel_grad, panel)
    x_two, z_two = pair(panel, x_swp, z_swp, inv)
    x_recv = [None] * 4
    z_recv = [None] * 4
    for k in (2, 1, 3):
        z_recv[k] = shift(z_two, "z", k)
        x_recv[k] = shift(x_two, "x", k)
    pair_own = shift(z_two, "c", 1, 2)
    pair_recv = [None] + [shift(z_recv[k], "c", 1, 2) for k in (1, 2, 3)]

    d_mine, d_other = direct(d_scal, flip, panel, x_swp, x_recv[1:], *z_recv[1:])
    d_pair = shift(d_other, "c", 1, 2)
    t_own, st = transposed(
        t_scal, flip, (panel, z_swp), z_recv[1:], pair_own, pair_recv[1:], (panel, x_swp), x_recv[1:]
    )

    half = lambda v: (v * 64.0).astype(f16)
    full = lambda v: v.astype(f32) * (1 / 64.0)
    t_in = [None] * 4
    for k in (2, 1, 3):
        t_in[k] = shift(half(t_own[k]), "x", k)
    d_sum = [d_mine[k] + d_pair[k] for k in range(4)]
    d_in = [None] * 4
    for k in (2, 1, 3):
        d_in[k] = shift(half(d_sum[k]), "z", k)
    t_far = t_own[0][1] + (full(t_in[1][1]) + full(t_in[2][1]) + full(t_in[3][1]))
    d_far = d_sum[0][1] + (full(d_in[1][1]) + full(d_in[2][1]) + full(d_in[3][1]))
    t_last = shift(t_far, "yh", 1, 2)
    d_last = shift(d_far, "yl", 1, 2)
    near = (
        panel_grad
        - (t_own[0][0] + (full(t_in[1][0]) + full(t_in[2][0]) + full(t_in[3][0])))
        - (d_sum[0][0] + (full(d_in[1][0]) + full(d_in[2][0]) + full(d_in[3][0])))
    )
    panel_adj = solve(near, d_last, t_last, diag_factor, inv)

    q_mine, q_other = pack(cy, g, st)
    q_pair = shift(q_other, "c", 1, 2)
    q = [q_mine[k] + q_pair[k] for k in range(4)]
    q_in = [shift(q[k], ("yh", "yl"), k) for k in (1, 2, 3)]
    part = q[0] + q_in[0] + q_in[1] + q_in[2]
    part = ring_sum(part, *[shift(part, "z", k) for k in (1, 2, 3)])
    part = ring_sum(part, *[shift(part, "x", k) for k in (1, 2, 3)], t_far, d_far)
    q_all = jnp.stack([part] + [shift(part, ("yh", "yl"), k) for k in (1, 2, 3)])
    diag_adj = tail(cy, q_all, shift(q_all, "c", 1, 2), diag_factor, inv, diag_grad)
    return panel_adj, diag_adj


def solution(mesh):
    fine = Mesh(mesh.devices.reshape(2, 4, 2, 4, 2), ("yh", "x", "yl", "z", "c"))
    row, col = ("yh", "x"), ("yl", "z", "c")
    return jax.shard_map(
        on_device,
        mesh=fine,
        in_specs=(P(None, col, None, row), P(row + col, None), P(row + col, None), P(), P()),
        out_specs=(P(row + col, None), P()),
        check_vma=False,
    )
```

time: 198 us -> 198 us (level)
  waiting for transfers between devices: 85.6 us -> 45.8 us
  Pallas kernels: 55.2 us -> 78.6 us
  starting transfers between devices: 41 us -> 57 us
    ppermute x35, waiting for transfers between devices: 85.6 us -> 45.8 us  [shift(): return lax.ppermute(x, axis, [(i, (i + k) % n) for i in range(n)])]
    pallas_call x0 -> x3, Pallas kernels: none -> 28.3 us  [the longest x1 25 us: pair(): pl.pallas_call(pair_kernel, out_shape=[jax.ShapeDtypeStruct((2, U, B), bf...]
    ppermute x35, starting transfers between devices: 41 us -> 57 us  [shift(): return lax.ppermute(x, axis, [(i, (i + k) % n) for i in range(n)])]
    convert_element_type x0 -> x4, other arithmetic: none -> 5.58 us  [on_device(): half = lambda v: (v * 64.0).astype(f16)]
    pallas_call x1, Pallas kernels: 13.5 us -> 8.13 us  [tail(): pl.pallas_call(tail_kernel, out_shape=jax.ShapeDtypeStruct((B, B), f32),...]
    add x5 -> x2, other arithmetic: 4.76 us -> 2.86 us  [the longest x1 2 us: on_device(): d_sum[0][1] + (full(d_in[1][1]) + full(d_in[2][1]) + full(d_in[3][1]))]
  transfers between devices with their start and end apart: 35 -> 35, of which waited for: 20 -> 16; matrix products, arithmetic and copies ran while one was open for 6% -> 7% of each run, Pallas kernels for 19% -> 15%
where the time goes in v2:
time: 198 us; the launch traced here: 197 us
  Pallas kernels  78.6 us (40%)
  starting transfers between devices  57 us (29%)
  waiting for transfers between devices  45.8 us (23%)
  other arithmetic  12 us (6%)
  local copies, waits for them, and re-layouts  2.88 us (1%)
    ppermute x35, starting transfers between devices, shift(): return lax.ppermute(x, axis, [(i, (i + k) % n) for i in range(n)])  57 us
    ppermute x35, waiting for transfers between devices, shift(): return lax.ppermute(x, axis, [(i, (i + k) % n) for i in range(n)])  45.8 us
    pallas_call x1, Pallas kernels, pair(): pl.pallas_call(pair_kernel, out_shape=[jax.ShapeDtypeStruct((2, U, B), bf...  25 us
    pallas_call x1, Pallas kernels, direct(): pl.pallas_call(direct_kernel, grid_spec=grid_spec, out_shape=[jax.ShapeDt...  14.4 us
    pallas_call x1, Pallas kernels, transposed(): pl.pallas_call(transposed_kernel, grid_spec=grid_spec, out_shape=[jax.Sha...  14.2 us
    pallas_call x1, Pallas kernels, tail(): pl.pallas_call(tail_kernel, out_shape=jax.ShapeDtypeStruct((B, B), f32),...  8.13 us
    pallas_call x1, Pallas kernels, prep(): pl.pallas_call(prep_kernel, out_shape=(jax.ShapeDtypeStruct((NB, BLK, BLK...  6.59 us
    convert_element_type x4, other arithmetic, on_device(): half = lambda v: (v * 64.0).astype(f16)  5.58 us
  transfers between devices with their start and end apart: 35, of which 16 were waited for; matrix products, arithmetic and copies ran while one was open for 7% of the time, Pallas kernels for 15%

profile of v2, /device:TPU:8, one launch (start us, length us, event | category | flops | bytes accessed | tf_op | source)
XLA Modules:
  0.0 197.3 jit_solution(18247246487861440738)
XLA Ops:
  0.6 2.4 %collective-permute-start.1 = (bf16[192,512]{1,0:T(8,128)(2,1)}, bf16[192,512]{1,0:T(8,128)(2,1)S(1)}, u32[]{:S(2)}, u32[]{:S(2)}) collective-permute-start(bf16[192,512]{1,0:T(8,128)(2,1)} %own.1), channel_id=1, source_target_pairs={{0,64},{64,0},{1,65},{65,1},{2,66},{66,2},{3,67},{67,3},{4,68},{68... | collective-permute-start | bytes 589832 | tf_op jit(solution)/shard_map/ppermute | solution.py:37
  3.0 1.3 collective-permute-start
  4.4 6.6 %prep.1 = (f32[4,128,128]{2,1,0:T(8,128)}, f32[512,512]{1,0:T(8,128)}) custom-call(f32[512,512]{1,0:T(8,128)} %l_ref.5, f32[192,512]{1,0:T(8,128)} %pg_ref.1, bf16[192,512]{1,0:T(8,128)(2,1)} %own.1), custom_call_target="tpu_custom_call" | custom-call | flops 4000000000 | bytes 3000000 | tf_op jit(solution)/shard_map/prep/pallas_call | solution.py:79
  10.9 2.4 %collective-permute-done.zs.refs_1_ = bf16[192,512]{1,0:T(8,128)(2,1)S(1)} collective-permute-done((bf16[192,512]{1,0:T(8,128)(2,1)}, bf16[192,512]{1,0:T(8,128)(2,1)S(1)}, u32[]{:S(2)}, u32[]{:S(2)}) %collective-permute-start) | collective-permute-done | bytes 196640 | tf_op jit(solution)/shard_map/ppermute | solution.py:37
  14.1 25.0 %pair.1 = (bf16[2,192,512]{2,1,0:T(8,128)(2,1)}, bf16[2,192,512]{2,1,0:T(8,128)(2,1)}) custom-call(bf16[192,512]{1,0:T(8,128)(2,1)} %own.1, bf16[192,512]{1,0:T(8,128)(2,1)} %copy-done.16, bf16[192,512]{1,0:T(8,128)(2,1)} %copy-done.17, f32[4,128,128]{2,1,0:T(8,128)} %get-tuple-element.21.refs_0_.inv_ref), custom_call_target="tpu_custom_call" | custom-call | bytes 1600000 | tf_op jit(solution)/shard_map/pair/pallas_call | solution.py:112
  39.0 2.0 %collective-permute-start.2 = (bf16[2,192,512]{2,1,0:T(8,128)(2,1)}, bf16[2,192,512]{2,1,0:T(8,128)(2,1)S(1)}, u32[]{:S(2)}, u32[]{:S(2)}) collective-permute-start(bf16[2,192,512]{2,1,0:T(8,128)(2,1)} %get-tuple-element.22), channel_id=1, source_target_pairs={{0,2},{2,4},{4,6},{6,0},{1,3},{3,5},{5,7},{7,1},{8,10},{10,12},{12... | collective-permute-start | bytes 1179656 | tf_op jit(solution)/shard_map/ppermute | solution.py:37
  41.0 3.6 %collective-permute-start.3 = (bf16[2,192,512]{2,1,0:T(8,128)(2,1)}, bf16[2,192,512]{2,1,0:T(8,128)(2,1)S(1)}, u32[]{:S(2)}, u32[]{:S(2)}) collective-permute-start(bf16[2,192,512]{2,1,0:T(8,128)(2,1)} %get-tuple-element.22), channel_id=1, source_target_pairs={{0,4},{2,6},{4,0},{6,2},{1,5},{3,7},{5,1},{7,3},{8,12},{10,14},{12... | collective-permute-start | bytes 1179656 | tf_op jit(solution)/shard_map/ppermute | solution.py:37
  44.6 1.0 collective-permute-start.4
  45.6 3.0 %collective-permute-start.10 = (bf16[2,192,512]{2,1,0:T(8,128)(2,1)}, bf16[2,192,512]{2,1,0:T(8,128)(2,1)S(1)}, u32[]{:S(2)}, u32[]{:S(2)}) collective-permute-start(bf16[2,192,512]{2,1,0:T(8,128)(2,1)} %get-tuple-element.23), channel_id=1, source_target_pairs={{0,32},{16,48},{32,0},{48,16},{1,33},{17,49},{33,1},{49,17},{2,34}... | collective-permute-start | bytes 1179656 | tf_op jit(solution)/shard_map/ppermute | solution.py:37
  48.6 1.1 collective-permute-start.11
  49.8 2.7 %collective-permute-done.2.refs_2_.refs_0_ = bf16[2,192,512]{2,1,0:T(8,128)(2,1)S(1)} collective-permute-done((bf16[2,192,512]{2,1,0:T(8,128)(2,1)}, bf16[2,192,512]{2,1,0:T(8,128)(2,1)S(1)}, u32[]{:S(2)}, u32[]{:S(2)}) %collective-permute-start.2) | collective-permute-done | bytes 393248 | tf_op jit(solution)/shard_map/ppermute | solution.py:37
  52.5 1.5 collective-permute-start.9
  54.7 6.5 %collective-permute-done.3.refs_3_.refs_1_ = bf16[2,192,512]{2,1,0:T(8,128)(2,1)S(1)} collective-permute-done((bf16[2,192,512]{2,1,0:T(8,128)(2,1)}, bf16[2,192,512]{2,1,0:T(8,128)(2,1)S(1)}, u32[]{:S(2)}, u32[]{:S(2)}) %collective-permute-start.3) | collective-permute-done | bytes 393248 | tf_op jit(solution)/shard_map/ppermute | solution.py:37
  61.2 3.8 %collective-permute-done.11.refs_13_.r3 = bf16[2,192,512]{2,1,0:T(8,128)(2,1)S(1)} collective-permute-done((bf16[2,192,512]{2,1,0:T(8,128)(2,1)}, bf16[2,192,512]{2,1,0:T(8,128)(2,1)S(1)}, u32[]{:S(2)}, u32[]{:S(2)}) %collective-permute-start.11) | collective-permute-done | bytes 393248 | tf_op jit(solution)/shard_map/ppermute | solution.py:37
  65.9 14.4 %direct.1 = (f32[2,192,512]{2,1,0:T(8,128)}, f32[2,192,512]{2,1,0:T(8,128)}, f32[2,192,512]{2,1,0:T(8,128)}, f32[2,192,512]{2,1,0:T(8,128)}, f32[4,2,192,512]{3,2,1,0:T(8,128)}) custom-call(s32[11]{0:T(128)} %stack.116.s_ref, bf16[1536,3072]{1,0:T(8,128)(2,1)} %bitcast.93, bf16[192,512]{1,0:T(8,128)(2,1)} %own.1, bf16[192,512]{1,0:T(8,128)(2,1)} %copy-done.16, ...), custom_call_target="tpu_custom_call" | custom-call | flops 14000000000 | bytes 17000000 | tf_op jit(solution)/shard_map/direct/pallas_call | solution.py:183
  82.7 4.7 %collective-permute-done.5.refs_5_ = bf16[2,192,512]{2,1,0:T(8,128)(2,1)S(1)} collective-permute-done((bf16[2,192,512]{2,1,0:T(8,128)(2,1)}, bf16[2,192,512]{2,1,0:T(8,128)(2,1)S(1)}, u32[]{:S(2)}, u32[]{:S(2)}) %collective-permute-start.5) | collective-permute-done | bytes 393248 | tf_op jit(solution)/shard_map/ppermute | solution.py:37
  88.7 14.2 %transposed.1 = (f32[2,192,512]{2,1,0:T(8,128)}, f32[2,192,512]{2,1,0:T(8,128)}, f32[2,192,512]{2,1,0:T(8,128)}, f32[2,192,512]{2,1,0:T(8,128)}, f32[512,512]{1,0:T(8,128)}) custom-call(s32[13]{0:T(128)} %stack.107.s_ref, bf16[1536,3072]{1,0:T(8,128)(2,1)} %bitcast.94, bf16[1536,3072]{1,0:T(8,128)(2,1)} %bitcast.95, bf16[192,512]{1,0:T(8,128)(2,1)} %own.1, ...), custom_call_target="tpu_custom_call" | custom-call | flops 15000000512 | bytes 17000000 | tf_op jit(solution)/shard_map/transposed/pallas_call | solution.py:278
  102.9 2.6 %pack.1 = (f32[160,128]{1,0:T(8,128)}, f32[160,128]{1,0:T(8,128)}, f32[160,128]{1,0:T(8,128)}, f32[160,128]{1,0:T(8,128)}, f32[4,160,128]{2,1,0:T(8,128)}) custom-call(s32[2]{0:T(128)} %pad_add_fusion.s_ref, f32[512,512]{1,0:T(8,128)} %get-tuple-element.33.g_ref, f32[512,512]{1,0:T(8,128)} %get-tuple-element.34.st_ref), custom_call_target="tpu_custom_call" | custom-call | flops 2000000 | bytes 3000000 | tf_op jit(solution)/shard_map/pack/pallas_call | solution.py:317
  105.8 1.4 multiply_convert_fusion.2
  107.2 1.4 collective-permute-start.12
  108.6 1.2 multiply_convert_fusion.1
  109.8 2.8 %collective-permute-start.13 = (f16[2,192,512]{2,1,0:T(8,128)(2,1)S(1)}, f16[2,192,512]{2,1,0:T(8,128)(2,1)S(1)}, u32[]{:S(2)}, u32[]{:S(2)}) collective-permute-start(f16[2,192,512]{2,1,0:T(8,128)(2,1)S(1)} %multiply_convert_fusion.1), channel_id=1, source_target_pairs={{0,32},{16,48},{32,0},{48,16},{1,33},{17,49},{33,1},{49,17},{2,34}... | collective-permute-start | bytes 1179656 | tf_op jit(solution)/shard_map/ppermute | solution.py:37
  112.6 1.2 multiply_convert_fusion
  113.8 1.6 collective-permute-start.14
  116.0 4.0 %collective-permute-done.12 = f16[2,192,512]{2,1,0:T(8,128)(2,1)S(1)} collective-permute-done((f16[2,192,512]{2,1,0:T(8,128)(2,1)S(1)}, f16[2,192,512]{2,1,0:T(8,128)(2,1)S(1)}, u32[]{:S(2)}, u32[]{:S(2)}) %collective-permute-start.12) | collective-permute-done | bytes 393248 | tf_op jit(solution)/shard_map/ppermute | solution.py:37
  120.0 2.5 %collective-permute-start.24 = (f32[160,128]{1,0:T(8,128)S(1)}, f32[160,128]{1,0:T(8,128)S(1)}, u32[]{:S(2)}, u32[]{:S(2)}) collective-permute-start(f32[160,128]{1,0:T(8,128)S(1)} %get-tuple-element.45), channel_id=1, source_target_pairs={{0,72},{8,0},{64,8},{72,64},{1,73},{9,1},{65,9},{73,65},{2,74},{10... | collective-permute-start | bytes 245768 | tf_op jit(solution)/shard_map/ppermute | solution.py:37
  122.5 1.8 fusion.8
  124.3 11.8 %collective-permute-start.16 = (f16[2,192,512]{2,1,0:T(8,128)(2,1)}, f16[2,192,512]{2,1,0:T(8,128)(2,1)S(1)}, u32[]{:S(2)}, u32[]{:S(2)}) collective-permute-start(f16[2,192,512]{2,1,0:T(8,128)(2,1)} %get-tuple-element.40), channel_id=1, source_target_pairs={{0,2},{2,4},{4,6},{6,0},{1,3},{3,5},{5,7},{7,1},{8,10},{10,12},{12... | collective-permute-start | bytes 1179656 | tf_op jit(solution)/shard_map/ppermute | solution.py:37
  136.1 3.9 %collective-permute-start.17 = (f16[2,192,512]{2,1,0:T(8,128)(2,1)}, f16[2,192,512]{2,1,0:T(8,128)(2,1)}, u32[]{:S(2)}, u32[]{:S(2)}) collective-permute-start(f16[2,192,512]{2,1,0:T(8,128)(2,1)} %get-tuple-element.42), channel_id=1, source_target_pairs={{0,4},{2,6},{4,0},{6,2},{1,5},{3,7},{5,1},{7,3},{8,12},{10,14},{12... | collective-permute-start | bytes 1179656 | tf_op jit(solution)/shard_map/ppermute | solution.py:37
  140.0 1.1 collective-permute-start.18
  141.2 1.0 collective-permute-start.25
  142.7 7.3 %collective-permute-done.25.b = f32[160,128]{1,0:T(8,128)S(1)} collective-permute-done((f32[160,128]{1,0:T(8,128)S(1)}, f32[160,128]{1,0:T(8,128)S(1)}, u32[]{:S(2)}, u32[]{:S(2)}) %collective-permute-start.25) | collective-permute-done | bytes 81952 | tf_op jit(solution)/shard_map/ppermute | solution.py:37
  150.6 0.9 add_bitcast_fusion.refs_0_
  151.5 3.0 %collective-permute-done.27.d = f32[160,128]{1,0:T(8,128)} collective-permute-done((f32[160,128]{1,0:T(8,128)S(1)}, f32[160,128]{1,0:T(8,128)}, u32[]{:S(2)}, u32[]{:S(2)}) %collective-permute-start.27) | collective-permute-done | bytes 81952 | tf_op jit(solution)/shard_map/ppermute | solution.py:37
  154.6 1.7 ring_sum.2.a
  156.3 3.2 %collective-permute-start.30 = (f32[160,128]{1,0:T(8,128)}, f32[160,128]{1,0:T(8,128)}, u32[]{:S(2)}, u32[]{:S(2)}) collective-permute-start(f32[160,128]{1,0:T(8,128)} %ring_sum.2.a), channel_id=1, source_target_pairs={{0,48},{16,0},{32,16},{48,32},{1,49},{17,1},{33,17},{49,33},{2,50}... | collective-permute-start | bytes 245768 | tf_op jit(solution)/shard_map/ppermute | solution.py:37
  159.5 2.0 %fusion.10.refs_1_ = f32[192,512]{1,0:T(8,128)} fusion(f32[2,192,512]{2,1,0:T(8,128)} %get-tuple-element.43, f16[2,192,512]{2,1,0:T(8,128)(2,1)} %collective-permute-done.18, f16[2,192,512]{2,1,0:T(8,128)(2,1)} %collective-permute-done.17, f16[2,192,512]{2,1,0:T(8,128)(2,1)S(1)} %collective-permute-done.16), kind=kLoop, calls=%fused_computation.18 | loop fusion | flops 688128 | bytes 1376256 | tf_op jit(solution)/shard_map/add | solution.py:485
  161.5 1.5 collective-permute-done.28.b
  163.0 1.0 collective-permute-done.30.d
  164.0 1.6 ring_sum.3
  165.6 4.3 %collective-permute-start.32 = (f32[160,128]{1,0:T(8,128)}, f32[160,128]{1,0:T(8,128)S(1)}, u32[]{:S(2)}, u32[]{:S(2)}) collective-permute-start(f32[160,128]{1,0:T(8,128)} %ring_sum.3), channel_id=1, source_target_pairs={{0,64},{8,72},{64,0},{72,8},{1,65},{9,73},{65,1},{73,9},{2,66},{10... | collective-permute-start | bytes 245768 | tf_op jit(solution)/shard_map/ppermute | solution.py:37
  170.8 3.2 %collective-permute-start.19 = (f32[192,512]{1,0:T(8,128)}, f32[192,512]{1,0:T(8,128)}, u32[]{:S(2)}, u32[]{:S(2)}) collective-permute-start(f32[192,512]{1,0:T(8,128)} %fusion.10.refs_1_), channel_id=1, source_target_pairs={{0,8},{8,0},{1,9},{9,1},{2,10},{10,2},{3,11},{11,3},{4,12},{12,4},... | collective-permute-start | bytes 1179656 | tf_op jit(solution)/shard_map/ppermute | solution.py:37
  174.5 0.9 pad_maximum_fusion.mine
  175.9 2.0 %fusion.12.r_ref = f32[192,512]{1,0:T(8,128)} fusion(f32[2,192,512]{2,1,0:T(8,128)S(1)} %copy-done, f32[192,512]{1,0:T(8,128)S(1)} %copy-done.7, f32[2,192,512]{2,1,0:T(8,128)S(1)} %copy-done.2, f16[2,192,512]{2,1,0:T(8,128)(2,1)} %collective-permute-done.18, f16[2,192,512]{2,1,0:T(8,128)(2,1)} %collective-permute-done.17, ...), kind=kLoop, calls=%fused_computation.21 | loop fusion | flops 1572864 | bytes 2752512 | tf_op jit(solution)/shard_map/sub | solution.py:489
  177.9 2.5 %collective-permute-done.20.t_ref = f32[192,512]{1,0:T(8,128)} collective-permute-done((f32[192,512]{1,0:T(8,128)}, f32[192,512]{1,0:T(8,128)}, u32[]{:S(2)}, u32[]{:S(2)}) %collective-permute-start.20) | collective-permute-done | bytes 393248 | tf_op jit(solution)/shard_map/ppermute | solution.py:37
  180.4 4.5 %collective-permute-done.19.d_ref = f32[192,512]{1,0:T(8,128)} collective-permute-done((f32[192,512]{1,0:T(8,128)}, f32[192,512]{1,0:T(8,128)}, u32[]{:S(2)}, u32[]{:S(2)}) %collective-permute-start.19) | collective-permute-done | bytes 393248 | tf_op jit(solution)/shard_map/ppermute | solution.py:37
  184.9 4.3 %solve.1 = f32[192,512]{1,0:T(8,128)} custom-call(f32[192,512]{1,0:T(8,128)} %fusion.12.r_ref, f32[192,512]{1,0:T(8,128)} %collective-permute-done.19.d_ref, f32[192,512]{1,0:T(8,128)} %collective-permute-done.20.t_ref, f32[512,512]{1,0:T(8,128)} %l_ref.5, f32[4,128,128]{2,1,0:T(8,128)} %get-tuple-element.21.refs_0_.inv_ref), custom_call_target="tpu_custom_call" | custom-call | flops 1000000000 | bytes 3000000 | tf_op jit(solution)/shard_map/solve/pallas_call | solution.py:436
  189.2 8.1 %tail.1 = f32[512,512]{1,0:T(8,128)} custom-call(s32[2]{0:T(128)} %pad_add_fusion.s_ref, f32[4,160,128]{2,1,0:T(8,128)} %copy-done.14, f32[4,160,128]{2,1,0:T(8,128)} %collective-permute-done.34.other, f32[512,512]{1,0:T(8,128)} %l_ref.5, f32[4,128,128]{2,1,0:T(8,128)} %get-tuple-element.21.refs_0_.inv_ref, f32[512,512]{1,0:T(8,128)} %dg_ref.1), custom_call_target="tpu_custom_call" | custom-call | flops 8000000000 | bytes 5000000 | tf_op jit(solution)/shard_map/tail/pallas_call | solution.py:412
  (108 shorter events, 9.7 us)
Async XLA Ops:
  0.6 10.3 %collective-permute-start.1 = (bf16[192,512]{1,0:T(8,128)(2,1)}, bf16[192,512]{1,0:T(8,128)(2,1)S(1)}, u32[]{:S(2)}, u32[]{:S(2)}) collective-permute-start(bf16[192,512]{1,0:T(8,128)(2,1)} %own.1), channel_id=1, source_target_pairs={{0,64},{64,0},{1,65},{65,1},{2,66},{66,2},{3,67},{67,3},{4,68},{68... | collective-permute-start | bytes 589832 | tf_op jit(solution)/shard_map/ppermute | solution.py:37
  3.0 10.4 %collective-permute-start = (bf16[192,512]{1,0:T(8,128)(2,1)}, bf16[192,512]{1,0:T(8,128)(2,1)S(1)}, u32[]{:S(2)}, u32[]{:S(2)}) collective-permute-start(bf16[192,512]{1,0:T(8,128)(2,1)} %own.1), channel_id=1, source_target_pairs={{0,8},{8,0},{1,9},{9,1},{2,10},{10,2},{3,11},{11,3},{4,12},{12,4},... | collective-permute-start | bytes 589832 | tf_op jit(solution)/shard_map/ppermute | solution.py:37
  39.0 13.4 %collective-permute-start.2 = (bf16[2,192,512]{2,1,0:T(8,128)(2,1)}, bf16[2,192,512]{2,1,0:T(8,128)(2,1)S(1)}, u32[]{:S(2)}, u32[]{:S(2)}) collective-permute-start(bf16[2,192,512]{2,1,0:T(8,128)(2,1)} %get-tuple-element.22), channel_id=1, source_target_pairs={{0,2},{2,4},{4,6},{6,0},{1,3},{3,5},{5,7},{7,1},{8,10},{10,12},{12... | collective-permute-start | bytes 1179656 | tf_op jit(solution)/shard_map/ppermute | solution.py:37
  41.0 20.2 %collective-permute-start.3 = (bf16[2,192,512]{2,1,0:T(8,128)(2,1)}, bf16[2,192,512]{2,1,0:T(8,128)(2,1)S(1)}, u32[]{:S(2)}, u32[]{:S(2)}) collective-permute-start(bf16[2,192,512]{2,1,0:T(8,128)(2,1)} %get-tuple-element.22), channel_id=1, source_target_pairs={{0,4},{2,6},{4,0},{6,2},{1,5},{3,7},{5,1},{7,3},{8,12},{10,14},{12... | collective-permute-start | bytes 1179656 | tf_op jit(solution)/shard_map/ppermute | solution.py:37
  44.6 16.6 %collective-permute-start.4 = (bf16[2,192,512]{2,1,0:T(8,128)(2,1)}, bf16[2,192,512]{2,1,0:T(8,128)(2,1)S(1)}, u32[]{:S(2)}, u32[]{:S(2)}) collective-permute-start(bf16[2,192,512]{2,1,0:T(8,128)(2,1)} %get-tuple-element.22), channel_id=1, source_target_pairs={{0,6},{2,0},{4,2},{6,4},{1,7},{3,1},{5,3},{7,5},{8,14},{10,8},{12,... | collective-permute-start | bytes 1179656 | tf_op jit(solution)/shard_map/ppermute | solution.py:37
  45.6 15.6 %collective-permute-start.10 = (bf16[2,192,512]{2,1,0:T(8,128)(2,1)}, bf16[2,192,512]{2,1,0:T(8,128)(2,1)S(1)}, u32[]{:S(2)}, u32[]{:S(2)}) collective-permute-start(bf16[2,192,512]{2,1,0:T(8,128)(2,1)} %get-tuple-element.23), channel_id=1, source_target_pairs={{0,32},{16,48},{32,0},{48,16},{1,33},{17,49},{33,1},{49,17},{2,34}... | collective-permute-start | bytes 1179656 | tf_op jit(solution)/shard_map/ppermute | solution.py:37
  48.6 16.4 %collective-permute-start.11 = (bf16[2,192,512]{2,1,0:T(8,128)(2,1)}, bf16[2,192,512]{2,1,0:T(8,128)(2,1)S(1)}, u32[]{:S(2)}, u32[]{:S(2)}) collective-permute-start(bf16[2,192,512]{2,1,0:T(8,128)(2,1)} %get-tuple-element.23), channel_id=1, source_target_pairs={{0,48},{16,0},{32,16},{48,32},{1,49},{17,1},{33,17},{49,33},{2,50}... | collective-permute-start | bytes 1179656 | tf_op jit(solution)/shard_map/ppermute | solution.py:37
  52.5 12.5 %collective-permute-start.9 = (bf16[2,192,512]{2,1,0:T(8,128)(2,1)}, bf16[2,192,512]{2,1,0:T(8,128)(2,1)S(1)}, u32[]{:S(2)}, u32[]{:S(2)}) collective-permute-start(bf16[2,192,512]{2,1,0:T(8,128)(2,1)} %get-tuple-element.23), channel_id=1, source_target_pairs={{0,16},{16,32},{32,48},{48,0},{1,17},{17,33},{33,49},{49,1},{2,18}... | collective-permute-start | bytes 1179656 | tf_op jit(solution)/shard_map/ppermute | solution.py:37
  80.3 39.6 %collective-permute-start.15 = (f32[4,2,192,512]{3,2,1,0:T(8,128)}, f32[4,2,192,512]{3,2,1,0:T(8,128)S(1)}, u32[]{:S(2)}, u32[]{:S(2)}) collective-permute-start(f32[4,2,192,512]{3,2,1,0:T(8,128)} %get-tuple-element.29), channel_id=1, source_target_pairs={{0,1},{1,0},{2,3},{3,2},{4,5},{5,4},{6,7},{7,6},{8,9},{9,8},{10,11... | collective-permute-start | bytes 9437192 | tf_op jit(solution)/shard_map/ppermute | solution.py:37
  80.4 7.0 %collective-permute-start.5 = (bf16[2,192,512]{2,1,0:T(8,128)(2,1)}, bf16[2,192,512]{2,1,0:T(8,128)(2,1)S(1)}, u32[]{:S(2)}, u32[]{:S(2)}) collective-permute-start(bf16[2,192,512]{2,1,0:T(8,128)(2,1)} %get-tuple-element.22), channel_id=1, source_target_pairs={{0,1},{1,0},{2,3},{3,2},{4,5},{5,4},{6,7},{7,6},{8,9},{9,8},{10,11... | collective-permute-start | bytes 1179656 | tf_op jit(solution)/shard_map/ppermute | solution.py:37
  80.9 6.6 %collective-permute-start.6 = (bf16[2,192,512]{2,1,0:T(8,128)(2,1)}, bf16[2,192,512]{2,1,0:T(8,128)(2,1)}, u32[]{:S(2)}, u32[]{:S(2)}) collective-permute-start(bf16[2,192,512]{2,1,0:T(8,128)(2,1)} %copy-done.25), channel_id=1, source_target_pairs={{0,1},{1,0},{2,3},{3,2},{4,5},{5,4},{6,7},{7,6},{8,9},{9,8},{10,11... | collective-permute-start | bytes 1179656 | tf_op jit(solution)/shard_map/ppermute | solution.py:37
  81.0 7.1 %collective-permute-start.7 = (bf16[2,192,512]{2,1,0:T(8,128)(2,1)}, bf16[2,192,512]{2,1,0:T(8,128)(2,1)}, u32[]{:S(2)}, u32[]{:S(2)}) collective-permute-start(bf16[2,192,512]{2,1,0:T(8,128)(2,1)} %copy-done.26), channel_id=1, source_target_pairs={{0,1},{1,0},{2,3},{3,2},{4,5},{5,4},{6,7},{7,6},{8,9},{9,8},{10,11... | collective-permute-start | bytes 1179656 | tf_op jit(solution)/shard_map/ppermute | solution.py:37
  81.4 7.2 %collective-permute-start.8 = (bf16[2,192,512]{2,1,0:T(8,128)(2,1)}, bf16[2,192,512]{2,1,0:T(8,128)(2,1)}, u32[]{:S(2)}, u32[]{:S(2)}) collective-permute-start(bf16[2,192,512]{2,1,0:T(8,128)(2,1)} %copy-done.27), channel_id=1, source_target_pairs={{0,1},{1,0},{2,3},{3,2},{4,5},{5,4},{6,7},{7,6},{8,9},{9,8},{10,11... | collective-permute-start | bytes 1179656 | tf_op jit(solution)/shard_map/ppermute | solution.py:37
  105.5 16.9 %copy-start.3 = (f32[2,192,512]{2,1,0:T(8,128)S(1)}, f32[2,192,512]{2,1,0:T(8,128)}, u32[]{:S(2)}) copy-start(f32[2,192,512]{2,1,0:T(8,128)} %get-tuple-element.28) | copy-start | bytes 2359300
  105.6 16.9 %copy-start.4 = (f32[2,192,512]{2,1,0:T(8,128)S(1)}, f32[2,192,512]{2,1,0:T(8,128)}, u32[]{:S(2)}) copy-start(f32[2,192,512]{2,1,0:T(8,128)} %get-tuple-element.30) | copy-start | bytes 2359300
  105.6 16.9 %copy-start.5 = (f32[2,192,512]{2,1,0:T(8,128)S(1)}, f32[2,192,512]{2,1,0:T(8,128)}, u32[]{:S(2)}) copy-start(f32[2,192,512]{2,1,0:T(8,128)} %get-tuple-element.31) | copy-start | bytes 2359300
  105.6 16.9 %copy-start.6 = (f32[2,192,512]{2,1,0:T(8,128)S(1)}, f32[2,192,512]{2,1,0:T(8,128)}, u32[]{:S(2)}) copy-start(f32[2,192,512]{2,1,0:T(8,128)} %get-tuple-element.32) | copy-start | bytes 2359300
  105.6 9.8 %collective-permute-start.21 = (f32[4,160,128]{2,1,0:T(8,128)}, f32[4,160,128]{2,1,0:T(8,128)S(1)}, u32[]{:S(2)}, u32[]{:S(2)}) collective-permute-start(f32[4,160,128]{2,1,0:T(8,128)} %get-tuple-element.36), channel_id=1, source_target_pairs={{0,1},{1,0},{2,3},{3,2},{4,5},{5,4},{6,7},{7,6},{8,9},{9,8},{10,11... | collective-permute-start | bytes 983048 | tf_op jit(solution)/shard_map/ppermute | solution.py:37
  107.2 12.8 %collective-permute-start.12 = (f16[2,192,512]{2,1,0:T(8,128)(2,1)S(1)}, f16[2,192,512]{2,1,0:T(8,128)(2,1)S(1)}, u32[]{:S(2)}, u32[]{:S(2)}) collective-permute-start(f16[2,192,512]{2,1,0:T(8,128)(2,1)S(1)} %multiply_convert_fusion.2), channel_id=1, source_target_pairs={{0,16},{16,32},{32,48},{48,0},{1,17},{17,33},{33,49},{49,1},{2,18}... | collective-permute-start | bytes 1179656 | tf_op jit(solution)/shard_map/ppermute | solution.py:37
  109.8 31.3 %collective-permute-start.13 = (f16[2,192,512]{2,1,0:T(8,128)(2,1)S(1)}, f16[2,192,512]{2,1,0:T(8,128)(2,1)S(1)}, u32[]{:S(2)}, u32[]{:S(2)}) collective-permute-start(f16[2,192,512]{2,1,0:T(8,128)(2,1)S(1)} %multiply_convert_fusion.1), channel_id=1, source_target_pairs={{0,32},{16,48},{32,0},{48,16},{1,33},{17,49},{33,1},{49,17},{2,34}... | collective-permute-start | bytes 1179656 | tf_op jit(solution)/shard_map/ppermute | solution.py:37
  113.8 28.3 %collective-permute-start.14 = (f16[2,192,512]{2,1,0:T(8,128)(2,1)S(1)}, f16[2,192,512]{2,1,0:T(8,128)(2,1)S(1)}, u32[]{:S(2)}, u32[]{:S(2)}) collective-permute-start(f16[2,192,512]{2,1,0:T(8,128)(2,1)S(1)} %multiply_convert_fusion), channel_id=1, source_target_pairs={{0,48},{16,0},{32,16},{48,32},{1,49},{17,1},{33,17},{49,33},{2,50}... | collective-permute-start | bytes 1179656 | tf_op jit(solution)/shard_map/ppermute | solution.py:37
  115.5 8.9 %collective-permute-start.22 = (f32[160,128]{1,0:T(8,128)S(1)}, f32[160,128]{1,0:T(8,128)S(1)}, u32[]{:S(2)}, u32[]{:S(2)}) collective-permute-start(f32[160,128]{1,0:T(8,128)S(1)} %get-tuple-element.44), channel_id=1, source_target_pairs={{0,8},{8,64},{64,72},{72,0},{1,9},{9,65},{65,73},{73,1},{2,10},{10... | collective-permute-start | bytes 245768 | tf_op jit(solution)/shard_map/ppermute | solution.py:37
  120.0 30.6 %copy-start.8 = (f16[2,192,512]{2,1,0:T(8,128)(2,1)}, f16[2,192,512]{2,1,0:T(8,128)(2,1)S(1)}, u32[]{:S(2)}) copy-start(f16[2,192,512]{2,1,0:T(8,128)(2,1)S(1)} %collective-permute-done.12) | copy-start | bytes 1179652
  120.0 16.1 %collective-permute-start.23 = (f32[160,128]{1,0:T(8,128)S(1)}, f32[160,128]{1,0:T(8,128)S(1)}, u32[]{:S(2)}, u32[]{:S(2)}) collective-permute-start(f32[160,128]{1,0:T(8,128)S(1)} %get-tuple-element.46), channel_id=1, source_target_pairs={{0,64},{8,72},{64,0},{72,8},{1,65},{9,73},{65,1},{73,9},{2,66},{10... | collective-permute-start | bytes 245768 | tf_op jit(solution)/shard_map/ppermute | solution.py:37
  120.0 20.0 %collective-permute-start.24 = (f32[160,128]{1,0:T(8,128)S(1)}, f32[160,128]{1,0:T(8,128)S(1)}, u32[]{:S(2)}, u32[]{:S(2)}) collective-permute-start(f32[160,128]{1,0:T(8,128)S(1)} %get-tuple-element.45), channel_id=1, source_target_pairs={{0,72},{8,0},{64,8},{72,64},{1,73},{9,1},{65,9},{73,65},{2,74},{10... | collective-permute-start | bytes 245768 | tf_op jit(solution)/shard_map/ppermute | solution.py:37
  122.5 18.6 %copy-start.21 = (f32[160,128]{1,0:T(8,128)S(1)}, f32[160,128]{1,0:T(8,128)}, u32[]{:S(2)}) copy-start(f32[160,128]{1,0:T(8,128)} %get-tuple-element.35) | copy-start | bytes 245764
  122.5 28.1 %copy-start.1 = (f32[2,192,512]{2,1,0:T(8,128)S(1)}, f32[2,192,512]{2,1,0:T(8,128)}, u32[]{:S(2)}) copy-start(f32[2,192,512]{2,1,0:T(8,128)} %get-tuple-element.24) | copy-start | bytes 2359300
  124.3 51.5 %copy-start = (f32[2,192,512]{2,1,0:T(8,128)S(1)}, f32[2,192,512]{2,1,0:T(8,128)}, u32[]{:S(2)}) copy-start(f32[2,192,512]{2,1,0:T(8,128)} %get-tuple-element.43) | copy-start | bytes 2359300
  124.3 51.5 %copy-start.2 = (f32[2,192,512]{2,1,0:T(8,128)S(1)}, f32[2,192,512]{2,1,0:T(8,128)}, u32[]{:S(2)}) copy-start(f32[2,192,512]{2,1,0:T(8,128)} %get-tuple-element.24) | copy-start | bytes 2359300
  124.3 51.5 %copy-start.7 = (f32[192,512]{1,0:T(8,128)S(1)}, f32[192,512]{1,0:T(8,128)}, u32[]{:S(2)}) copy-start(f32[192,512]{1,0:T(8,128)} %pg_ref.1) | copy-start | bytes 1179652
  124.3 31.9 %collective-permute-start.16 = (f16[2,192,512]{2,1,0:T(8,128)(2,1)}, f16[2,192,512]{2,1,0:T(8,128)(2,1)S(1)}, u32[]{:S(2)}, u32[]{:S(2)}) collective-permute-start(f16[2,192,512]{2,1,0:T(8,128)(2,1)} %get-tuple-element.40), channel_id=1, source_target_pairs={{0,2},{2,4},{4,6},{6,0},{1,3},{3,5},{5,7},{7,1},{8,10},{10,12},{12... | collective-permute-start | bytes 1179656 | tf_op jit(solution)/shard_map/ppermute | solution.py:37
  136.1 23.4 %collective-permute-start.17 = (f16[2,192,512]{2,1,0:T(8,128)(2,1)}, f16[2,192,512]{2,1,0:T(8,128)(2,1)}, u32[]{:S(2)}, u32[]{:S(2)}) collective-permute-start(f16[2,192,512]{2,1,0:T(8,128)(2,1)} %get-tuple-element.42), channel_id=1, source_target_pairs={{0,4},{2,6},{4,0},{6,2},{1,5},{3,7},{5,1},{7,3},{8,12},{10,14},{12... | collective-permute-start | bytes 1179656 | tf_op jit(solution)/shard_map/ppermute | solution.py:37
  140.0 19.5 %collective-permute-start.18 = (f16[2,192,512]{2,1,0:T(8,128)(2,1)S(1)}, f16[2,192,512]{2,1,0:T(8,128)(2,1)}, u32[]{:S(2)}, u32[]{:S(2)}) collective-permute-start(f16[2,192,512]{2,1,0:T(8,128)(2,1)S(1)} %get-tuple-element.41), channel_id=1, source_target_pairs={{0,6},{2,0},{4,2},{6,4},{1,7},{3,1},{5,3},{7,5},{8,14},{10,8},{12,... | collective-permute-start | bytes 1179656 | tf_op jit(solution)/shard_map/ppermute | solution.py:37
  141.2 8.8 %collective-permute-start.25 = (f32[160,128]{1,0:T(8,128)S(1)}, f32[160,128]{1,0:T(8,128)S(1)}, u32[]{:S(2)}, u32[]{:S(2)}) collective-permute-start(f32[160,128]{1,0:T(8,128)S(1)} %fusion.19.a), channel_id=1, source_target_pairs={{0,2},{2,4},{4,6},{6,0},{1,3},{3,5},{5,7},{7,1},{8,10},{10,12},{12... | collective-permute-start | bytes 245768 | tf_op jit(solution)/shard_map/ppermute | solution.py:37
  142.2 9.3 %collective-permute-start.26 = (f32[160,128]{1,0:T(8,128)S(1)}, f32[160,128]{1,0:T(8,128)}, u32[]{:S(2)}, u32[]{:S(2)}) collective-permute-start(f32[160,128]{1,0:T(8,128)S(1)} %fusion.19.a), channel_id=1, source_target_pairs={{0,4},{2,6},{4,0},{6,2},{1,5},{3,7},{5,1},{7,3},{8,12},{10,14},{12... | collective-permute-start | bytes 245768 | tf_op jit(solution)/shard_map/ppermute | solution.py:37
  150.0 4.5 %collective-permute-start.27 = (f32[160,128]{1,0:T(8,128)S(1)}, f32[160,128]{1,0:T(8,128)}, u32[]{:S(2)}, u32[]{:S(2)}) collective-permute-start(f32[160,128]{1,0:T(8,128)S(1)} %fusion.19.a), channel_id=1, source_target_pairs={{0,6},{2,0},{4,2},{6,4},{1,7},{3,1},{5,3},{7,5},{8,14},{10,8},{12,... | collective-permute-start | bytes 245768 | tf_op jit(solution)/shard_map/ppermute | solution.py:37
  151.5 24.3 %copy-start.9 = (f16[2,192,512]{2,1,0:T(8,128)(2,1)S(1)}, f16[2,192,512]{2,1,0:T(8,128)(2,1)}, u32[]{:S(2)}) copy-start(f16[2,192,512]{2,1,0:T(8,128)(2,1)} %copy-done.8) | copy-start | bytes 1179652
  151.5 24.3 %copy-start.11 = (f16[2,192,512]{2,1,0:T(8,128)(2,1)S(1)}, f16[2,192,512]{2,1,0:T(8,128)(2,1)}, u32[]{:S(2)}) copy-start(f16[2,192,512]{2,1,0:T(8,128)(2,1)} %copy-done.10) | copy-start | bytes 1179652
  154.6 21.3 %copy-start.13 = (f16[2,192,512]{2,1,0:T(8,128)(2,1)S(1)}, f16[2,192,512]{2,1,0:T(8,128)(2,1)}, u32[]{:S(2)}) copy-start(f16[2,192,512]{2,1,0:T(8,128)(2,1)} %copy-done.12) | copy-start | bytes 1179652
  156.3 6.7 %collective-permute-start.28 = (f32[160,128]{1,0:T(8,128)}, f32[160,128]{1,0:T(8,128)S(1)}, u32[]{:S(2)}, u32[]{:S(2)}) collective-permute-start(f32[160,128]{1,0:T(8,128)} %ring_sum.2.a), channel_id=1, source_target_pairs={{0,16},{16,32},{32,48},{48,0},{1,17},{17,33},{33,49},{49,1},{2,18}... | collective-permute-start | bytes 245768 | tf_op jit(solution)/shard_map/ppermute | solution.py:37
  156.3 6.7 %collective-permute-start.29 = (f32[160,128]{1,0:T(8,128)}, f32[160,128]{1,0:T(8,128)S(1)}, u32[]{:S(2)}, u32[]{:S(2)}) collective-permute-start(f32[160,128]{1,0:T(8,128)} %ring_sum.2.a), channel_id=1, source_target_pairs={{0,32},{16,48},{32,0},{48,16},{1,33},{17,49},{33,1},{49,17},{2,34}... | collective-permute-start | bytes 245768 | tf_op jit(solution)/shard_map/ppermute | solution.py:37
  156.3 7.7 %collective-permute-start.30 = (f32[160,128]{1,0:T(8,128)}, f32[160,128]{1,0:T(8,128)}, u32[]{:S(2)}, u32[]{:S(2)}) collective-permute-start(f32[160,128]{1,0:T(8,128)} %ring_sum.2.a), channel_id=1, source_target_pairs={{0,48},{16,0},{32,16},{48,32},{1,49},{17,1},{33,17},{49,33},{2,50}... | collective-permute-start | bytes 245768 | tf_op jit(solution)/shard_map/ppermute | solution.py:37
  165.6 8.4 %collective-permute-start.31 = (f32[160,128]{1,0:T(8,128)}, f32[160,128]{1,0:T(8,128)S(1)}, u32[]{:S(2)}, u32[]{:S(2)}) collective-permute-start(f32[160,128]{1,0:T(8,128)} %ring_sum.3), channel_id=1, source_target_pairs={{0,8},{8,64},{64,72},{72,0},{1,9},{9,65},{65,73},{73,1},{2,10},{10... | collective-permute-start | bytes 245768 | tf_op jit(solution)/shard_map/ppermute | solution.py:37
  165.6 8.4 %collective-permute-start.32 = (f32[160,128]{1,0:T(8,128)}, f32[160,128]{1,0:T(8,128)S(1)}, u32[]{:S(2)}, u32[]{:S(2)}) collective-permute-start(f32[160,128]{1,0:T(8,128)} %ring_sum.3), channel_id=1, source_target_pairs={{0,64},{8,72},{64,0},{72,8},{1,65},{9,73},{65,1},{73,9},{2,66},{10... | collective-permute-start | bytes 245768 | tf_op jit(solution)/shard_map/ppermute | solution.py:37
  169.9 4.7 %collective-permute-start.33 = (f32[160,128]{1,0:T(8,128)}, f32[160,128]{1,0:T(8,128)S(1)}, u32[]{:S(2)}, u32[]{:S(2)}) collective-permute-start(f32[160,128]{1,0:T(8,128)} %ring_sum.3), channel_id=1, source_target_pairs={{0,72},{8,0},{64,8},{72,64},{1,73},{9,1},{65,9},{73,65},{2,74},{10... | collective-permute-start | bytes 245768 | tf_op jit(solution)/shard_map/ppermute | solution.py:37
  169.9 10.5 %collective-permute-start.20 = (f32[192,512]{1,0:T(8,128)}, f32[192,512]{1,0:T(8,128)}, u32[]{:S(2)}, u32[]{:S(2)}) collective-permute-start(f32[192,512]{1,0:T(8,128)} %add_bitcast_fusion.refs_0_), channel_id=1, source_target_pairs={{0,64},{64,0},{1,65},{65,1},{2,66},{66,2},{3,67},{67,3},{4,68},{68... | collective-permute-start | bytes 1179656 | tf_op jit(solution)/shard_map/ppermute | solution.py:37
  170.8 14.1 %collective-permute-start.19 = (f32[192,512]{1,0:T(8,128)}, f32[192,512]{1,0:T(8,128)}, u32[]{:S(2)}, u32[]{:S(2)}) collective-permute-start(f32[192,512]{1,0:T(8,128)} %fusion.10.refs_1_), channel_id=1, source_target_pairs={{0,8},{8,0},{1,9},{9,1},{2,10},{10,2},{3,11},{11,3},{4,12},{12,4},... | collective-permute-start | bytes 1179656 | tf_op jit(solution)/shard_map/ppermute | solution.py:37
  175.5 13.7 %collective-permute-start.34 = (f32[4,160,128]{2,1,0:T(8,128)S(1)}, f32[4,160,128]{2,1,0:T(8,128)}, u32[]{:S(2)}, u32[]{:S(2)}) collective-permute-start(f32[4,160,128]{2,1,0:T(8,128)S(1)} %pad_maximum_fusion.mine), channel_id=1, source_target_pairs={{0,1},{1,0},{2,3},{3,2},{4,5},{5,4},{6,7},{7,6},{8,9},{9,8},{10,11... | collective-permute-start | bytes 983048 | tf_op jit(solution)/shard_map/ppermute | solution.py:37
  (19 other events, 112.9 us)

commit v3 on v2

v3 whole, which is shorter than its diff:
```python
import functools

import jax
import jax.numpy as jnp
from jax import lax
from jax.experimental import pallas as pl
from jax.experimental.pallas import tpu as pltpu
from jax.sharding import Mesh, PartitionSpec as P

f32 = jnp.float32
bf16 = jnp.bfloat16
f16 = jnp.float16
U = 192
B = 512
BLK = 128
NB = B // BLK
LOWER = [(i, j) for i in range(NB) for j in range(i + 1)]
CH = len(LOWER) * BLK // 8
VMEM_LIMIT = 60 * 1024 * 1024
NEAR = (1, 3, 2)


def whole():
    return pl.BlockSpec(memory_space=pltpu.VMEM)


def params(**kw):
    return pltpu.CompilerParams(vmem_limit_bytes=VMEM_LIMIT, **kw)


def hi_dot(a, b, dims):
    return lax.dot_general(
        a, b, (dims, ((), ())), precision=lax.Precision.HIGHEST, preferred_element_type=f32
    )


def shift(x, axis, k, n=4):
    return lax.ppermute(x, axis, [(i, (i + k) % n) for i in range(n)])


def after(x, *done):
    return lax.optimization_barrier((x, *done))[0]


def iotas(n):
    return (
        lax.broadcasted_iota(jnp.int32, (n, n), 0),
        lax.broadcasted_iota(jnp.int32, (n, n), 1),
    )


def block(ref, i, j):
    return ref[i * BLK : (i + 1) * BLK, j * BLK : (j + 1) * BLK]


def prep_kernel(l_ref, pg_ref, p_ref, inv_ref, g_ref):
    rows, cols = iotas(BLK)
    blocks = []
    inv = []
    for b in range(NB):
        m = jnp.where(rows >= cols, block(l_ref, b, b), 0.0)
        blocks.append(m)
        inv.append(jnp.where(rows == cols, 1.0 / jnp.where(rows == cols, m, 1.0), 0.0))
    s = 1
    while s < BLK:
        sel = (rows // s != cols // s) & (rows // (2 * s) == cols // (2 * s))
        right = [hi_dot(jnp.where(sel, blocks[b], 0.0), inv[b], ((1,), (0,))) for b in range(NB)]
        inv = [inv[b] - hi_dot(inv[b], right[b], ((1,), (0,))) for b in range(NB)]
        s *= 2
    for b in range(NB):
        inv_ref[b] = inv[b]
    p = p_ref[...]
    g = pg_ref[...]
    total = None
    for _ in range(3):
        part = g.astype(bf16)
        g = g - part.astype(f32)
        term = lax.dot_general(part, p, (((0,), (0,)), ((), ())), preferred_element_type=f32)
        total = term if total is None else total + term
    g_ref[...] = total


def prep(lower, panel_grad, panel):
    return pl.pallas_call(
        prep_kernel,
        out_shape=(
            jax.ShapeDtypeStruct((NB, BLK, BLK), f32),
            jax.ShapeDtypeStruct((B, B), f32),
        ),
        in_specs=[whole()] * 3,
        out_specs=(whole(), whole()),
        compiler_params=params(),
        cost_estimate=pl.CostEstimate(flops=4_000_000_000, bytes_accessed=3_000_000, transcendentals=0),
        name="prep",
    )(lower, panel_grad, panel)


DIM0 = (((0,), (0,)), ((), ()))
ANY = pl.BlockSpec(memory_space=pl.ANY)


def band(ref, i):
    return ref.at[pl.ds(pl.multiple_of(i * U, U), U), :]


def pair_kernel(p, xs, zs, *refs):
    x_two, z_two = refs[-2:]
    x_two[0] = p[...]
    z_two[0] = p[...]
    x_two[1] = xs[...]
    z_two[1] = zs[...]


def pair(p, xs, zs, *after):
    return pl.pallas_call(
        pair_kernel,
        out_shape=[jax.ShapeDtypeStruct((2, U, B), bf16)] * 2,
        in_specs=[whole()] * 3 + [ANY] * len(after),
        out_specs=[whole()] * 2,
        compiler_params=params(),
        cost_estimate=pl.CostEstimate(flops=0, bytes_accessed=1_600_000, transcendentals=0),
        name="pair",
    )(p, xs, zs, *after)


def direct_kernel(f_hbm, x_two, r1, r3, r2, *refs):
    mine, other, fbuf, pc, keep, give, s_f, s_in, s_out = refs[-9:]
    x, yh = lax.axis_index("x"), lax.axis_index("yh")
    z, yl, c = lax.axis_index("z"), lax.axis_index("yl"), lax.axis_index("c")

    def f_copy(i):
        k, m = i // 2, lax.rem(i, 2)
        pair_at = lax.rem(yl + m, 2) * 4 + lax.rem(z + k, 4)
        cols = pl.ds(pl.multiple_of(pair_at * 2 * U, 2 * U), 2 * U)
        return pltpu.make_async_copy(f_hbm.at[:, cols], fbuf.at[lax.rem(i, 2)], s_f.at[lax.rem(i, 2)])

    jobs = [(yh * 4 + x, x_two.at[0]), ((1 - yh) * 4 + x, x_two.at[1])]
    for k, r in zip(NEAR, (r1, r3, r2)):
        xs = lax.rem(x + 4 - k, 4)
        jobs += [(yh * 4 + xs, r.at[0]), ((1 - yh) * 4 + xs, r.at[1])]
    ins = [pltpu.make_async_copy(src, band(pc, a), s_in.at[i]) for i, (a, src) in enumerate(jobs)]
    f_copy(0).start()
    for cp in ins:
        cp.start()
    for cp in ins:
        cp.wait()

    def out_copies(k):
        return (
            pltpu.make_async_copy(keep.at[k], mine.at[k], s_out.at[k]),
            pltpu.make_async_copy(give.at[k], other.at[k], s_out.at[4 + k]),
        )

    def step(i, _):
        @pl.when(i < 7)
        def _():
            f_copy(i + 1).start()

        f_copy(i).wait()
        d = lax.dot_general(fbuf[lax.rem(i, 2)], pc[...], DIM0, preferred_element_type=f32)
        lo, hi = d[:U], d[U:]
        k, m = i // 2, lax.rem(i, 2)
        keep[k, m] = jnp.where(c == 0, lo, hi)
        give[k, m] = jnp.where(c == 0, hi, lo)

        @pl.when(m == 1)
        def _():
            for cp in out_copies(k):
                cp.start()

        return 0

    lax.fori_loop(0, 8, step, 0)
    for k in range(4):
        for cp in out_copies(k):
            cp.wait()


def direct(flip, x_two, recv, *after):
    return pl.pallas_call(
        direct_kernel,
        in_specs=[ANY] * (5 + len(after)),
        out_specs=[ANY] * 2,
        scratch_shapes=[
            pltpu.VMEM((2, 8 * U, 2 * U), bf16),
            pltpu.VMEM((8 * U, B), bf16),
            pltpu.VMEM((4, 2, U, B), f32),
            pltpu.VMEM((4, 2, U, B), f32),
            pltpu.SemaphoreType.DMA((2,)),
            pltpu.SemaphoreType.DMA((8,)),
            pltpu.SemaphoreType.DMA((8,)),
        ],
        out_shape=[jax.ShapeDtypeStruct((4, 2, U, B), f32)] * 2,
        compiler_params=params(),
        cost_estimate=pl.CostEstimate(flops=14_000_000_000, bytes_accessed=17_000_000, transcendentals=0),
        name="direct",
    )(flip, x_two, *recv, *after)


def transposed_kernel(f_hbm, z_all, p_all, x_two, r1, r3, r2, g_hbm, *refs):
    out, mine, other, fbuf, pr, pc, acc, g, tbuf, flat, s_f, s_in, s_out = refs[-13:]
    x, yh = lax.axis_index("x"), lax.axis_index("yh")
    z, yl, c = lax.axis_index("z"), lax.axis_index("yl"), lax.axis_index("c")
    y = yh * 2 + yl

    def f_copies(k):
        slot = lax.rem(k, 2)
        made = []
        for m in (0, 1):
            a = lax.rem(yh + m, 2) * 4 + lax.rem(x + k, 4)
            made.append(pltpu.make_async_copy(band(f_hbm, a), fbuf.at[slot, pl.ds(m * U, U)], s_f.at[slot, m]))
        return made

    first = []
    for k in range(4):
        zs = lax.rem(z + 4 - k, 4)
        for m, yb in ((0, yl), (1, 1 - yl)):
            first.append(((yb * 4 + zs) * 2 + c, z_all.at[k, m]))
            first.append(((yb * 4 + zs) * 2 + 1 - c, p_all.at[k, m]))
    ins = [pltpu.make_async_copy(src, band(pr, a), s_in.at[i]) for i, (a, src) in enumerate(first)]
    local_rows = {0: x_two}
    for k, r in zip(NEAR, (r1, r3, r2)):
        local_rows[4 - k] = r
    late = [
        pltpu.make_async_copy(r.at[m], band(pc, 2 * k + m), s_in.at[16 + 2 * k + m])
        for k, r in local_rows.items()
        for m in (0, 1)
    ]
    late.append(pltpu.make_async_copy(g_hbm, g, s_in.at[24]))
    for cp in f_copies(0) + ins:
        cp.start()
    acc[...] = jnp.zeros_like(acc)
    for cp in ins:
        cp.wait()
    for cp in late:
        cp.start()

    def out_copy(k):
        return pltpu.make_async_copy(tbuf.at[k], out.at[k], s_out.at[k])

    def step(k, _):
        @pl.when(k < 3)
        def _():
            for cp in f_copies(k + 1):
                cp.start()

        for cp in f_copies(k):
            cp.wait()
        t = jnp.dot(fbuf[lax.rem(k, 2)], pr[...], preferred_element_type=f32)
        tbuf[k, 0] = t[:U]
        tbuf[k, 1] = t[U:]
        out_copy(k).start()

        @pl.when(k == 0)
        def _():
            for cp in late:
                cp.wait()

        hi = t.astype(bf16)
        lo = (t - hi.astype(f32)).astype(bf16)
        p = pc[pl.ds(pl.multiple_of(k * 2 * U, 2 * U), 2 * U), :]
        acc[...] += lax.dot_general(p, hi, DIM0, preferred_element_type=f32) + lax.dot_general(
            p, lo, DIM0, preferred_element_type=f32
        )
        return 0

    lax.fori_loop(0, 4, step, 0)
    for n, (i, j) in enumerate(LOWER):
        flat[n * BLK : (n + 1) * BLK, :] = block(g, i, j) - block(acc, i, j) - block(acc, j, i).T
    for k in range(4):
        q = lax.rem(y + k, 4)
        mine[k] = flat[pl.ds(pl.multiple_of((c * 4 + q) * CH, CH), CH), :]
        other[k] = flat[pl.ds(pl.multiple_of(((1 - c) * 4 + q) * CH, CH), CH), :]
    for k in range(4):
        out_copy(k).wait()


def transposed(flip, z_all, p_all, x_two, xr, g, *after):
    return pl.pallas_call(
        transposed_kernel,
        in_specs=[ANY] * (8 + len(after)),
        out_specs=[ANY, whole(), whole()],
        scratch_shapes=[
            pltpu.VMEM((2, 2 * U, 16 * U), bf16),
            pltpu.VMEM((16 * U, B), bf16),
            pltpu.VMEM((8 * U, B), bf16),
            pltpu.VMEM((B, B), f32),
            pltpu.VMEM((B, B), f32),
            pltpu.VMEM((4, 2, U, B), f32),
            pltpu.VMEM((8 * CH, BLK), f32),
            pltpu.SemaphoreType.DMA((2, 2)),
            pltpu.SemaphoreType.DMA((25,)),
            pltpu.SemaphoreType.DMA((4,)),
        ],
        out_shape=[
            jax.ShapeDtypeStruct((4, 2, U, B), f32),
            jax.ShapeDtypeStruct((4, CH, BLK), f32),
            jax.ShapeDtypeStruct((4, CH, BLK), f32),
        ],
        compiler_params=params(),
        cost_estimate=pl.CostEstimate(flops=15_000_000_000, bytes_accessed=17_000_000, transcendentals=0),
        name="transposed",
    )(flip, z_all, p_all, x_two, *xr, g, *after)


def split(a):
    hi = a.astype(bf16)
    return hi, (a - hi.astype(f32)).astype(bf16)


def cat(parts, axis):
    return parts[0] if len(parts) == 1 else jnp.concatenate(parts, axis=axis)


def cat2(pairs, axis):
    return cat([p[0] for p in pairs], axis), cat([p[1] for p in pairs], axis)


def dot3(a, b):
    return jnp.dot(cat([a[0], a[0], a[1]], 1), cat([b[0], b[1], b[0]], 0), preferred_element_type=f32)


def tail_kernel(mine, other, l_ref, inv_ref, dg_ref, *refs):
    out_ref, flat = refs[-2:]
    c, y = lax.axis_index("c"), lax.axis_index("yh") * 2 + lax.axis_index("yl")
    for k in range(4):
        q = lax.rem(y + 4 - k, 4)
        flat[pl.ds(pl.multiple_of((c * 4 + q) * CH, CH), CH), :] = mine[k]
        flat[pl.ds(pl.multiple_of(((1 - c) * 4 + q) * CH, CH), CH), :] = other[k]
    rows, cols = iotas(BLK)
    tri = rows >= cols
    low = {ij: block(l_ref, *ij) for ij in LOWER}
    for i in range(NB):
        low[i, i] = jnp.where(tri, low[i, i], 0.0)
    low_t = {ij: split(v.T) for ij, v in low.items()}
    low_n = {ij: split(v) for ij, v in low.items()}
    inv_n = [split(inv_ref[i]) for i in range(NB)]
    inv_t = [split(inv_ref[i].T) for i in range(NB)]
    q = {ij: flat[n * BLK : (n + 1) * BLK, :] for n, ij in enumerate(LOWER)}
    acc = {i: cat([q[i, j] for j in range(i + 1)], 1) for i in range(NB)}
    new = {}
    for i in reversed(range(NB)):
        con = dot3(inv_t[i], split(acc[i]))
        if i:
            part = tuple(v[:, : i * BLK] for v in split(con))
            upd = dot3(cat2([low_t[i, r] for r in range(i)], 0), part)
            for r in range(i):
                acc[r] = acc[r] - upd[r * BLK : (r + 1) * BLK, : (r + 1) * BLK]
        n = dg_ref[i * BLK : (i + 1) * BLK, : (i + 1) * BLK] - con
        corner = jnp.where(tri, n[:, i * BLK :], 0.0)
        new[i] = split(corner if i == 0 else cat([n[:, : i * BLK], corner], 1))
    keep = jnp.where(rows > cols, 1.0, jnp.where(rows == cols, 0.5, 0.0))
    inner = {}
    for i in range(NB):
        width = (i + 1) * BLK
        r = dot3(
            cat2([low_t[k, i] for k in range(i, NB)], 1),
            cat2([tuple(v[:, :width] for v in new[k]) for k in range(i, NB)], 0),
        )
        parts = [] if i == 0 else [r[:, : i * BLK]]
        parts.append(r[:, i * BLK :] * keep)
        if width < B:
            parts.append(jnp.zeros((BLK, B - width), f32))
        inner[i] = cat(parts, 1)
    left = {}
    for i in reversed(range(NB)):
        left[i] = dot3(inv_t[i], split(inner[i]))
        if i:
            upd = dot3(cat2([low_t[i, r] for r in range(i)], 0), split(left[i]))
            for r in range(i):
                inner[r] = inner[r] - upd[r * BLK : (r + 1) * BLK]
    acc = cat([left[i] for i in range(NB)], 0)
    right = {}
    for j in reversed(range(NB)):
        right[j] = dot3(split(acc[:, j * BLK : (j + 1) * BLK]), inv_n[j])
        if j:
            upd = dot3(split(right[j]), cat2([low_n[j, r] for r in range(j)], 1))
            acc = acc[:, : j * BLK] - upd
    for i in range(NB):
        for j in range(i + 1):
            v = 0.5 * (right[j][i * BLK : (i + 1) * BLK] + right[i][j * BLK : (j + 1) * BLK].T)
            out_ref[i * BLK : (i + 1) * BLK, j * BLK : (j + 1) * BLK] = v
            if i != j:
                out_ref[j * BLK : (j + 1) * BLK, i * BLK : (i + 1) * BLK] = v.T


def tail(mine, other, lower, inv, diag_grad, *after):
    return pl.pallas_call(
        tail_kernel,
        out_shape=jax.ShapeDtypeStruct((B, B), f32),
        in_specs=[whole()] * 5 + [ANY] * len(after),
        out_specs=whole(),
        scratch_shapes=[pltpu.VMEM((8 * CH, BLK), f32)],
        compiler_params=params(),
        cost_estimate=pl.CostEstimate(flops=8_000_000_000, bytes_accessed=5_000_000, transcendentals=0),
        name="tail",
    )(mine, other, lower, inv, diag_grad, *after)


def solve_kernel(r_ref, d_ref, t_ref, l_ref, inv_ref, out_ref):
    acc = r_ref[...] - d_ref[...] - t_ref[...]
    for j in reversed(range(NB)):
        x = dot3(split(acc[:, j * BLK :]), split(inv_ref[j]))
        out_ref[:, j * BLK : (j + 1) * BLK] = x
        if j:
            acc = acc[:, : j * BLK] - dot3(split(x), split(l_ref[j * BLK : (j + 1) * BLK, : j * BLK]))


def solve(r, d, t, lower, inv):
    return pl.pallas_call(
        solve_kernel,
        out_shape=jax.ShapeDtypeStruct((U, B), f32),
        in_specs=[whole()] * 5,
        out_specs=whole(),
        compiler_params=params(),
        cost_estimate=pl.CostEstimate(flops=1_000_000_000, bytes_accessed=3_000_000, transcendentals=0),
        name="solve",
    )(r, d, t, lower, inv)


def on_device(trailing_grad, panel, panel_grad, diag_factor, diag_grad):
    flip = trailing_grad.reshape(-1, trailing_grad.shape[3])

    x_swp = shift(panel, "yh", 1, 2)
    z_swp = shift(panel, "yl", 1, 2)
    inv, g = prep(diag_factor, panel_grad, panel)
    x_two, z_two = pair(panel, x_swp, z_swp, inv)
    z_recv = [shift(z_two, "z", k) for k in NEAR]
    x_recv = [shift(x_two, "x", k) for k in NEAR]
    z_recv, x_recv = lax.optimization_barrier((z_recv, x_recv))
    z_all = jnp.stack([z_two, z_recv[0], z_recv[2], z_recv[1]])
    p_all = shift(z_all, "c", 1, 2)

    half = lambda v: (v * 64.0).astype(f16)
    full = lambda v: v.astype(f32) * (1 / 64.0)

    t_all, q_mine, q_other = transposed(flip, z_all, p_all, x_two, x_recv, g)
    t_in = {k: shift(half(t_all[k]), "x", k) for k in NEAR}
    q_pair = shift(q_other, "c", 1, 2)
    q = [q_mine[k] + q_pair[k] for k in range(4)]
    q_in = [shift(q[k], ("yh", "yl"), k) for k in NEAR]
    part = q[0] + q_in[0] + q_in[1] + q_in[2]
    t_far = t_all[0][1] + (full(t_in[2][1]) + full(t_in[3][1]) + full(t_in[1][1]))
    t_last = shift(t_far, "yh", 1, 2)
    x_two = after(x_two, part, t_in[1], t_in[3])
    d_mine, d_other = direct(flip, x_two, x_recv)
    d_pair = shift(d_other, "c", 1, 2)
    got = {k: shift(part, "z", k) for k in NEAR}
    part = (part + got[2]) + (got[1] + got[3])
    d_pair = after(d_pair, part)
    d_own = d_mine[0] + d_pair[0]
    d_out = {k: half(d_mine[k] + d_pair[k]) for k in NEAR}
    d_in = {k: shift(d_out[k], "z", k) for k in NEAR}
    part = after(part, *d_out.values())
    got = {k: shift(part, "x", k) for k in NEAR}
    part = after(part, d_in[1], d_in[3])
    part = (part + got[2]) + (got[1] + got[3])
    q_all = jnp.stack([part] + [shift(part, ("yh", "yl"), k) for k in (1, 2, 3)])
    q_all = after(q_all, t_last)
    d_far = d_own[1] + (full(d_in[2][1]) + full(d_in[3][1]) + full(d_in[1][1]))
    d_last = shift(d_far, "yl", 1, 2)
    near = (
        panel_grad
        - (t_all[0][0] + (full(t_in[2][0]) + full(t_in[3][0]) + full(t_in[1][0])))
        - (d_own[0] + (full(d_in[2][0]) + full(d_in[3][0]) + full(d_in[1][0])))
    )
    q_pair = after(shift(q_all, "c", 1, 2), d_far)
    diag_adj = tail(q_all, q_pair, diag_factor, inv, diag_grad)
    near = after(near, diag_adj)
    return solve(near, d_last, t_last, diag_factor, inv), diag_adj


def solution(mesh):
    fine = Mesh(mesh.devices.reshape(2, 4, 2, 4, 2), ("yh", "x", "yl", "z", "c"))
    row, col = ("yh", "x"), ("yl", "z", "c")
    return jax.shard_map(
        on_device,
        mesh=fine,
        in_specs=(P(None, col, None, row), P(row + col, None), P(row + col, None), P(), P()),
        out_specs=(P(row + col, None), P()),
        check_vma=False,
    )
```

time: 198 us -> 158 us (0.80)
  Pallas kernels: 78.6 us -> 46.3 us
  starting transfers between devices: 57 us -> 46.4 us
  waiting for transfers between devices: 45.8 us -> 49.5 us
  other arithmetic: 12 us -> 8.34 us
    pallas_call x1, Pallas kernels: 25 us -> 2.04 us  [pair(): pl.pallas_call(pair_kernel, out_shape=[jax.ShapeDtypeStruct((2, U, B), bf...]
    ppermute x35 -> x32, starting transfers between devices: 57 us -> 46.4 us  [shift(): return lax.ppermute(x, axis, [(i, (i + k) % n) for i in range(n)])]
    pallas_call x5 -> x2, Pallas kernels: 34.7 us -> 26 us  [the longest x1 13.1 us: transposed(): pl.pallas_call(transposed_kernel, in_specs=[ANY] * (8 + len(after)), out_...]
    ppermute x35 -> x32, waiting for transfers between devices: 45.8 us -> 49.5 us  [shift(): return lax.ppermute(x, axis, [(i, (i + k) % n) for i in range(n)])]
    unnamed x64 -> x26, local copies, waits for them, and re-layouts: 1.61 us -> 4.18 us
    sub x1 -> x0, other arithmetic: 2.02 us -> none  [on_device(): panel_grad - (t_own[0][0] + (full(t_in[1][0]) + full(t_in[2][0]) + full(t...]
    convert_element_type x4 -> x2, other arithmetic: 5.58 us -> 4.64 us  [on_device(): half = lambda v: (v * 64.0).astype(f16)]
  transfers between devices with their start and end apart: 35 -> 32, of which waited for: 16 -> 15; matrix products, arithmetic and copies ran while one was open for 7% -> 5% of each run, Pallas kernels for 15% -> 9%
where the time goes in v3:
time: 158 us; the launch traced here: 156 us
  waiting for transfers between devices  49.5 us (31%)
  starting transfers between devices  46.4 us (29%)
  Pallas kernels  46.3 us (29%)
  other arithmetic  8.34 us (5%)
  local copies, waits for them, and re-layouts  4.18 us (3%)
    ppermute x32, waiting for transfers between devices, shift(): return lax.ppermute(x, axis, [(i, (i + k) % n) for i in range(n)])  49.5 us
    ppermute x32, starting transfers between devices, shift(): return lax.ppermute(x, axis, [(i, (i + k) % n) for i in range(n)])  46.4 us
    pallas_call x1, Pallas kernels, transposed(): pl.pallas_call(transposed_kernel, in_specs=[ANY] * (8 + len(after)), out_...  13.1 us
    pallas_call x1, Pallas kernels, direct(): pl.pallas_call(direct_kernel, in_specs=[ANY] * (5 + len(after)), out_spec...  12.9 us
    pallas_call x1, Pallas kernels, tail(): pl.pallas_call(tail_kernel, out_shape=jax.ShapeDtypeStruct((B, B), f32),...  8.13 us
    pallas_call x1, Pallas kernels, prep(): pl.pallas_call(prep_kernel, out_shape=(jax.ShapeDtypeStruct((NB, BLK, BLK...  6.59 us
    convert_element_type x2, other arithmetic, on_device(): half = lambda v: (v * 64.0).astype(f16)  4.64 us
    unnamed x26, local copies, waits for them, and re-layouts  4.18 us
  transfers between devices with their start and end apart: 32, of which 15 were waited for; matrix products, arithmetic and copies ran while one was open for 5% of the time, Pallas kernels for 9%

profile of v3, /device:TPU:8, one launch (start us, length us, event | category | flops | bytes accessed | tf_op | source)
XLA Modules:
  0.0 155.6 jit_solution(7629945206955861112)
XLA Ops:
  1.1 2.7 %collective-permute-start = (bf16[192,512]{1,0:T(8,128)(2,1)}, bf16[192,512]{1,0:T(8,128)(2,1)S(1)}, u32[]{:S(2)}, u32[]{:S(2)}) collective-permute-start(bf16[192,512]{1,0:T(8,128)(2,1)} %p.1), channel_id=1, source_target_pairs={{0,64},{64,0},{1,65},{65,1},{2,66},{66,2},{3,67},{67,3},{4,68},{68... | collective-permute-start | bytes 589832 | tf_op jit(solution)/shard_map/ppermute | solution.py:38
  3.7 6.6 %prep.1 = (f32[4,128,128]{2,1,0:T(8,128)}, f32[512,512]{1,0:T(8,128)}) custom-call(f32[512,512]{1,0:T(8,128)} %l_ref.5, f32[192,512]{1,0:T(8,128)} %pg_ref.1, bf16[192,512]{1,0:T(8,128)(2,1)} %p.1), custom_call_target="tpu_custom_call" | custom-call | flops 4000000000 | bytes 3000000 | tf_op jit(solution)/shard_map/prep/pallas_call | solution.py:84
  10.3 2.4 %collective-permute-done.xs = bf16[192,512]{1,0:T(8,128)(2,1)S(1)} collective-permute-done((bf16[192,512]{1,0:T(8,128)(2,1)}, bf16[192,512]{1,0:T(8,128)(2,1)S(1)}, u32[]{:S(2)}, u32[]{:S(2)}) %collective-permute-start) | collective-permute-done | bytes 196640 | tf_op jit(solution)/shard_map/ppermute | solution.py:38
  13.5 2.0 %pair.1 = (bf16[2,192,512]{2,1,0:T(8,128)(2,1)}, bf16[2,192,512]{2,1,0:T(8,128)(2,1)}) custom-call(bf16[192,512]{1,0:T(8,128)(2,1)} %p.1, bf16[192,512]{1,0:T(8,128)(2,1)} %copy-done.5, bf16[192,512]{1,0:T(8,128)(2,1)} %copy-done.4, f32[4,128,128]{2,1,0:T(8,128)} %get-tuple-element.24.refs_0_.inv_ref), custom_call_target="tpu_custom_call" | custom-call | bytes 1600000 | tf_op jit(solution)/shard_map/pair/pallas_call | solution.py:115
  15.5 3.9 %collective-permute-start.4 = (bf16[2,192,512]{2,1,0:T(8,128)(2,1)}, bf16[2,192,512]{2,1,0:T(8,128)(2,1)S(1)}, u32[]{:S(2)}, u32[]{:S(2)}) collective-permute-start(bf16[2,192,512]{2,1,0:T(8,128)(2,1)} %get-tuple-element.25), channel_id=1, source_target_pairs={{0,4},{2,6},{4,0},{6,2},{1,5},{3,7},{5,1},{7,3},{8,12},{10,14},{12... | collective-permute-start | bytes 1179656 | tf_op jit(solution)/shard_map/ppermute | solution.py:38
  20.1 1.3 collective-permute-start.2
  21.4 3.0 %collective-permute-start.7 = (bf16[2,192,512]{2,1,0:T(8,128)(2,1)}, bf16[2,192,512]{2,1,0:T(8,128)(2,1)S(1)}, u32[]{:S(2)}, u32[]{:S(2)}) collective-permute-start(bf16[2,192,512]{2,1,0:T(8,128)(2,1)} %get-tuple-element.37.x_two), channel_id=1, source_target_pairs={{0,32},{16,48},{32,0},{48,16},{1,33},{17,49},{33,1},{49,17},{2,34}... | collective-permute-start | bytes 1179656 | tf_op jit(solution)/shard_map/ppermute | solution.py:38
  24.4 1.1 collective-permute-start.6
  25.6 4.1 %collective-permute-done.4 = bf16[2,192,512]{2,1,0:T(8,128)(2,1)S(1)} collective-permute-done((bf16[2,192,512]{2,1,0:T(8,128)(2,1)}, bf16[2,192,512]{2,1,0:T(8,128)(2,1)S(1)}, u32[]{:S(2)}, u32[]{:S(2)}) %collective-permute-start.4) | collective-permute-done | bytes 393248 | tf_op jit(solution)/shard_map/ppermute | solution.py:38
  29.7 1.5 collective-permute-start.5
  31.2 5.9 %collective-permute-done.3 = bf16[2,192,512]{2,1,0:T(8,128)(2,1)S(1)} collective-permute-done((bf16[2,192,512]{2,1,0:T(8,128)(2,1)}, bf16[2,192,512]{2,1,0:T(8,128)(2,1)S(1)}, u32[]{:S(2)}, u32[]{:S(2)}) %collective-permute-start.3) | collective-permute-done | bytes 393248 | tf_op jit(solution)/shard_map/ppermute | solution.py:38
  37.1 3.8 %collective-permute-done.6.r3 = bf16[2,192,512]{2,1,0:T(8,128)(2,1)S(1)} collective-permute-done((bf16[2,192,512]{2,1,0:T(8,128)(2,1)}, bf16[2,192,512]{2,1,0:T(8,128)(2,1)S(1)}, u32[]{:S(2)}, u32[]{:S(2)}) %collective-permute-start.6) | collective-permute-done | bytes 393248 | tf_op jit(solution)/shard_map/ppermute | solution.py:38
  40.8 0.8 copy-done.9
  41.6 1.2 pad_maximum_fusion.z_all
  42.9 3.4 %collective-permute-done.8.p_all = bf16[4,2,192,512]{3,2,1,0:T(8,128)(2,1)S(1)} collective-permute-done((bf16[4,2,192,512]{3,2,1,0:T(8,128)(2,1)S(1)}, bf16[4,2,192,512]{3,2,1,0:T(8,128)(2,1)S(1)}, u32[]{:S(2)}, u32[]{:S(2)}) %collective-permute-start.8) | collective-permute-done | bytes 1572896 | tf_op jit(solution)/shard_map/ppermute | solution.py:38
  46.3 1.2 copy-done.6
  47.5 13.1 %transposed.1 = (f32[4,2,192,512]{3,2,1,0:T(8,128)}, f32[4,160,128]{2,1,0:T(8,128)}, f32[4,160,128]{2,1,0:T(8,128)}) custom-call(bf16[1536,3072]{1,0:T(8,128)(2,1)} %bitcast.69, bf16[4,2,192,512]{3,2,1,0:T(8,128)(2,1)} %copy-done, bf16[4,2,192,512]{3,2,1,0:T(8,128)(2,1)} %copy-done.6, bf16[2,192,512]{2,1,0:T(8,128)(2,1)} %get-tuple-element.37.x_two, ...), custom_call_target="tpu_custom_call" | custom-call | flops 15000000512 | bytes 17000000 | tf_op jit(solution)/shard_map/transposed/pallas_call | solution.py:279
  60.8 1.9 %fusion = (f16[2,192,512]{2,1,0:T(8,128)(2,1)S(1)}, f16[2,192,512]{2,1,0:T(8,128)(2,1)S(1)}, f16[2,192,512]{2,1,0:T(8,128)(2,1)S(1)}) fusion(f32[4,2,192,512]{3,2,1,0:T(8,128)} %get-tuple-element.34), kind=kLoop, calls=%fused_computation.8 | loop fusion | flops 1179648 | bytes 3538944 | tf_op jit(solution)/shard_map/convert_element_type | solution.py:434
  62.7 1.5 collective-permute-start.11
  64.2 1.8 %collective-permute-start.10 = (f16[2,192,512]{2,1,0:T(8,128)(2,1)S(1)}, f16[2,192,512]{2,1,0:T(8,128)(2,1)S(1)}, u32[]{:S(2)}, u32[]{:S(2)}) collective-permute-start(f16[2,192,512]{2,1,0:T(8,128)(2,1)S(1)} %get-tuple-element.54), channel_id=1, source_target_pairs={{0,48},{16,0},{32,16},{48,32},{1,49},{17,1},{33,17},{49,33},{2,50}... | collective-permute-start | bytes 1179656 | tf_op jit(solution)/shard_map/ppermute | solution.py:38
  66.6 3.5 %collective-permute-start.15 = (f32[160,128]{1,0:T(8,128)S(1)}, f32[160,128]{1,0:T(8,128)S(1)}, u32[]{:S(2)}, u32[]{:S(2)}) collective-permute-start(f32[160,128]{1,0:T(8,128)S(1)} %get-tuple-element.57), channel_id=1, source_target_pairs={{0,64},{8,72},{64,0},{72,8},{1,65},{9,73},{65,1},{73,9},{2,66},{10... | collective-permute-start | bytes 245768 | tf_op jit(solution)/shard_map/ppermute | solution.py:38
  70.1 1.3 collective-permute-done.13
  71.4 1.8 %collective-permute-done.15 = f32[160,128]{1,0:T(8,128)S(1)} collective-permute-done((f32[160,128]{1,0:T(8,128)S(1)}, f32[160,128]{1,0:T(8,128)S(1)}, u32[]{:S(2)}, u32[]{:S(2)}) %collective-permute-start.15) | collective-permute-done | bytes 81952 | tf_op jit(solution)/shard_map/ppermute | solution.py:38
  73.2 1.3 collective-permute-done.14
  74.6 0.8 collective-permute-done.11
  75.4 12.9 %direct.1 = (f32[4,2,192,512]{3,2,1,0:T(8,128)}, f32[4,2,192,512]{3,2,1,0:T(8,128)}) custom-call(bf16[1536,3072]{1,0:T(8,128)(2,1)} %bitcast.70, bf16[2,192,512]{2,1,0:T(8,128)(2,1)} %get-tuple-element.37.x_two, bf16[2,192,512]{2,1,0:T(8,128)(2,1)} %copy-done.9, bf16[2,192,512]{2,1,0:T(8,128)(2,1)} %copy-done.8, bf16[2,192,512]{2,1,0:T(8,128)(2,1)} %copy-done.7), custom_call_target="tpu_custom_call" | custom-call | flops 14000000000 | bytes 17000000 | tf_op jit(solution)/shard_map/direct/pallas_call | solution.py:180
  88.5 2.0 %collective-permute-start.19 = (f32[160,128]{1,0:T(8,128)S(1)}, f32[160,128]{1,0:T(8,128)S(1)}, u32[]{:S(2)}, u32[]{:S(2)}) collective-permute-start(f32[160,128]{1,0:T(8,128)S(1)} %fusion.16), channel_id=1, source_target_pairs={{0,6},{2,0},{4,2},{6,4},{1,7},{3,1},{5,3},{7,5},{8,14},{10,8},{12,... | collective-permute-start | bytes 245768 | tf_op jit(solution)/shard_map/ppermute | solution.py:38
  90.6 1.5 collective-permute-start.17
  92.1 2.5 %collective-permute-start.9 = (f16[2,192,512]{2,1,0:T(8,128)(2,1)S(1)}, f16[2,192,512]{2,1,0:T(8,128)(2,1)S(1)}, u32[]{:S(2)}, u32[]{:S(2)}) collective-permute-start(f16[2,192,512]{2,1,0:T(8,128)(2,1)S(1)} %get-tuple-element.52), channel_id=1, source_target_pairs={{0,32},{16,48},{32,0},{48,16},{1,33},{17,49},{33,1},{49,17},{2,34}... | collective-permute-start | bytes 1179656 | tf_op jit(solution)/shard_map/ppermute | solution.py:38
  94.6 3.3 %collective-permute-done.18 = f32[160,128]{1,0:T(8,128)S(1)} collective-permute-done((f32[160,128]{1,0:T(8,128)S(1)}, f32[160,128]{1,0:T(8,128)S(1)}, u32[]{:S(2)}, u32[]{:S(2)}) %collective-permute-start.18) | collective-permute-done | bytes 81952 | tf_op jit(solution)/shard_map/ppermute | solution.py:38
  98.0 2.7 %fusion.3 = (f16[2,192,512]{2,1,0:T(8,128)(2,1)S(1)}, f16[2,192,512]{2,1,0:T(8,128)(2,1)S(1)}, f16[2,192,512]{2,1,0:T(8,128)(2,1)S(1)}, f32[1,2,192,512]{3,2,1,0:T(8,128)S(1)}) fusion(f32[4,2,192,512]{3,2,1,0:T(8,128)S(1)} %collective-permute-done.16, f32[4,2,192,512]{3,2,1,0:T(8,128)} %get-tuple-element.38), kind=kLoop, calls=%fused_computation.11 | loop fusion | flops 1966080 | bytes 8257536 | tf_op jit(solution)/shard_map/convert_element_type | solution.py:434
  101.4 2.0 %collective-permute-start.22 = (f16[2,192,512]{2,1,0:T(8,128)(2,1)S(1)}, f16[2,192,512]{2,1,0:T(8,128)(2,1)S(1)}, u32[]{:S(2)}, u32[]{:S(2)}) collective-permute-start(f16[2,192,512]{2,1,0:T(8,128)(2,1)S(1)} %get-tuple-element.47), channel_id=1, source_target_pairs={{0,2},{2,4},{4,6},{6,0},{1,3},{3,5},{5,7},{7,1},{8,10},{10,12},{12... | collective-permute-start | bytes 1179656 | tf_op jit(solution)/shard_map/ppermute | solution.py:38
  103.4 1.3 collective-permute-start.21
  104.6 3.0 %collective-permute-start.25 = (f32[160,128]{1,0:T(8,128)S(1)}, f32[160,128]{1,0:T(8,128)S(1)}, u32[]{:S(2)}, u32[]{:S(2)}) collective-permute-start(f32[160,128]{1,0:T(8,128)S(1)} %add_add_fusion.1), channel_id=1, source_target_pairs={{0,48},{16,0},{32,16},{48,32},{1,49},{17,1},{33,17},{49,33},{2,50}... | collective-permute-start | bytes 245768 | tf_op jit(solution)/shard_map/ppermute | solution.py:38
  107.6 6.8 %collective-permute-done.20 = f16[2,192,512]{2,1,0:T(8,128)(2,1)S(1)} collective-permute-done((f16[2,192,512]{2,1,0:T(8,128)(2,1)S(1)}, f16[2,192,512]{2,1,0:T(8,128)(2,1)S(1)}, u32[]{:S(2)}, u32[]{:S(2)}) %collective-permute-start.20) | collective-permute-done | bytes 393248 | tf_op jit(solution)/shard_map/ppermute | solution.py:38
  114.3 2.6 %collective-permute-start.23 = (f32[160,128]{1,0:T(8,128)S(1)}, f32[160,128]{1,0:T(8,128)S(1)}, u32[]{:S(2)}, u32[]{:S(2)}) collective-permute-start(f32[160,128]{1,0:T(8,128)S(1)} %add_add_fusion.1), channel_id=1, source_target_pairs={{0,32},{16,48},{32,0},{48,16},{1,33},{17,49},{33,1},{49,17},{2,34}... | collective-permute-start | bytes 245768 | tf_op jit(solution)/shard_map/ppermute | solution.py:38
  116.9 4.4 %collective-permute-done.22 = f16[2,192,512]{2,1,0:T(8,128)(2,1)S(1)} collective-permute-done((f16[2,192,512]{2,1,0:T(8,128)(2,1)S(1)}, f16[2,192,512]{2,1,0:T(8,128)(2,1)S(1)}, u32[]{:S(2)}, u32[]{:S(2)}) %collective-permute-start.22) | collective-permute-done | bytes 393248 | tf_op jit(solution)/shard_map/ppermute | solution.py:38
  121.3 2.4 %bitcast_add_fusion = (f32[192,512]{1,0:T(8,128)S(1)}, f32[192,512]{1,0:T(8,128)}, f32[192,512]{1,0:T(8,128)S(1)}) fusion(f32[4,2,192,512]{3,2,1,0:T(8,128)} %get-tuple-element.34, f16[2,192,512]{2,1,0:T(8,128)(2,1)S(1)} %collective-permute-done.11, f16[2,192,512]{2,1,0:T(8,128)(2,1)S(1)} %collective-permute-done.10, ...), kind=kLoop, calls=%fused_computation.19 | loop fusion | flops 2949120 | bytes 5505024 | tf_op jit(solution)/shard_map/add | solution.py:443
  123.7 1.6 %collective-permute-start.29 = (f32[192,512]{1,0:T(8,128)S(1)}, f32[192,512]{1,0:T(8,128)S(1)}, u32[]{:S(2)}, u32[]{:S(2)}) collective-permute-start(f32[192,512]{1,0:T(8,128)S(1)} %get-tuple-element.50), channel_id=1, source_target_pairs={{0,64},{64,0},{1,65},{65,1},{2,66},{66,2},{3,67},{67,3},{4,68},{68... | collective-permute-start | bytes 1179656 | tf_op jit(solution)/shard_map/ppermute | solution.py:38
  125.3 1.0 collective-permute-start.28
  126.3 2.3 %collective-permute-start.27 = (f32[160,128]{1,0:T(8,128)S(1)}, f32[160,128]{1,0:T(8,128)S(1)}, u32[]{:S(2)}, u32[]{:S(2)}) collective-permute-start(f32[160,128]{1,0:T(8,128)S(1)} %add_add_fusion), channel_id=1, source_target_pairs={{0,64},{8,72},{64,0},{72,8},{1,65},{9,73},{65,1},{73,9},{2,66},{10... | collective-permute-start | bytes 245768 | tf_op jit(solution)/shard_map/ppermute | solution.py:38
  128.6 1.3 collective-permute-start.26
  129.9 8.6 %collective-permute-done.28 = f32[160,128]{1,0:T(8,128)S(1)} collective-permute-done((f32[160,128]{1,0:T(8,128)S(1)}, f32[160,128]{1,0:T(8,128)S(1)}, u32[]{:S(2)}, u32[]{:S(2)}) %collective-permute-start.28) | collective-permute-done | bytes 81952 | tf_op jit(solution)/shard_map/ppermute | solution.py:38
  138.6 1.0 collective-permute-done.27
  139.7 2.1 %collective-permute-start.31 = (f32[192,512]{1,0:T(8,128)S(1)}, f32[192,512]{1,0:T(8,128)S(1)}, u32[]{:S(2)}, u32[]{:S(2)}) collective-permute-start(f32[192,512]{1,0:T(8,128)S(1)} %get-tuple-element.55), channel_id=1, source_target_pairs={{0,8},{8,0},{1,9},{9,1},{2,10},{10,2},{3,11},{11,3},{4,12},{12,4},... | collective-permute-start | bytes 1179656 | tf_op jit(solution)/shard_map/ppermute | solution.py:38
  142.6 8.1 %tail.1 = f32[512,512]{1,0:T(8,128)} custom-call(f32[4,160,128]{2,1,0:T(8,128)} %copy-done.2, f32[4,160,128]{2,1,0:T(8,128)} %copy-done.12, f32[512,512]{1,0:T(8,128)} %l_ref.5, f32[4,128,128]{2,1,0:T(8,128)} %get-tuple-element.24.refs_0_.inv_ref, f32[512,512]{1,0:T(8,128)} %dg_ref.1), custom_call_target="tpu_custom_call" | custom-call | flops 8000000000 | bytes 5000000 | tf_op jit(solution)/shard_map/tail/pallas_call | solution.py:388
  151.3 0.8 copy-done.11
  152.1 3.5 %solve.1 = f32[192,512]{1,0:T(8,128)} custom-call(f32[192,512]{1,0:T(8,128)} %get-tuple-element.45.r_ref, f32[192,512]{1,0:T(8,128)} %copy-done.11, f32[192,512]{1,0:T(8,128)} %copy-done.10, f32[512,512]{1,0:T(8,128)} %l_ref.5, f32[4,128,128]{2,1,0:T(8,128)} %get-tuple-element.24.refs_0_.inv_ref), custom_call_target="tpu_custom_call" | custom-call | flops 1000000000 | bytes 3000000 | tf_op jit(solution)/shard_map/solve/pallas_call | solution.py:410
  (57 shorter events, 5.1 us)
Async XLA Ops:
  0.6 9.7 %collective-permute-start.1 = (bf16[192,512]{1,0:T(8,128)(2,1)}, bf16[192,512]{1,0:T(8,128)(2,1)S(1)}, u32[]{:S(2)}, u32[]{:S(2)}) collective-permute-start(bf16[192,512]{1,0:T(8,128)(2,1)} %p.1), channel_id=1, source_target_pairs={{0,8},{8,0},{1,9},{9,1},{2,10},{10,2},{3,11},{11,3},{4,12},{12,4},... | collective-permute-start | bytes 589832 | tf_op jit(solution)/shard_map/ppermute | solution.py:38
  1.1 11.7 %collective-permute-start = (bf16[192,512]{1,0:T(8,128)(2,1)}, bf16[192,512]{1,0:T(8,128)(2,1)S(1)}, u32[]{:S(2)}, u32[]{:S(2)}) collective-permute-start(bf16[192,512]{1,0:T(8,128)(2,1)} %p.1), channel_id=1, source_target_pairs={{0,64},{64,0},{1,65},{65,1},{2,66},{66,2},{3,67},{67,3},{4,68},{68... | collective-permute-start | bytes 589832 | tf_op jit(solution)/shard_map/ppermute | solution.py:38
  10.3 2.4 %copy-start.4 = (bf16[192,512]{1,0:T(8,128)(2,1)}, bf16[192,512]{1,0:T(8,128)(2,1)S(1)}, u32[]{:S(2)}) copy-start(bf16[192,512]{1,0:T(8,128)(2,1)S(1)} %collective-permute-done.1.zs) | copy-start | bytes 589828
  12.8 0.7 copy-start.5
  15.5 14.2 %collective-permute-start.4 = (bf16[2,192,512]{2,1,0:T(8,128)(2,1)}, bf16[2,192,512]{2,1,0:T(8,128)(2,1)S(1)}, u32[]{:S(2)}, u32[]{:S(2)}) collective-permute-start(bf16[2,192,512]{2,1,0:T(8,128)(2,1)} %get-tuple-element.25), channel_id=1, source_target_pairs={{0,4},{2,6},{4,0},{6,2},{1,5},{3,7},{5,1},{7,3},{8,12},{10,14},{12... | collective-permute-start | bytes 1179656 | tf_op jit(solution)/shard_map/ppermute | solution.py:38
  19.4 17.7 %collective-permute-start.3 = (bf16[2,192,512]{2,1,0:T(8,128)(2,1)}, bf16[2,192,512]{2,1,0:T(8,128)(2,1)S(1)}, u32[]{:S(2)}, u32[]{:S(2)}) collective-permute-start(bf16[2,192,512]{2,1,0:T(8,128)(2,1)} %get-tuple-element.25), channel_id=1, source_target_pairs={{0,6},{2,0},{4,2},{6,4},{1,7},{3,1},{5,3},{7,5},{8,14},{10,8},{12,... | collective-permute-start | bytes 1179656 | tf_op jit(solution)/shard_map/ppermute | solution.py:38
  20.1 16.9 %collective-permute-start.2 = (bf16[2,192,512]{2,1,0:T(8,128)(2,1)}, bf16[2,192,512]{2,1,0:T(8,128)(2,1)S(1)}, u32[]{:S(2)}, u32[]{:S(2)}) collective-permute-start(bf16[2,192,512]{2,1,0:T(8,128)(2,1)} %get-tuple-element.25), channel_id=1, source_target_pairs={{0,2},{2,4},{4,6},{6,0},{1,3},{3,5},{5,7},{7,1},{8,10},{10,12},{12... | collective-permute-start | bytes 1179656 | tf_op jit(solution)/shard_map/ppermute | solution.py:38
  21.4 15.6 %collective-permute-start.7 = (bf16[2,192,512]{2,1,0:T(8,128)(2,1)}, bf16[2,192,512]{2,1,0:T(8,128)(2,1)S(1)}, u32[]{:S(2)}, u32[]{:S(2)}) collective-permute-start(bf16[2,192,512]{2,1,0:T(8,128)(2,1)} %get-tuple-element.37.x_two), channel_id=1, source_target_pairs={{0,32},{16,48},{32,0},{48,16},{1,33},{17,49},{33,1},{49,17},{2,34}... | collective-permute-start | bytes 1179656 | tf_op jit(solution)/shard_map/ppermute | solution.py:38
  24.4 16.4 %collective-permute-start.6 = (bf16[2,192,512]{2,1,0:T(8,128)(2,1)}, bf16[2,192,512]{2,1,0:T(8,128)(2,1)S(1)}, u32[]{:S(2)}, u32[]{:S(2)}) collective-permute-start(bf16[2,192,512]{2,1,0:T(8,128)(2,1)} %get-tuple-element.37.x_two), channel_id=1, source_target_pairs={{0,48},{16,0},{32,16},{48,32},{1,49},{17,1},{33,17},{49,33},{2,50}... | collective-permute-start | bytes 1179656 | tf_op jit(solution)/shard_map/ppermute | solution.py:38
  29.7 11.2 %collective-permute-start.5 = (bf16[2,192,512]{2,1,0:T(8,128)(2,1)}, bf16[2,192,512]{2,1,0:T(8,128)(2,1)S(1)}, u32[]{:S(2)}, u32[]{:S(2)}) collective-permute-start(bf16[2,192,512]{2,1,0:T(8,128)(2,1)} %get-tuple-element.37.x_two), channel_id=1, source_target_pairs={{0,16},{16,32},{32,48},{48,0},{1,17},{17,33},{33,49},{49,1},{2,18}... | collective-permute-start | bytes 1179656 | tf_op jit(solution)/shard_map/ppermute | solution.py:38
  37.1 9.3 %copy-start.7 = (bf16[2,192,512]{2,1,0:T(8,128)(2,1)}, bf16[2,192,512]{2,1,0:T(8,128)(2,1)S(1)}, u32[]{:S(2)}) copy-start(bf16[2,192,512]{2,1,0:T(8,128)(2,1)S(1)} %collective-permute-done.7.r2) | copy-start | bytes 1179652
  40.8 5.5 %copy-start.8 = (bf16[2,192,512]{2,1,0:T(8,128)(2,1)}, bf16[2,192,512]{2,1,0:T(8,128)(2,1)S(1)}, u32[]{:S(2)}) copy-start(bf16[2,192,512]{2,1,0:T(8,128)(2,1)S(1)} %collective-permute-done.6.r3) | copy-start | bytes 1179652
  40.8 0.8 copy-start.9
  42.8 3.5 %copy-start = (bf16[4,2,192,512]{3,2,1,0:T(8,128)(2,1)}, bf16[4,2,192,512]{3,2,1,0:T(8,128)(2,1)S(1)}, u32[]{:S(2)}) copy-start(bf16[4,2,192,512]{3,2,1,0:T(8,128)(2,1)S(1)} %pad_maximum_fusion.z_all) | copy-start | bytes 4718596
  42.8 3.5 %collective-permute-start.8 = (bf16[4,2,192,512]{3,2,1,0:T(8,128)(2,1)S(1)}, bf16[4,2,192,512]{3,2,1,0:T(8,128)(2,1)S(1)}, u32[]{:S(2)}, u32[]{:S(2)}) collective-permute-start(bf16[4,2,192,512]{3,2,1,0:T(8,128)(2,1)S(1)} %pad_maximum_fusion.z_all), channel_id=1, source_target_pairs={{0,1},{1,0},{2,3},{3,2},{4,5},{5,4},{6,7},{7,6},{8,9},{9,8},{10,11... | collective-permute-start | bytes 4718600 | tf_op jit(solution)/shard_map/ppermute | solution.py:38
  46.3 1.2 copy-start.6
  60.6 5.5 %copy-start.3 = (f32[4,160,128]{2,1,0:T(8,128)S(1)}, f32[4,160,128]{2,1,0:T(8,128)}, u32[]{:S(2)}) copy-start(f32[4,160,128]{2,1,0:T(8,128)} %get-tuple-element.35) | copy-start | bytes 983044
  60.6 5.5 %collective-permute-start.12 = (f32[4,160,128]{2,1,0:T(8,128)}, f32[4,160,128]{2,1,0:T(8,128)S(1)}, u32[]{:S(2)}, u32[]{:S(2)}) collective-permute-start(f32[4,160,128]{2,1,0:T(8,128)} %get-tuple-element.36), channel_id=1, source_target_pairs={{0,1},{1,0},{2,3},{3,2},{4,5},{5,4},{6,7},{7,6},{8,9},{9,8},{10,11... | collective-permute-start | bytes 983048 | tf_op jit(solution)/shard_map/ppermute | solution.py:38
  62.7 12.7 %collective-permute-start.11 = (f16[2,192,512]{2,1,0:T(8,128)(2,1)S(1)}, f16[2,192,512]{2,1,0:T(8,128)(2,1)S(1)}, u32[]{:S(2)}, u32[]{:S(2)}) collective-permute-start(f16[2,192,512]{2,1,0:T(8,128)(2,1)S(1)} %get-tuple-element.53), channel_id=1, source_target_pairs={{0,16},{16,32},{32,48},{48,0},{1,17},{17,33},{33,49},{49,1},{2,18}... | collective-permute-start | bytes 1179656 | tf_op jit(solution)/shard_map/ppermute | solution.py:38
  64.2 11.2 %collective-permute-start.10 = (f16[2,192,512]{2,1,0:T(8,128)(2,1)S(1)}, f16[2,192,512]{2,1,0:T(8,128)(2,1)S(1)}, u32[]{:S(2)}, u32[]{:S(2)}) collective-permute-start(f16[2,192,512]{2,1,0:T(8,128)(2,1)S(1)} %get-tuple-element.54), channel_id=1, source_target_pairs={{0,48},{16,0},{32,16},{48,32},{1,49},{17,1},{33,17},{49,33},{2,50}... | collective-permute-start | bytes 1179656 | tf_op jit(solution)/shard_map/ppermute | solution.py:38
  66.1 5.3 %collective-permute-start.13 = (f32[160,128]{1,0:T(8,128)S(1)}, f32[160,128]{1,0:T(8,128)S(1)}, u32[]{:S(2)}, u32[]{:S(2)}) collective-permute-start(f32[160,128]{1,0:T(8,128)S(1)} %get-tuple-element.56), channel_id=1, source_target_pairs={{0,8},{8,64},{64,72},{72,0},{1,9},{9,65},{65,73},{73,1},{2,10},{10... | collective-permute-start | bytes 245768 | tf_op jit(solution)/shard_map/ppermute | solution.py:38
  66.6 6.6 %collective-permute-start.15 = (f32[160,128]{1,0:T(8,128)S(1)}, f32[160,128]{1,0:T(8,128)S(1)}, u32[]{:S(2)}, u32[]{:S(2)}) collective-permute-start(f32[160,128]{1,0:T(8,128)S(1)} %get-tuple-element.57), channel_id=1, source_target_pairs={{0,64},{8,72},{64,0},{72,8},{1,65},{9,73},{65,1},{73,9},{2,66},{10... | collective-permute-start | bytes 245768 | tf_op jit(solution)/shard_map/ppermute | solution.py:38
  70.1 4.4 %collective-permute-start.14 = (f32[160,128]{1,0:T(8,128)S(1)}, f32[160,128]{1,0:T(8,128)S(1)}, u32[]{:S(2)}, u32[]{:S(2)}) collective-permute-start(f32[160,128]{1,0:T(8,128)S(1)} %get-tuple-element.58), channel_id=1, source_target_pairs={{0,72},{8,0},{64,8},{72,64},{1,73},{9,1},{65,9},{73,65},{2,74},{10... | collective-permute-start | bytes 245768 | tf_op jit(solution)/shard_map/ppermute | solution.py:38
  88.4 9.6 %collective-permute-start.16 = (f32[4,2,192,512]{3,2,1,0:T(8,128)}, f32[4,2,192,512]{3,2,1,0:T(8,128)S(1)}, u32[]{:S(2)}, u32[]{:S(2)}) collective-permute-start(f32[4,2,192,512]{3,2,1,0:T(8,128)} %get-tuple-element.39), channel_id=1, source_target_pairs={{0,1},{1,0},{2,3},{3,2},{4,5},{5,4},{6,7},{7,6},{8,9},{9,8},{10,11... | collective-permute-start | bytes 9437192 | tf_op jit(solution)/shard_map/ppermute | solution.py:38
  88.5 6.1 %collective-permute-start.19 = (f32[160,128]{1,0:T(8,128)S(1)}, f32[160,128]{1,0:T(8,128)S(1)}, u32[]{:S(2)}, u32[]{:S(2)}) collective-permute-start(f32[160,128]{1,0:T(8,128)S(1)} %fusion.16), channel_id=1, source_target_pairs={{0,6},{2,0},{4,2},{6,4},{1,7},{3,1},{5,3},{7,5},{8,14},{10,8},{12,... | collective-permute-start | bytes 245768 | tf_op jit(solution)/shard_map/ppermute | solution.py:38
  90.5 7.5 %collective-permute-start.18 = (f32[160,128]{1,0:T(8,128)S(1)}, f32[160,128]{1,0:T(8,128)S(1)}, u32[]{:S(2)}, u32[]{:S(2)}) collective-permute-start(f32[160,128]{1,0:T(8,128)S(1)} %fusion.16), channel_id=1, source_target_pairs={{0,2},{2,4},{4,6},{6,0},{1,3},{3,5},{5,7},{7,1},{8,10},{10,12},{12... | collective-permute-start | bytes 245768 | tf_op jit(solution)/shard_map/ppermute | solution.py:38
  90.6 7.4 %collective-permute-start.17 = (f32[160,128]{1,0:T(8,128)S(1)}, f32[160,128]{1,0:T(8,128)S(1)}, u32[]{:S(2)}, u32[]{:S(2)}) collective-permute-start(f32[160,128]{1,0:T(8,128)S(1)} %fusion.16), channel_id=1, source_target_pairs={{0,4},{2,6},{4,0},{6,2},{1,5},{3,7},{5,1},{7,3},{8,12},{10,14},{12... | collective-permute-start | bytes 245768 | tf_op jit(solution)/shard_map/ppermute | solution.py:38
  92.1 15.5 %collective-permute-start.9 = (f16[2,192,512]{2,1,0:T(8,128)(2,1)S(1)}, f16[2,192,512]{2,1,0:T(8,128)(2,1)S(1)}, u32[]{:S(2)}, u32[]{:S(2)}) collective-permute-start(f16[2,192,512]{2,1,0:T(8,128)(2,1)S(1)} %get-tuple-element.52), channel_id=1, source_target_pairs={{0,32},{16,48},{32,0},{48,16},{1,33},{17,49},{33,1},{49,17},{2,34}... | collective-permute-start | bytes 1179656 | tf_op jit(solution)/shard_map/ppermute | solution.py:38
  98.0 23.3 %copy-start.1 = (f32[192,512]{1,0:T(8,128)S(1)}, f32[192,512]{1,0:T(8,128)}, u32[]{:S(2)}) copy-start(f32[192,512]{1,0:T(8,128)} %pg_ref.1) | copy-start | bytes 1179652
  100.7 13.6 %collective-permute-start.20 = (f16[2,192,512]{2,1,0:T(8,128)(2,1)S(1)}, f16[2,192,512]{2,1,0:T(8,128)(2,1)S(1)}, u32[]{:S(2)}, u32[]{:S(2)}) collective-permute-start(f16[2,192,512]{2,1,0:T(8,128)(2,1)S(1)} %get-tuple-element.46), channel_id=1, source_target_pairs={{0,4},{2,6},{4,0},{6,2},{1,5},{3,7},{5,1},{7,3},{8,12},{10,14},{12... | collective-permute-start | bytes 1179656 | tf_op jit(solution)/shard_map/ppermute | solution.py:38
  101.4 19.9 %collective-permute-start.22 = (f16[2,192,512]{2,1,0:T(8,128)(2,1)S(1)}, f16[2,192,512]{2,1,0:T(8,128)(2,1)S(1)}, u32[]{:S(2)}, u32[]{:S(2)}) collective-permute-start(f16[2,192,512]{2,1,0:T(8,128)(2,1)S(1)} %get-tuple-element.47), channel_id=1, source_target_pairs={{0,2},{2,4},{4,6},{6,0},{1,3},{3,5},{5,7},{7,1},{8,10},{10,12},{12... | collective-permute-start | bytes 1179656 | tf_op jit(solution)/shard_map/ppermute | solution.py:38
  103.4 17.9 %collective-permute-start.21 = (f16[2,192,512]{2,1,0:T(8,128)(2,1)S(1)}, f16[2,192,512]{2,1,0:T(8,128)(2,1)S(1)}, u32[]{:S(2)}, u32[]{:S(2)}) collective-permute-start(f16[2,192,512]{2,1,0:T(8,128)(2,1)S(1)} %get-tuple-element.48), channel_id=1, source_target_pairs={{0,6},{2,0},{4,2},{6,4},{1,7},{3,1},{5,3},{7,5},{8,14},{10,8},{12,... | collective-permute-start | bytes 1179656 | tf_op jit(solution)/shard_map/ppermute | solution.py:38
  104.6 20.7 %collective-permute-start.25 = (f32[160,128]{1,0:T(8,128)S(1)}, f32[160,128]{1,0:T(8,128)S(1)}, u32[]{:S(2)}, u32[]{:S(2)}) collective-permute-start(f32[160,128]{1,0:T(8,128)S(1)} %add_add_fusion.1), channel_id=1, source_target_pairs={{0,48},{16,0},{32,16},{48,32},{1,49},{17,1},{33,17},{49,33},{2,50}... | collective-permute-start | bytes 245768 | tf_op jit(solution)/shard_map/ppermute | solution.py:38
  107.6 17.7 %collective-permute-start.24 = (f32[160,128]{1,0:T(8,128)S(1)}, f32[160,128]{1,0:T(8,128)S(1)}, u32[]{:S(2)}, u32[]{:S(2)}) collective-permute-start(f32[160,128]{1,0:T(8,128)S(1)} %add_add_fusion.1), channel_id=1, source_target_pairs={{0,16},{16,32},{32,48},{48,0},{1,17},{17,33},{33,49},{49,1},{2,18}... | collective-permute-start | bytes 245768 | tf_op jit(solution)/shard_map/ppermute | solution.py:38
  114.3 11.0 %collective-permute-start.23 = (f32[160,128]{1,0:T(8,128)S(1)}, f32[160,128]{1,0:T(8,128)S(1)}, u32[]{:S(2)}, u32[]{:S(2)}) collective-permute-start(f32[160,128]{1,0:T(8,128)S(1)} %add_add_fusion.1), channel_id=1, source_target_pairs={{0,32},{16,48},{32,0},{48,16},{1,33},{17,49},{33,1},{49,17},{2,34}... | collective-permute-start | bytes 245768 | tf_op jit(solution)/shard_map/ppermute | solution.py:38
  123.7 15.9 %collective-permute-start.29 = (f32[192,512]{1,0:T(8,128)S(1)}, f32[192,512]{1,0:T(8,128)S(1)}, u32[]{:S(2)}, u32[]{:S(2)}) collective-permute-start(f32[192,512]{1,0:T(8,128)S(1)} %get-tuple-element.50), channel_id=1, source_target_pairs={{0,64},{64,0},{1,65},{65,1},{2,66},{66,2},{3,67},{67,3},{4,68},{68... | collective-permute-start | bytes 1179656 | tf_op jit(solution)/shard_map/ppermute | solution.py:38
  125.3 13.3 %collective-permute-start.28 = (f32[160,128]{1,0:T(8,128)S(1)}, f32[160,128]{1,0:T(8,128)S(1)}, u32[]{:S(2)}, u32[]{:S(2)}) collective-permute-start(f32[160,128]{1,0:T(8,128)S(1)} %add_add_fusion), channel_id=1, source_target_pairs={{0,72},{8,0},{64,8},{72,64},{1,73},{9,1},{65,9},{73,65},{2,74},{10... | collective-permute-start | bytes 245768 | tf_op jit(solution)/shard_map/ppermute | solution.py:38
  126.3 13.3 %collective-permute-start.27 = (f32[160,128]{1,0:T(8,128)S(1)}, f32[160,128]{1,0:T(8,128)S(1)}, u32[]{:S(2)}, u32[]{:S(2)}) collective-permute-start(f32[160,128]{1,0:T(8,128)S(1)} %add_add_fusion), channel_id=1, source_target_pairs={{0,64},{8,72},{64,0},{72,8},{1,65},{9,73},{65,1},{73,9},{2,66},{10... | collective-permute-start | bytes 245768 | tf_op jit(solution)/shard_map/ppermute | solution.py:38
  128.6 11.0 %collective-permute-start.26 = (f32[160,128]{1,0:T(8,128)S(1)}, f32[160,128]{1,0:T(8,128)S(1)}, u32[]{:S(2)}, u32[]{:S(2)}) collective-permute-start(f32[160,128]{1,0:T(8,128)S(1)} %add_add_fusion), channel_id=1, source_target_pairs={{0,8},{8,64},{64,72},{72,0},{1,9},{9,65},{65,73},{73,1},{2,10},{10... | collective-permute-start | bytes 245768 | tf_op jit(solution)/shard_map/ppermute | solution.py:38
  139.6 2.3 %copy-start.2 = (f32[4,160,128]{2,1,0:T(8,128)}, f32[4,160,128]{2,1,0:T(8,128)S(1)}, u32[]{:S(2)}) copy-start(f32[4,160,128]{2,1,0:T(8,128)S(1)} %pad_maximum_fusion.1.mine) | copy-start | bytes 983044
  139.6 11.1 %copy-start.10 = (f32[192,512]{1,0:T(8,128)}, f32[192,512]{1,0:T(8,128)S(1)}, u32[]{:S(2)}) copy-start(f32[192,512]{1,0:T(8,128)S(1)} %collective-permute-done.29.t_ref) | copy-start | bytes 1179652
  139.6 2.2 %collective-permute-start.30 = (f32[4,160,128]{2,1,0:T(8,128)S(1)}, f32[4,160,128]{2,1,0:T(8,128)S(1)}, u32[]{:S(2)}, u32[]{:S(2)}) collective-permute-start(f32[4,160,128]{2,1,0:T(8,128)S(1)} %pad_maximum_fusion.1.mine), channel_id=1, source_target_pairs={{0,1},{1,0},{2,3},{3,2},{4,5},{5,4},{6,7},{7,6},{8,9},{9,8},{10,11... | collective-permute-start | bytes 983048 | tf_op jit(solution)/shard_map/ppermute | solution.py:38
  139.7 11.6 %collective-permute-start.31 = (f32[192,512]{1,0:T(8,128)S(1)}, f32[192,512]{1,0:T(8,128)S(1)}, u32[]{:S(2)}, u32[]{:S(2)}) collective-permute-start(f32[192,512]{1,0:T(8,128)S(1)} %get-tuple-element.55), channel_id=1, source_target_pairs={{0,8},{8,0},{1,9},{9,1},{2,10},{10,2},{3,11},{11,3},{4,12},{12,4},... | collective-permute-start | bytes 1179656 | tf_op jit(solution)/shard_map/ppermute | solution.py:38
  141.9 0.7 copy-start.12
  151.3 0.8 copy-start.11

commit v4 on v3

--- a/solution.py
+++ b/solution.py
@@ -17,7 +17,7 @@
 LOWER = [(i, j) for i in range(NB) for j in range(i + 1)]
 CH = len(LOWER) * BLK // 8
 VMEM_LIMIT = 60 * 1024 * 1024
-NEAR = (1, 3, 2)
+NEAR = (2, 3, 1)
 
 
 def whole():
@@ -40,6 +40,15 @@
 
 def after(x, *done):
     return lax.optimization_barrier((x, *done))[0]
+
+
+def swap(x, axis, far):
+    return lax.ppermute(x, axis, [(i, 3 - i if far else i ^ 1) for i in range(4)])
+
+
+def chunk_order(y):
+    near = y + 1 - 2 * lax.rem(y, 2)
+    return (y, 3 - y, near, 3 - near)
 
 
 def iotas(n):
@@ -103,44 +112,27 @@
     return ref.at[pl.ds(pl.multiple_of(i * U, U), U), :]
 
 
-def pair_kernel(p, xs, zs, *refs):
-    x_two, z_two = refs[-2:]
-    x_two[0] = p[...]
-    z_two[0] = p[...]
-    x_two[1] = xs[...]
-    z_two[1] = zs[...]
-
-
-def pair(p, xs, zs, *after):
-    return pl.pallas_call(
-        pair_kernel,
-        out_shape=[jax.ShapeDtypeStruct((2, U, B), bf16)] * 2,
-        in_specs=[whole()] * 3 + [ANY] * len(after),
-        out_specs=[whole()] * 2,
-        compiler_params=params(),
-        cost_estimate=pl.CostEstimate(flops=0, bytes_accessed=1_600_000, transcendentals=0),
-        name="pair",
-    )(p, xs, zs, *after)
-
-
-def direct_kernel(f_hbm, x_two, r1, r3, r2, *refs):
+def direct_kernel(f_hbm, x_two, r2, r3, r1, *refs):
     mine, other, fbuf, pc, keep, give, s_f, s_in, s_out = refs[-9:]
     x, yh = lax.axis_index("x"), lax.axis_index("yh")
     z, yl, c = lax.axis_index("z"), lax.axis_index("yl"), lax.axis_index("c")
 
-    def f_copy(i):
-        k, m = i // 2, lax.rem(i, 2)
-        pair_at = lax.rem(yl + m, 2) * 4 + lax.rem(z + k, 4)
-        cols = pl.ds(pl.multiple_of(pair_at * 2 * U, 2 * U), 2 * U)
-        return pltpu.make_async_copy(f_hbm.at[:, cols], fbuf.at[lax.rem(i, 2)], s_f.at[lax.rem(i, 2)])
+    def f_copies(k):
+        slot = lax.rem(k, 2)
+        made = []
+        for m in (0, 1):
+            at = lax.rem(yl + m, 2) * 4 + lax.rem(z + k, 4)
+            cols = pl.ds(pl.multiple_of(at * 2 * U, 2 * U), 2 * U)
+            dst = fbuf.at[slot, :, m * 2 * U : (m + 1) * 2 * U]
+            made.append(pltpu.make_async_copy(f_hbm.at[:, cols], dst, s_f.at[slot, m]))
+        return made
 
     jobs = [(yh * 4 + x, x_two.at[0]), ((1 - yh) * 4 + x, x_two.at[1])]
-    for k, r in zip(NEAR, (r1, r3, r2)):
+    for k, r in zip(NEAR, (r2, r3, r1)):
         xs = lax.rem(x + 4 - k, 4)
         jobs += [(yh * 4 + xs, r.at[0]), ((1 - yh) * 4 + xs, r.at[1])]
     ins = [pltpu.make_async_copy(src, band(pc, a), s_in.at[i]) for i, (a, src) in enumerate(jobs)]
-    f_copy(0).start()
-    for cp in ins:
+    for cp in f_copies(0) + ins:
         cp.start()
     for cp in ins:
         cp.wait()
@@ -151,26 +143,24 @@
             pltpu.make_async_copy(give.at[k], other.at[k], s_out.at[4 + k]),
         )
 
-    def step(i, _):
-        @pl.when(i < 7)
+    def step(k, _):
+        @pl.when(k < 3)
         def _():
-            f_copy(i + 1).start()
-
-        f_copy(i).wait()
-        d = lax.dot_general(fbuf[lax.rem(i, 2)], pc[...], DIM0, preferred_element_type=f32)
-        lo, hi = d[:U], d[U:]
-        k, m = i // 2, lax.rem(i, 2)
-        keep[k, m] = jnp.where(c == 0, lo, hi)
-        give[k, m] = jnp.where(c == 0, hi, lo)
-
-        @pl.when(m == 1)
-        def _():
-            for cp in out_copies(k):
+            for cp in f_copies(k + 1):
                 cp.start()
 
+        for cp in f_copies(k):
+            cp.wait()
+        d = lax.dot_general(fbuf[lax.rem(k, 2)], pc[...], DIM0, preferred_element_type=f32)
+        for m in (0, 1):
+            lo, hi = d[2 * m * U : (2 * m + 1) * U], d[(2 * m + 1) * U : (2 * m + 2) * U]
+            keep[k, m] = jnp.where(c == 0, lo, hi)
+            give[k, m] = jnp.where(c == 0, hi, lo)
+        for cp in out_copies(k):
+            cp.start()
         return 0
 
-    lax.fori_loop(0, 8, step, 0)
+    lax.fori_loop(0, 4, step, 0)
     for k in range(4):
         for cp in out_copies(k):
             cp.wait()
@@ -182,11 +172,11 @@
         in_specs=[ANY] * (5 + len(after)),
         out_specs=[ANY] * 2,
         scratch_shapes=[
-            pltpu.VMEM((2, 8 * U, 2 * U), bf16),
+            pltpu.VMEM((2, 8 * U, 4 * U), bf16),
             pltpu.VMEM((8 * U, B), bf16),
             pltpu.VMEM((4, 2, U, B), f32),
             pltpu.VMEM((4, 2, U, B), f32),
-            pltpu.SemaphoreType.DMA((2,)),
+            pltpu.SemaphoreType.DMA((2, 2)),
             pltpu.SemaphoreType.DMA((8,)),
             pltpu.SemaphoreType.DMA((8,)),
         ],
@@ -197,18 +187,17 @@
     )(flip, x_two, *recv, *after)
 
 
-def transposed_kernel(f_hbm, z_all, p_all, x_two, r1, r3, r2, g_hbm, *refs):
+def transposed_kernel(f_hbm, z_all, p_all, x_two, r2, r3, r1, g_hbm, *refs):
     out, mine, other, fbuf, pr, pc, acc, g, tbuf, flat, s_f, s_in, s_out = refs[-13:]
     x, yh = lax.axis_index("x"), lax.axis_index("yh")
     z, yl, c = lax.axis_index("z"), lax.axis_index("yl"), lax.axis_index("c")
     y = yh * 2 + yl
 
-    def f_copies(k):
-        slot = lax.rem(k, 2)
+    def f_copies(s):
         made = []
-        for m in (0, 1):
-            a = lax.rem(yh + m, 2) * 4 + lax.rem(x + k, 4)
-            made.append(pltpu.make_async_copy(band(f_hbm, a), fbuf.at[slot, pl.ds(m * U, U)], s_f.at[slot, m]))
+        for j in range(4):
+            a = lax.rem(yh + j % 2, 2) * 4 + lax.rem(x + 2 * s + j // 2, 4)
+            made.append(pltpu.make_async_copy(band(f_hbm, a), fbuf.at[s, pl.ds(j * U, U)], s_f.at[s, j]))
         return made
 
     first = []
@@ -219,7 +208,7 @@
             first.append(((yb * 4 + zs) * 2 + 1 - c, p_all.at[k, m]))
     ins = [pltpu.make_async_copy(src, band(pr, a), s_in.at[i]) for i, (a, src) in enumerate(first)]
     local_rows = {0: x_two}
-    for k, r in zip(NEAR, (r1, r3, r2)):
+    for k, r in zip(NEAR, (r2, r3, r1)):
         local_rows[4 - k] = r
     late = [
         pltpu.make_async_copy(r.at[m], band(pc, 2 * k + m), s_in.at[16 + 2 * k + m])
@@ -238,37 +227,37 @@
     def out_copy(k):
         return pltpu.make_async_copy(tbuf.at[k], out.at[k], s_out.at[k])
 
-    def step(k, _):
-        @pl.when(k < 3)
+    def step(s, _):
+        @pl.when(s == 0)
         def _():
-            for cp in f_copies(k + 1):
+            for cp in f_copies(1):
                 cp.start()
 
-        for cp in f_copies(k):
+        for cp in f_copies(s):
             cp.wait()
-        t = jnp.dot(fbuf[lax.rem(k, 2)], pr[...], preferred_element_type=f32)
-        tbuf[k, 0] = t[:U]
-        tbuf[k, 1] = t[U:]
-        out_copy(k).start()
-
-        @pl.when(k == 0)
+        t = jnp.dot(fbuf[s], pr[...], preferred_element_type=f32)
+        for j in range(4):
+            tbuf[2 * s + j // 2, j % 2] = t[j * U : (j + 1) * U]
+        out_copy(2 * s).start()
+        out_copy(2 * s + 1).start()
+
+        @pl.when(s == 0)
         def _():
             for cp in late:
                 cp.wait()
 
         hi = t.astype(bf16)
         lo = (t - hi.astype(f32)).astype(bf16)
-        p = pc[pl.ds(pl.multiple_of(k * 2 * U, 2 * U), 2 * U), :]
+        p = pc[pl.ds(pl.multiple_of(s * 4 * U, 4 * U), 4 * U), :]
         acc[...] += lax.dot_general(p, hi, DIM0, preferred_element_type=f32) + lax.dot_general(
             p, lo, DIM0, preferred_element_type=f32
         )
         return 0
 
-    lax.fori_loop(0, 4, step, 0)
+    lax.fori_loop(0, 2, step, 0)
     for n, (i, j) in enumerate(LOWER):
         flat[n * BLK : (n + 1) * BLK, :] = block(g, i, j) - block(acc, i, j) - block(acc, j, i).T
-    for k in range(4):
-        q = lax.rem(y + k, 4)
+    for k, q in enumerate(chunk_order(y)):
         mine[k] = flat[pl.ds(pl.multiple_of((c * 4 + q) * CH, CH), CH), :]
         other[k] = flat[pl.ds(pl.multiple_of(((1 - c) * 4 + q) * CH, CH), CH), :]
     for k in range(4):
@@ -281,14 +270,14 @@
         in_specs=[ANY] * (8 + len(after)),
         out_specs=[ANY, whole(), whole()],
         scratch_shapes=[
-            pltpu.VMEM((2, 2 * U, 16 * U), bf16),
+            pltpu.VMEM((2, 4 * U, 16 * U), bf16),
             pltpu.VMEM((16 * U, B), bf16),
             pltpu.VMEM((8 * U, B), bf16),
             pltpu.VMEM((B, B), f32),
             pltpu.VMEM((B, B), f32),
             pltpu.VMEM((4, 2, U, B), f32),
             pltpu.VMEM((8 * CH, BLK), f32),
-            pltpu.SemaphoreType.DMA((2, 2)),
+            pltpu.SemaphoreType.DMA((2, 4)),
             pltpu.SemaphoreType.DMA((25,)),
             pltpu.SemaphoreType.DMA((4,)),
         ],
@@ -323,8 +312,7 @@
 def tail_kernel(mine, other, l_ref, inv_ref, dg_ref, *refs):
     out_ref, flat = refs[-2:]
     c, y = lax.axis_index("c"), lax.axis_index("yh") * 2 + lax.axis_index("yl")
-    for k in range(4):
-        q = lax.rem(y + 4 - k, 4)
+    for k, q in enumerate(chunk_order(y)):
         flat[pl.ds(pl.multiple_of((c * 4 + q) * CH, CH), CH), :] = mine[k]
         flat[pl.ds(pl.multiple_of(((1 - c) * 4 + q) * CH, CH), CH), :] = other[k]
     rows, cols = iotas(BLK)
@@ -424,44 +412,46 @@
     x_swp = shift(panel, "yh", 1, 2)
     z_swp = shift(panel, "yl", 1, 2)
     inv, g = prep(diag_factor, panel_grad, panel)
-    x_two, z_two = pair(panel, x_swp, z_swp, inv)
+    x_swp, z_swp = after(x_swp, inv), after(z_swp, inv)
+    x_two, z_two = jnp.stack([panel, x_swp]), jnp.stack([panel, z_swp])
     z_recv = [shift(z_two, "z", k) for k in NEAR]
     x_recv = [shift(x_two, "x", k) for k in NEAR]
     z_recv, x_recv = lax.optimization_barrier((z_recv, x_recv))
-    z_all = jnp.stack([z_two, z_recv[0], z_recv[2], z_recv[1]])
+    z_all = jnp.stack([z_two, z_recv[2], z_recv[0], z_recv[1]])
     p_all = shift(z_all, "c", 1, 2)
 
     half = lambda v: (v * 64.0).astype(f16)
     full = lambda v: v.astype(f32) * (1 / 64.0)
 
     t_all, q_mine, q_other = transposed(flip, z_all, p_all, x_two, x_recv, g)
-    t_in = {k: shift(half(t_all[k]), "x", k) for k in NEAR}
-    q_pair = shift(q_other, "c", 1, 2)
-    q = [q_mine[k] + q_pair[k] for k in range(4)]
-    q_in = [shift(q[k], ("yh", "yl"), k) for k in NEAR]
-    part = q[0] + q_in[0] + q_in[1] + q_in[2]
-    t_far = t_all[0][1] + (full(t_in[2][1]) + full(t_in[3][1]) + full(t_in[1][1]))
-    t_last = shift(t_far, "yh", 1, 2)
+    t_out = {k: half(t_all[k]) for k in NEAR}
+    t_in = {k: shift(t_out[k], "x", k) for k in NEAR}
+    q_pair = shift(after(q_other, *t_out.values()), "c", 1, 2)
+    y_axis = ("yh", "yl")
+    two = q_mine[:2] + q_pair[:2] + swap(q_mine[2:] + q_pair[2:], y_axis, False)
+    part = two[0] + swap(two[1], y_axis, True)
+    t_sum = after(t_all[0] + (full(t_in[2]) + full(t_in[3]) + full(t_in[1])))
+    t_last = shift(t_sum[1], "yh", 1, 2)
     x_two = after(x_two, part, t_in[1], t_in[3])
     d_mine, d_other = direct(flip, x_two, x_recv)
     d_pair = shift(d_other, "c", 1, 2)
-    got = {k: shift(part, "z", k) for k in NEAR}
-    part = (part + got[2]) + (got[1] + got[3])
+    for far in (False, True):
+        part = part + swap(part, "z", far)
     d_pair = after(d_pair, part)
     d_own = d_mine[0] + d_pair[0]
     d_out = {k: half(d_mine[k] + d_pair[k]) for k in NEAR}
     d_in = {k: shift(d_out[k], "z", k) for k in NEAR}
     part = after(part, *d_out.values())
-    got = {k: shift(part, "x", k) for k in NEAR}
+    part = after(part + swap(part, "x", False), t_sum)
+    part = part + swap(part, "x", True)
     part = after(part, d_in[1], d_in[3])
-    part = (part + got[2]) + (got[1] + got[3])
-    q_all = jnp.stack([part] + [shift(part, ("yh", "yl"), k) for k in (1, 2, 3)])
-    q_all = after(q_all, t_last)
+    two = after(jnp.stack([part, swap(part, y_axis, True)]), t_last)
+    q_all = jnp.concatenate([two, swap(two, y_axis, False)])
     d_far = d_own[1] + (full(d_in[2][1]) + full(d_in[3][1]) + full(d_in[1][1]))
     d_last = shift(d_far, "yl", 1, 2)
     near = (
         panel_grad
-        - (t_all[0][0] + (full(t_in[2][0]) + full(t_in[3][0]) + full(t_in[1][0])))
+        - t_sum[0]
         - (d_own[0] + (full(d_in[2][0]) + full(d_in[3][0]) + full(d_in[1][0])))
     )
     q_pair = after(shift(q_all, "c", 1, 2), d_far)

time: 158 us -> 149 us (0.943)
  Pallas kernels: 46.3 us -> 40.6 us
  other arithmetic: 8.34 us -> 5.63 us
    ppermute x32 -> x20, waiting for transfers between devices: 49.5 us -> 28.9 us  [shift(): return lax.ppermute(x, axis, [(i, (i + k) % n) for i in range(n)])]
    ppermute x0 -> x8, waiting for transfers between devices: none -> 20.6 us  [swap(): lax.ppermute(x, axis, [(i, 3 - i if far else i ^ 1) for i in range(4)])]
    ppermute x0 -> x8, starting transfers between devices: none -> 16.9 us  [swap(): lax.ppermute(x, axis, [(i, 3 - i if far else i ^ 1) for i in range(4)])]
    ppermute x32 -> x20, starting transfers between devices: 46.4 us -> 30.5 us  [shift(): return lax.ppermute(x, axis, [(i, (i + k) % n) for i in range(n)])]
    pallas_call x1, Pallas kernels: 12.9 us -> 10.3 us  [direct(): pl.pallas_call(direct_kernel, in_specs=[ANY] * (5 + len(after)), out_spec...]
    pallas_call x1 -> x0, Pallas kernels: 2.04 us -> none  [pair(): pl.pallas_call(pair_kernel, out_shape=[jax.ShapeDtypeStruct((2, U, B), bf...]
    convert_element_type x2, other arithmetic: 4.64 us -> 2.81 us  [on_device(): half = lambda v: (v * 64.0).astype(f16)]
    unnamed x26 -> x31, local copies, waits for them, and re-layouts: 4.18 us -> 3.42 us
  transfers between devices with their start and end apart: 32 -> 28, of which waited for: 15 -> 17; matrix products, arithmetic and copies ran while one was open for 5% -> 2% of each run, Pallas kernels for 9% -> 10%
where the time goes in v4:
time: 149 us; the launch traced here: 147 us
  waiting for transfers between devices  49.5 us (33%)
  starting transfers between devices  47.3 us (32%)
  Pallas kernels  40.6 us (27%)
  other arithmetic  5.63 us (4%)
  local copies, waits for them, and re-layouts  3.47 us (2%)
    ppermute x20, starting transfers between devices, shift(): return lax.ppermute(x, axis, [(i, (i + k) % n) for i in range(n)])  30.5 us
    ppermute x20, waiting for transfers between devices, shift(): return lax.ppermute(x, axis, [(i, (i + k) % n) for i in range(n)])  28.9 us
    ppermute x8, waiting for transfers between devices, swap(): lax.ppermute(x, axis, [(i, 3 - i if far else i ^ 1) for i in range(4)])  20.6 us
    ppermute x8, starting transfers between devices, swap(): lax.ppermute(x, axis, [(i, 3 - i if far else i ^ 1) for i in range(4)])  16.9 us
    pallas_call x1, Pallas kernels, transposed(): pl.pallas_call(transposed_kernel, in_specs=[ANY] * (8 + len(after)), out_...  12 us
    pallas_call x1, Pallas kernels, direct(): pl.pallas_call(direct_kernel, in_specs=[ANY] * (5 + len(after)), out_spec...  10.3 us
    pallas_call x1, Pallas kernels, tail(): pl.pallas_call(tail_kernel, out_shape=jax.ShapeDtypeStruct((B, B), f32),...  8.12 us
    pallas_call x1, Pallas kernels, prep(): pl.pallas_call(prep_kernel, out_shape=(jax.ShapeDtypeStruct((NB, BLK, BLK...  6.59 us
  transfers between devices with their start and end apart: 28, of which 17 were waited for; matrix products, arithmetic and copies ran while one was open for 2% of the time, Pallas kernels for 10%

profile of v4, /device:TPU:8, one launch (start us, length us, event | category | flops | bytes accessed | tf_op | source)
XLA Modules:
  0.0 147.5 jit_solution(12875865125901694315)
XLA Ops:
  0.6 0.4 collective-permute-start
  1.1 2.7 %collective-permute-start.4 = (bf16[192,512]{1,0:T(8,128)(2,1)}, bf16[192,512]{1,0:T(8,128)(2,1)S(1)}, u32[]{:S(2)}, u32[]{:S(2)}) collective-permute-start(bf16[192,512]{1,0:T(8,128)(2,1)} %p_ref.1), channel_id=1, source_target_pairs={{0,64},{64,0},{1,65},{65,1},{2,66},{66,2},{3,67},{67,3},{4,68},{68... | collective-permute-start | bytes 589832 | tf_op jit(solution)/shard_map/ppermute | solution.py:38
  3.8 6.6 %prep.1 = (f32[4,128,128]{2,1,0:T(8,128)}, f32[512,512]{1,0:T(8,128)}) custom-call(f32[512,512]{1,0:T(8,128)} %l_ref.5, f32[192,512]{1,0:T(8,128)} %pg_ref.1, bf16[192,512]{1,0:T(8,128)(2,1)} %p_ref.1), custom_call_target="tpu_custom_call" | custom-call | flops 4000000000 | bytes 3000000 | tf_op jit(solution)/shard_map/prep/pallas_call | solution.py:93
  10.3 2.4 %collective-permute-done.4 = bf16[192,512]{1,0:T(8,128)(2,1)S(1)} collective-permute-done((bf16[192,512]{1,0:T(8,128)(2,1)}, bf16[192,512]{1,0:T(8,128)(2,1)S(1)}, u32[]{:S(2)}, u32[]{:S(2)}) %collective-permute-start.4) | collective-permute-done | bytes 196640 | tf_op jit(solution)/shard_map/ppermute | solution.py:38
  12.9 4.1 %collective-permute-start.2 = (bf16[2,192,512]{2,1,0:T(8,128)(2,1)S(1)}, bf16[2,192,512]{2,1,0:T(8,128)(2,1)S(1)}, u32[]{:S(2)}, u32[]{:S(2)}) collective-permute-start(bf16[2,192,512]{2,1,0:T(8,128)(2,1)S(1)} %get-tuple-element.60), channel_id=1, source_target_pairs={{0,6},{2,0},{4,2},{6,4},{1,7},{3,1},{5,3},{7,5},{8,14},{10,8},{12,... | collective-permute-start | bytes 1179656 | tf_op jit(solution)/shard_map/ppermute | solution.py:38
  17.0 1.3 collective-permute-start.3
  18.3 1.5 %collective-permute-start.7 = (bf16[2,192,512]{2,1,0:T(8,128)(2,1)S(1)}, bf16[2,192,512]{2,1,0:T(8,128)(2,1)S(1)}, u32[]{:S(2)}, u32[]{:S(2)}) collective-permute-start(bf16[2,192,512]{2,1,0:T(8,128)(2,1)S(1)} %get-tuple-element.40.x_two), channel_id=1, source_target_pairs={{0,16},{16,32},{32,48},{48,0},{1,17},{17,33},{33,49},{49,1},{2,18}... | collective-permute-start | bytes 1179656 | tf_op jit(solution)/shard_map/ppermute | solution.py:38
  19.8 1.7 %collective-permute-start.6 = (bf16[2,192,512]{2,1,0:T(8,128)(2,1)S(1)}, bf16[2,192,512]{2,1,0:T(8,128)(2,1)S(1)}, u32[]{:S(2)}, u32[]{:S(2)}) collective-permute-start(bf16[2,192,512]{2,1,0:T(8,128)(2,1)S(1)} %get-tuple-element.40.x_two), channel_id=1, source_target_pairs={{0,48},{16,0},{32,16},{48,32},{1,49},{17,1},{33,17},{49,33},{2,50}... | collective-permute-start | bytes 1179656 | tf_op jit(solution)/shard_map/ppermute | solution.py:38
  21.5 11.4 %collective-permute-done.2 = bf16[2,192,512]{2,1,0:T(8,128)(2,1)S(1)} collective-permute-done((bf16[2,192,512]{2,1,0:T(8,128)(2,1)S(1)}, bf16[2,192,512]{2,1,0:T(8,128)(2,1)S(1)}, u32[]{:S(2)}, u32[]{:S(2)}) %collective-permute-start.2) | collective-permute-done | bytes 393248 | tf_op jit(solution)/shard_map/ppermute | solution.py:38
  32.9 3.0 %collective-permute-start.5 = (bf16[2,192,512]{2,1,0:T(8,128)(2,1)S(1)}, bf16[2,192,512]{2,1,0:T(8,128)(2,1)S(1)}, u32[]{:S(2)}, u32[]{:S(2)}) collective-permute-start(bf16[2,192,512]{2,1,0:T(8,128)(2,1)S(1)} %get-tuple-element.40.x_two), channel_id=1, source_target_pairs={{0,32},{16,48},{32,0},{48,16},{1,33},{17,49},{33,1},{49,17},{2,34}... | collective-permute-start | bytes 1179656 | tf_op jit(solution)/shard_map/ppermute | solution.py:38
  36.4 5.8 %collective-permute-done.5.r2 = bf16[2,192,512]{2,1,0:T(8,128)(2,1)S(1)} collective-permute-done((bf16[2,192,512]{2,1,0:T(8,128)(2,1)S(1)}, bf16[2,192,512]{2,1,0:T(8,128)(2,1)S(1)}, u32[]{:S(2)}, u32[]{:S(2)}) %collective-permute-start.5) | collective-permute-done | bytes 393248 | tf_op jit(solution)/shard_map/ppermute | solution.py:38
  42.2 0.7 copy-done.10
  43.3 3.4 %collective-permute-done.8.p_all = bf16[4,2,192,512]{3,2,1,0:T(8,128)(2,1)S(1)} collective-permute-done((bf16[4,2,192,512]{3,2,1,0:T(8,128)(2,1)S(1)}, bf16[4,2,192,512]{3,2,1,0:T(8,128)(2,1)S(1)}, u32[]{:S(2)}, u32[]{:S(2)}) %collective-permute-start.8) | collective-permute-done | bytes 1572896 | tf_op jit(solution)/shard_map/ppermute | solution.py:38
  46.7 1.2 copy-done.7
  47.8 12.0 %transposed.1 = (f32[4,2,192,512]{3,2,1,0:T(8,128)}, f32[4,160,128]{2,1,0:T(8,128)}, f32[4,160,128]{2,1,0:T(8,128)}) custom-call(bf16[1536,3072]{1,0:T(8,128)(2,1)} %bitcast.61, bf16[4,2,192,512]{3,2,1,0:T(8,128)(2,1)} %copy-done.1, bf16[4,2,192,512]{3,2,1,0:T(8,128)(2,1)} %copy-done.7, bf16[2,192,512]{2,1,0:T(8,128)(2,1)} %copy-done.3, ...), custom_call_target="tpu_custom_call" | custom-call | flops 15000000512 | bytes 17000000 | tf_op jit(solution)/shard_map/transposed/pallas_call | solution.py:268
  59.9 2.0 %fusion.2 = (f16[2,192,512]{2,1,0:T(8,128)(2,1)S(1)}, f16[2,192,512]{2,1,0:T(8,128)(2,1)S(1)}, f16[2,192,512]{2,1,0:T(8,128)(2,1)S(1)}) fusion(f32[4,2,192,512]{3,2,1,0:T(8,128)} %get-tuple-element.36), kind=kLoop, calls=%fused_computation.13 | loop fusion | flops 1179648 | bytes 3538944 | tf_op jit(solution)/shard_map/convert_element_type | solution.py:423
  62.1 1.5 %collective-permute-done.12 = f32[4,160,128]{2,1,0:T(8,128)S(1)} collective-permute-done((f32[4,160,128]{2,1,0:T(8,128)S(1)}, f32[4,160,128]{2,1,0:T(8,128)S(1)}, u32[]{:S(2)}, u32[]{:S(2)}) %collective-permute-start.12) | collective-permute-done | bytes 327712 | tf_op jit(solution)/shard_map/ppermute | solution.py:38
  63.6 2.0 %collective-permute-start.13 = (f32[2,160,128]{2,1,0:T(8,128)S(1)}, f32[2,160,128]{2,1,0:T(8,128)S(1)}, u32[]{:S(2)}, u32[]{:S(2)}) collective-permute-start(f32[2,160,128]{2,1,0:T(8,128)S(1)} %slice_add_fusion.1), channel_id=1, source_target_pairs={{0,8},{8,0},{64,72},{72,64},{1,9},{9,1},{65,73},{73,65},{2,10},{10... | collective-permute-start | bytes 491528 | tf_op jit(solution)/shard_map/ppermute | solution.py:46
  65.6 1.5 %collective-permute-start.11 = (f16[2,192,512]{2,1,0:T(8,128)(2,1)S(1)}, f16[2,192,512]{2,1,0:T(8,128)(2,1)S(1)}, u32[]{:S(2)}, u32[]{:S(2)}) collective-permute-start(f16[2,192,512]{2,1,0:T(8,128)(2,1)S(1)} %get-tuple-element.54), channel_id=1, source_target_pairs={{0,16},{16,32},{32,48},{48,0},{1,17},{17,33},{33,49},{49,1},{2,18}... | collective-permute-start | bytes 1179656 | tf_op jit(solution)/shard_map/ppermute | solution.py:38
  67.1 1.7 %collective-permute-start.10 = (f16[2,192,512]{2,1,0:T(8,128)(2,1)S(1)}, f16[2,192,512]{2,1,0:T(8,128)(2,1)S(1)}, u32[]{:S(2)}, u32[]{:S(2)}) collective-permute-start(f16[2,192,512]{2,1,0:T(8,128)(2,1)S(1)} %get-tuple-element.55), channel_id=1, source_target_pairs={{0,48},{16,0},{32,16},{48,32},{1,49},{17,1},{33,17},{49,33},{2,50}... | collective-permute-start | bytes 1179656 | tf_op jit(solution)/shard_map/ppermute | solution.py:38
  68.8 1.3 collective-permute-done.13
  70.2 0.6 collective-permute-start.14
  70.7 4.1 %collective-permute-done.14 = f32[160,128]{1,0:T(8,128)S(1)} collective-permute-done((f32[160,128]{1,0:T(8,128)S(1)}, f32[160,128]{1,0:T(8,128)S(1)}, u32[]{:S(2)}, u32[]{:S(2)}) %collective-permute-start.14) | collective-permute-done | bytes 81952 | tf_op jit(solution)/shard_map/ppermute | solution.py:46
  74.9 2.8 %collective-permute-done.11 = f16[2,192,512]{2,1,0:T(8,128)(2,1)S(1)} collective-permute-done((f16[2,192,512]{2,1,0:T(8,128)(2,1)S(1)}, f16[2,192,512]{2,1,0:T(8,128)(2,1)S(1)}, u32[]{:S(2)}, u32[]{:S(2)}) %collective-permute-start.11) | collective-permute-done | bytes 393248 | tf_op jit(solution)/shard_map/ppermute | solution.py:38
  77.7 10.3 %direct.1 = (f32[4,2,192,512]{3,2,1,0:T(8,128)}, f32[4,2,192,512]{3,2,1,0:T(8,128)}) custom-call(bf16[1536,3072]{1,0:T(8,128)(2,1)} %bitcast.62, bf16[2,192,512]{2,1,0:T(8,128)(2,1)} %copy-done.3, bf16[2,192,512]{2,1,0:T(8,128)(2,1)} %copy-done.10, bf16[2,192,512]{2,1,0:T(8,128)(2,1)} %copy-done.9, bf16[2,192,512]{2,1,0:T(8,128)(2,1)} %copy-done.8), custom_call_target="tpu_custom_call" | custom-call | flops 14000000000 | bytes 17000000 | tf_op jit(solution)/shard_map/direct/pallas_call | solution.py:170
  88.2 2.8 %collective-permute-start.9 = (f16[2,192,512]{2,1,0:T(8,128)(2,1)S(1)}, f16[2,192,512]{2,1,0:T(8,128)(2,1)S(1)}, u32[]{:S(2)}, u32[]{:S(2)}) collective-permute-start(f16[2,192,512]{2,1,0:T(8,128)(2,1)S(1)} %get-tuple-element.56), channel_id=1, source_target_pairs={{0,32},{16,48},{32,0},{48,16},{1,33},{17,49},{33,1},{49,17},{2,34}... | collective-permute-start | bytes 1179656 | tf_op jit(solution)/shard_map/ppermute | solution.py:38
  91.0 4.5 %collective-permute-done.16 = f32[160,128]{1,0:T(8,128)S(1)} collective-permute-done((f32[160,128]{1,0:T(8,128)S(1)}, f32[160,128]{1,0:T(8,128)S(1)}, u32[]{:S(2)}, u32[]{:S(2)}) %collective-permute-start.16) | collective-permute-done | bytes 81952 | tf_op jit(solution)/shard_map/ppermute | solution.py:46
  95.5 5.1 %collective-permute-start.17 = (f32[160,128]{1,0:T(8,128)S(1)}, f32[160,128]{1,0:T(8,128)S(1)}, u32[]{:S(2)}, u32[]{:S(2)}) collective-permute-start(f32[160,128]{1,0:T(8,128)S(1)} %add.88), channel_id=1, source_target_pairs={{0,6},{2,4},{4,2},{6,0},{1,7},{3,5},{5,3},{7,1},{8,14},{10,12},{12... | collective-permute-start | bytes 245768 | tf_op jit(solution)/shard_map/ppermute | solution.py:46
  100.5 0.7 collective-permute-done.9
  101.2 1.3 bitcast_add_fusion
  102.5 0.4 collective-permute-done.17
  103.0 0.8 fusion.3
  103.9 4.6 %collective-permute-start.19 = (f16[2,192,512]{2,1,0:T(8,128)(2,1)S(1)}, f16[2,192,512]{2,1,0:T(8,128)(2,1)S(1)}, u32[]{:S(2)}, u32[]{:S(2)}) collective-permute-start(f16[2,192,512]{2,1,0:T(8,128)(2,1)S(1)} %get-tuple-element.52), channel_id=1, source_target_pairs={{0,6},{2,0},{4,2},{6,4},{1,7},{3,1},{5,3},{7,5},{8,14},{10,8},{12,... | collective-permute-start | bytes 1179656 | tf_op jit(solution)/shard_map/ppermute | solution.py:38
  108.7 1.6 %collective-permute-start.21 = (f32[160,128]{1,0:T(8,128)S(1)}, f32[160,128]{1,0:T(8,128)S(1)}, u32[]{:S(2)}, u32[]{:S(2)}) collective-permute-start(f32[160,128]{1,0:T(8,128)S(1)} %add.89), channel_id=1, source_target_pairs={{0,16},{16,0},{32,48},{48,32},{1,17},{17,1},{33,49},{49,33},{2,18}... | collective-permute-start | bytes 245768 | tf_op jit(solution)/shard_map/ppermute | solution.py:46
  110.3 3.0 %collective-permute-done.21 = f32[160,128]{1,0:T(8,128)S(1)} collective-permute-done((f32[160,128]{1,0:T(8,128)S(1)}, f32[160,128]{1,0:T(8,128)S(1)}, u32[]{:S(2)}, u32[]{:S(2)}) %collective-permute-start.21) | collective-permute-done | bytes 81952 | tf_op jit(solution)/shard_map/ppermute | solution.py:46
  113.2 3.0 %collective-permute-start.22 = (f32[160,128]{1,0:T(8,128)S(1)}, f32[160,128]{1,0:T(8,128)S(1)}, u32[]{:S(2)}, u32[]{:S(2)}) collective-permute-start(f32[160,128]{1,0:T(8,128)S(1)} %add.98), channel_id=1, source_target_pairs={{0,48},{16,32},{32,16},{48,0},{1,49},{17,33},{33,17},{49,1},{2,50}... | collective-permute-start | bytes 245768 | tf_op jit(solution)/shard_map/ppermute | solution.py:46
  116.2 2.7 %collective-permute-done.22 = f32[160,128]{1,0:T(8,128)S(1)} collective-permute-done((f32[160,128]{1,0:T(8,128)S(1)}, f32[160,128]{1,0:T(8,128)S(1)}, u32[]{:S(2)}, u32[]{:S(2)}) %collective-permute-start.22) | collective-permute-done | bytes 81952 | tf_op jit(solution)/shard_map/ppermute | solution.py:46
  119.0 1.8 %collective-permute-start.23 = (f32[160,128]{1,0:T(8,128)S(1)}, f32[160,128]{1,0:T(8,128)S(1)}, u32[]{:S(2)}, u32[]{:S(2)}) collective-permute-start(f32[160,128]{1,0:T(8,128)S(1)} %add.99), channel_id=1, source_target_pairs={{0,72},{8,64},{64,8},{72,0},{1,73},{9,65},{65,9},{73,1},{2,74},{10... | collective-permute-start | bytes 245768 | tf_op jit(solution)/shard_map/ppermute | solution.py:46
  120.8 1.4 collective-permute-start.18
  122.2 1.3 collective-permute-done.23
  123.6 2.9 %collective-permute-start.25 = (f32[2,160,128]{2,1,0:T(8,128)S(1)}, f32[2,160,128]{2,1,0:T(8,128)S(1)}, u32[]{:S(2)}, u32[]{:S(2)}) collective-permute-start(f32[2,160,128]{2,1,0:T(8,128)S(1)} %pad_maximum_fusion.3), channel_id=1, source_target_pairs={{0,8},{8,0},{64,72},{72,64},{1,9},{9,1},{65,73},{73,65},{2,10},{10... | collective-permute-start | bytes 491528 | tf_op jit(solution)/shard_map/ppermute | solution.py:46
  126.4 3.3 %collective-permute-done.25 = f32[2,160,128]{2,1,0:T(8,128)S(1)} collective-permute-done((f32[2,160,128]{2,1,0:T(8,128)S(1)}, f32[2,160,128]{2,1,0:T(8,128)S(1)}, u32[]{:S(2)}, u32[]{:S(2)}) %collective-permute-start.25) | collective-permute-done | bytes 163872 | tf_op jit(solution)/shard_map/ppermute | solution.py:46
  130.3 1.1 fusion.6
  131.3 3.0 %collective-permute-start.27 = (f32[192,512]{1,0:T(8,128)S(1)}, f32[192,512]{1,0:T(8,128)S(1)}, u32[]{:S(2)}, u32[]{:S(2)}) collective-permute-start(f32[192,512]{1,0:T(8,128)S(1)} %get-tuple-element.57), channel_id=1, source_target_pairs={{0,8},{8,0},{1,9},{9,1},{2,10},{10,2},{3,11},{11,3},{4,12},{12,4},... | collective-permute-start | bytes 1179656 | tf_op jit(solution)/shard_map/ppermute | solution.py:38
  134.4 0.7 copy-done.13
  135.1 8.1 %tail.1 = f32[512,512]{1,0:T(8,128)} custom-call(f32[4,160,128]{2,1,0:T(8,128)} %copy-done.6, f32[4,160,128]{2,1,0:T(8,128)} %copy-done.13, f32[512,512]{1,0:T(8,128)} %l_ref.5, f32[4,128,128]{2,1,0:T(8,128)} %get-tuple-element.26.inv_ref, f32[512,512]{1,0:T(8,128)} %dg_ref.1), custom_call_target="tpu_custom_call" | custom-call | flops 8000000000 | bytes 5000000 | tf_op jit(solution)/shard_map/tail/pallas_call | solution.py:376
  143.2 0.7 copy-done.12
  144.0 3.5 %solve.1 = f32[192,512]{1,0:T(8,128)} custom-call(f32[192,512]{1,0:T(8,128)} %get-tuple-element.49.r_ref, f32[192,512]{1,0:T(8,128)} %copy-done.12, f32[192,512]{1,0:T(8,128)} %copy-done.11, f32[512,512]{1,0:T(8,128)} %l_ref.5, f32[4,128,128]{2,1,0:T(8,128)} %get-tuple-element.26.inv_ref), custom_call_target="tpu_custom_call" | custom-call | flops 1000000000 | bytes 3000000 | tf_op jit(solution)/shard_map/solve/pallas_call | solution.py:398
  (61 shorter events, 2.0 us)
Async XLA Ops:
  0.6 12.2 %copy-start.5 = (bf16[192,512]{1,0:T(8,128)(2,1)S(1)}, bf16[192,512]{1,0:T(8,128)(2,1)}, u32[]{:S(2)}) copy-start(bf16[192,512]{1,0:T(8,128)(2,1)} %p_ref.1) | copy-start | bytes 589828
  0.6 12.2 %collective-permute-start = (bf16[192,512]{1,0:T(8,128)(2,1)}, bf16[192,512]{1,0:T(8,128)(2,1)S(1)}, u32[]{:S(2)}, u32[]{:S(2)}) collective-permute-start(bf16[192,512]{1,0:T(8,128)(2,1)} %p_ref.1), channel_id=1, source_target_pairs={{0,8},{8,0},{1,9},{9,1},{2,10},{10,2},{3,11},{11,3},{4,12},{12,4},... | collective-permute-start | bytes 589832 | tf_op jit(solution)/shard_map/ppermute | solution.py:38
  1.1 11.7 %collective-permute-start.4 = (bf16[192,512]{1,0:T(8,128)(2,1)}, bf16[192,512]{1,0:T(8,128)(2,1)S(1)}, u32[]{:S(2)}, u32[]{:S(2)}) collective-permute-start(bf16[192,512]{1,0:T(8,128)(2,1)} %p_ref.1), channel_id=1, source_target_pairs={{0,64},{64,0},{1,65},{65,1},{2,66},{66,2},{3,67},{67,3},{4,68},{68... | collective-permute-start | bytes 589832 | tf_op jit(solution)/shard_map/ppermute | solution.py:38
  12.9 33.8 %copy-start.3 = (bf16[2,192,512]{2,1,0:T(8,128)(2,1)}, bf16[2,192,512]{2,1,0:T(8,128)(2,1)S(1)}, u32[]{:S(2)}) copy-start(bf16[2,192,512]{2,1,0:T(8,128)(2,1)S(1)} %get-tuple-element.40.x_two) | copy-start | bytes 1179652
  12.9 20.0 %collective-permute-start.2 = (bf16[2,192,512]{2,1,0:T(8,128)(2,1)S(1)}, bf16[2,192,512]{2,1,0:T(8,128)(2,1)S(1)}, u32[]{:S(2)}, u32[]{:S(2)}) collective-permute-start(bf16[2,192,512]{2,1,0:T(8,128)(2,1)S(1)} %get-tuple-element.60), channel_id=1, source_target_pairs={{0,6},{2,0},{4,2},{6,4},{1,7},{3,1},{5,3},{7,5},{8,14},{10,8},{12,... | collective-permute-start | bytes 1179656 | tf_op jit(solution)/shard_map/ppermute | solution.py:38
  17.0 19.0 %collective-permute-start.1 = (bf16[2,192,512]{2,1,0:T(8,128)(2,1)S(1)}, bf16[2,192,512]{2,1,0:T(8,128)(2,1)S(1)}, u32[]{:S(2)}, u32[]{:S(2)}) collective-permute-start(bf16[2,192,512]{2,1,0:T(8,128)(2,1)S(1)} %get-tuple-element.60), channel_id=1, source_target_pairs={{0,4},{2,6},{4,0},{6,2},{1,5},{3,7},{5,1},{7,3},{8,12},{10,14},{12... | collective-permute-start | bytes 1179656 | tf_op jit(solution)/shard_map/ppermute | solution.py:38
  17.0 19.3 %collective-permute-start.3 = (bf16[2,192,512]{2,1,0:T(8,128)(2,1)S(1)}, bf16[2,192,512]{2,1,0:T(8,128)(2,1)S(1)}, u32[]{:S(2)}, u32[]{:S(2)}) collective-permute-start(bf16[2,192,512]{2,1,0:T(8,128)(2,1)S(1)} %get-tuple-element.60), channel_id=1, source_target_pairs={{0,2},{2,4},{4,6},{6,0},{1,3},{3,5},{5,7},{7,1},{8,10},{10,12},{12... | collective-permute-start | bytes 1179656 | tf_op jit(solution)/shard_map/ppermute | solution.py:38
  18.3 18.1 %collective-permute-start.7 = (bf16[2,192,512]{2,1,0:T(8,128)(2,1)S(1)}, bf16[2,192,512]{2,1,0:T(8,128)(2,1)S(1)}, u32[]{:S(2)}, u32[]{:S(2)}) collective-permute-start(bf16[2,192,512]{2,1,0:T(8,128)(2,1)S(1)} %get-tuple-element.40.x_two), channel_id=1, source_target_pairs={{0,16},{16,32},{32,48},{48,0},{1,17},{17,33},{33,49},{49,1},{2,18}... | collective-permute-start | bytes 1179656 | tf_op jit(solution)/shard_map/ppermute | solution.py:38
  19.8 16.6 %collective-permute-start.6 = (bf16[2,192,512]{2,1,0:T(8,128)(2,1)S(1)}, bf16[2,192,512]{2,1,0:T(8,128)(2,1)S(1)}, u32[]{:S(2)}, u32[]{:S(2)}) collective-permute-start(bf16[2,192,512]{2,1,0:T(8,128)(2,1)S(1)} %get-tuple-element.40.x_two), channel_id=1, source_target_pairs={{0,48},{16,0},{32,16},{48,32},{1,49},{17,1},{33,17},{49,33},{2,50}... | collective-permute-start | bytes 1179656 | tf_op jit(solution)/shard_map/ppermute | solution.py:38
  32.9 9.3 %collective-permute-start.5 = (bf16[2,192,512]{2,1,0:T(8,128)(2,1)S(1)}, bf16[2,192,512]{2,1,0:T(8,128)(2,1)S(1)}, u32[]{:S(2)}, u32[]{:S(2)}) collective-permute-start(bf16[2,192,512]{2,1,0:T(8,128)(2,1)S(1)} %get-tuple-element.40.x_two), channel_id=1, source_target_pairs={{0,32},{16,48},{32,0},{48,16},{1,33},{17,49},{33,1},{49,17},{2,34}... | collective-permute-start | bytes 1179656 | tf_op jit(solution)/shard_map/ppermute | solution.py:38
  36.4 10.3 %copy-start.8 = (bf16[2,192,512]{2,1,0:T(8,128)(2,1)}, bf16[2,192,512]{2,1,0:T(8,128)(2,1)S(1)}, u32[]{:S(2)}) copy-start(bf16[2,192,512]{2,1,0:T(8,128)(2,1)S(1)} %collective-permute-done.7.r1) | copy-start | bytes 1179652
  36.4 5.9 %copy-start.9 = (bf16[2,192,512]{2,1,0:T(8,128)(2,1)}, bf16[2,192,512]{2,1,0:T(8,128)(2,1)S(1)}, u32[]{:S(2)}) copy-start(bf16[2,192,512]{2,1,0:T(8,128)(2,1)S(1)} %collective-permute-done.6.r3) | copy-start | bytes 1179652
  42.2 0.7 copy-start.10
  43.2 3.5 %copy-start.1 = (bf16[4,2,192,512]{3,2,1,0:T(8,128)(2,1)}, bf16[4,2,192,512]{3,2,1,0:T(8,128)(2,1)S(1)}, u32[]{:S(2)}) copy-start(bf16[4,2,192,512]{3,2,1,0:T(8,128)(2,1)S(1)} %pad_maximum_fusion.z_all) | copy-start | bytes 4718596
  43.2 3.5 %collective-permute-start.8 = (bf16[4,2,192,512]{3,2,1,0:T(8,128)(2,1)S(1)}, bf16[4,2,192,512]{3,2,1,0:T(8,128)(2,1)S(1)}, u32[]{:S(2)}, u32[]{:S(2)}) collective-permute-start(bf16[4,2,192,512]{3,2,1,0:T(8,128)(2,1)S(1)} %pad_maximum_fusion.z_all), channel_id=1, source_target_pairs={{0,1},{1,0},{2,3},{3,2},{4,5},{5,4},{6,7},{7,6},{8,9},{9,8},{10,11... | collective-permute-start | bytes 4718600 | tf_op jit(solution)/shard_map/ppermute | solution.py:38
  46.7 1.2 copy-start.7
  59.9 2.0 %copy-start.14 = (f32[4,160,128]{2,1,0:T(8,128)S(1)}, f32[4,160,128]{2,1,0:T(8,128)}, u32[]{:S(2)}) copy-start(f32[4,160,128]{2,1,0:T(8,128)} %get-tuple-element.39) | copy-start | bytes 983044
  59.9 3.7 %copy-start.4 = (f32[4,160,128]{2,1,0:T(8,128)S(1)}, f32[4,160,128]{2,1,0:T(8,128)}, u32[]{:S(2)}) copy-start(f32[4,160,128]{2,1,0:T(8,128)} %get-tuple-element.37) | copy-start | bytes 983044
  61.9 1.7 %collective-permute-start.12 = (f32[4,160,128]{2,1,0:T(8,128)S(1)}, f32[4,160,128]{2,1,0:T(8,128)S(1)}, u32[]{:S(2)}, u32[]{:S(2)}) collective-permute-start(f32[4,160,128]{2,1,0:T(8,128)S(1)} %copy-done.14), channel_id=1, source_target_pairs={{0,1},{1,0},{2,3},{3,2},{4,5},{5,4},{6,7},{7,6},{8,9},{9,8},{10,11... | collective-permute-start | bytes 983048 | tf_op jit(solution)/shard_map/ppermute | solution.py:38
  63.6 6.5 %collective-permute-start.13 = (f32[2,160,128]{2,1,0:T(8,128)S(1)}, f32[2,160,128]{2,1,0:T(8,128)S(1)}, u32[]{:S(2)}, u32[]{:S(2)}) collective-permute-start(f32[2,160,128]{2,1,0:T(8,128)S(1)} %slice_add_fusion.1), channel_id=1, source_target_pairs={{0,8},{8,0},{64,72},{72,64},{1,9},{9,1},{65,73},{73,65},{2,10},{10... | collective-permute-start | bytes 491528 | tf_op jit(solution)/shard_map/ppermute | solution.py:46
  65.6 12.1 %collective-permute-start.11 = (f16[2,192,512]{2,1,0:T(8,128)(2,1)S(1)}, f16[2,192,512]{2,1,0:T(8,128)(2,1)S(1)}, u32[]{:S(2)}, u32[]{:S(2)}) collective-permute-start(f16[2,192,512]{2,1,0:T(8,128)(2,1)S(1)} %get-tuple-element.54), channel_id=1, source_target_pairs={{0,16},{16,32},{32,48},{48,0},{1,17},{17,33},{33,49},{49,1},{2,18}... | collective-permute-start | bytes 1179656 | tf_op jit(solution)/shard_map/ppermute | solution.py:38
  67.1 10.6 %collective-permute-start.10 = (f16[2,192,512]{2,1,0:T(8,128)(2,1)S(1)}, f16[2,192,512]{2,1,0:T(8,128)(2,1)S(1)}, u32[]{:S(2)}, u32[]{:S(2)}) collective-permute-start(f16[2,192,512]{2,1,0:T(8,128)(2,1)S(1)} %get-tuple-element.55), channel_id=1, source_target_pairs={{0,48},{16,0},{32,16},{48,32},{1,49},{17,1},{33,17},{49,33},{2,50}... | collective-permute-start | bytes 1179656 | tf_op jit(solution)/shard_map/ppermute | solution.py:38
  70.2 4.7 %collective-permute-start.14 = (f32[160,128]{1,0:T(8,128)S(1)}, f32[160,128]{1,0:T(8,128)S(1)}, u32[]{:S(2)}, u32[]{:S(2)}) collective-permute-start(f32[160,128]{1,0:T(8,128)S(1)} %slice_bitcast_fusion.4), channel_id=1, source_target_pairs={{0,72},{8,64},{64,8},{72,0},{1,73},{9,65},{65,9},{73,1},{2,74},{10... | collective-permute-start | bytes 245768 | tf_op jit(solution)/shard_map/ppermute | solution.py:46
  88.1 14.9 %copy-start = (f32[4,2,192,512]{3,2,1,0:T(8,128)S(1)}, f32[4,2,192,512]{3,2,1,0:T(8,128)}, u32[]{:S(2)}) copy-start(f32[4,2,192,512]{3,2,1,0:T(8,128)} %get-tuple-element.41) | copy-start | bytes 9437188
  88.1 14.9 %collective-permute-start.15 = (f32[4,2,192,512]{3,2,1,0:T(8,128)}, f32[4,2,192,512]{3,2,1,0:T(8,128)S(1)}, u32[]{:S(2)}, u32[]{:S(2)}) collective-permute-start(f32[4,2,192,512]{3,2,1,0:T(8,128)} %get-tuple-element.42), channel_id=1, source_target_pairs={{0,1},{1,0},{2,3},{3,2},{4,5},{5,4},{6,7},{7,6},{8,9},{9,8},{10,11... | collective-permute-start | bytes 9437192 | tf_op jit(solution)/shard_map/ppermute | solution.py:38
  88.2 13.0 %collective-permute-start.9 = (f16[2,192,512]{2,1,0:T(8,128)(2,1)S(1)}, f16[2,192,512]{2,1,0:T(8,128)(2,1)S(1)}, u32[]{:S(2)}, u32[]{:S(2)}) collective-permute-start(f16[2,192,512]{2,1,0:T(8,128)(2,1)S(1)} %get-tuple-element.56), channel_id=1, source_target_pairs={{0,32},{16,48},{32,0},{48,16},{1,33},{17,49},{33,1},{49,17},{2,34}... | collective-permute-start | bytes 1179656 | tf_op jit(solution)/shard_map/ppermute | solution.py:38
  91.0 4.5 %collective-permute-start.16 = (f32[160,128]{1,0:T(8,128)S(1)}, f32[160,128]{1,0:T(8,128)S(1)}, u32[]{:S(2)}, u32[]{:S(2)}) collective-permute-start(f32[160,128]{1,0:T(8,128)S(1)} %fusion.11), channel_id=1, source_target_pairs={{0,2},{2,0},{4,6},{6,4},{1,3},{3,1},{5,7},{7,5},{8,10},{10,8},{12,... | collective-permute-start | bytes 245768 | tf_op jit(solution)/shard_map/ppermute | solution.py:46
  95.5 7.5 %collective-permute-start.17 = (f32[160,128]{1,0:T(8,128)S(1)}, f32[160,128]{1,0:T(8,128)S(1)}, u32[]{:S(2)}, u32[]{:S(2)}) collective-permute-start(f32[160,128]{1,0:T(8,128)S(1)} %add.88), channel_id=1, source_target_pairs={{0,6},{2,4},{4,2},{6,0},{1,7},{3,5},{5,3},{7,1},{8,14},{10,12},{12... | collective-permute-start | bytes 245768 | tf_op jit(solution)/shard_map/ppermute | solution.py:46
  103.0 27.3 %copy-start.2 = (f32[192,512]{1,0:T(8,128)S(1)}, f32[192,512]{1,0:T(8,128)}, u32[]{:S(2)}) copy-start(f32[192,512]{1,0:T(8,128)} %pg_ref.1) | copy-start | bytes 1179652
  103.8 15.1 %collective-permute-start.20 = (f16[2,192,512]{2,1,0:T(8,128)(2,1)S(1)}, f16[2,192,512]{2,1,0:T(8,128)(2,1)S(1)}, u32[]{:S(2)}, u32[]{:S(2)}) collective-permute-start(f16[2,192,512]{2,1,0:T(8,128)(2,1)S(1)} %get-tuple-element.51), channel_id=1, source_target_pairs={{0,2},{2,4},{4,6},{6,0},{1,3},{3,5},{5,7},{7,1},{8,10},{10,12},{12... | collective-permute-start | bytes 1179656 | tf_op jit(solution)/shard_map/ppermute | solution.py:38
  103.9 15.1 %collective-permute-start.19 = (f16[2,192,512]{2,1,0:T(8,128)(2,1)S(1)}, f16[2,192,512]{2,1,0:T(8,128)(2,1)S(1)}, u32[]{:S(2)}, u32[]{:S(2)}) collective-permute-start(f16[2,192,512]{2,1,0:T(8,128)(2,1)S(1)} %get-tuple-element.52), channel_id=1, source_target_pairs={{0,6},{2,0},{4,2},{6,4},{1,7},{3,1},{5,3},{7,5},{8,14},{10,8},{12,... | collective-permute-start | bytes 1179656 | tf_op jit(solution)/shard_map/ppermute | solution.py:38
  108.6 14.9 %collective-permute-start.24 = (f32[192,512]{1,0:T(8,128)S(1)}, f32[192,512]{1,0:T(8,128)S(1)}, u32[]{:S(2)}, u32[]{:S(2)}) collective-permute-start(f32[192,512]{1,0:T(8,128)S(1)} %slice_bitcast_fusion.1), channel_id=1, source_target_pairs={{0,64},{64,0},{1,65},{65,1},{2,66},{66,2},{3,67},{67,3},{4,68},{68... | collective-permute-start | bytes 1179656 | tf_op jit(solution)/shard_map/ppermute | solution.py:38
  108.7 4.5 %collective-permute-start.21 = (f32[160,128]{1,0:T(8,128)S(1)}, f32[160,128]{1,0:T(8,128)S(1)}, u32[]{:S(2)}, u32[]{:S(2)}) collective-permute-start(f32[160,128]{1,0:T(8,128)S(1)} %add.89), channel_id=1, source_target_pairs={{0,16},{16,0},{32,48},{48,32},{1,17},{17,1},{33,49},{49,33},{2,18}... | collective-permute-start | bytes 245768 | tf_op jit(solution)/shard_map/ppermute | solution.py:46
  113.2 5.7 %collective-permute-start.22 = (f32[160,128]{1,0:T(8,128)S(1)}, f32[160,128]{1,0:T(8,128)S(1)}, u32[]{:S(2)}, u32[]{:S(2)}) collective-permute-start(f32[160,128]{1,0:T(8,128)S(1)} %add.98), channel_id=1, source_target_pairs={{0,48},{16,32},{32,16},{48,0},{1,49},{17,33},{33,17},{49,1},{2,50}... | collective-permute-start | bytes 245768 | tf_op jit(solution)/shard_map/ppermute | solution.py:46
  119.0 4.5 %collective-permute-start.23 = (f32[160,128]{1,0:T(8,128)S(1)}, f32[160,128]{1,0:T(8,128)S(1)}, u32[]{:S(2)}, u32[]{:S(2)}) collective-permute-start(f32[160,128]{1,0:T(8,128)S(1)} %add.99), channel_id=1, source_target_pairs={{0,72},{8,64},{64,8},{72,0},{1,73},{9,65},{65,9},{73,1},{2,74},{10... | collective-permute-start | bytes 245768 | tf_op jit(solution)/shard_map/ppermute | solution.py:46
  120.8 9.5 %collective-permute-start.18 = (f16[2,192,512]{2,1,0:T(8,128)(2,1)S(1)}, f16[2,192,512]{2,1,0:T(8,128)(2,1)S(1)}, u32[]{:S(2)}, u32[]{:S(2)}) collective-permute-start(f16[2,192,512]{2,1,0:T(8,128)(2,1)S(1)} %get-tuple-element.50), channel_id=1, source_target_pairs={{0,4},{2,6},{4,0},{6,2},{1,5},{3,7},{5,1},{7,3},{8,12},{10,14},{12... | collective-permute-start | bytes 1179656 | tf_op jit(solution)/shard_map/ppermute | solution.py:38
  123.5 19.7 %copy-start.11 = (f32[192,512]{1,0:T(8,128)}, f32[192,512]{1,0:T(8,128)S(1)}, u32[]{:S(2)}) copy-start(f32[192,512]{1,0:T(8,128)S(1)} %collective-permute-done.24.t_ref) | copy-start | bytes 1179652
  123.6 6.2 %collective-permute-start.25 = (f32[2,160,128]{2,1,0:T(8,128)S(1)}, f32[2,160,128]{2,1,0:T(8,128)S(1)}, u32[]{:S(2)}, u32[]{:S(2)}) collective-permute-start(f32[2,160,128]{2,1,0:T(8,128)S(1)} %pad_maximum_fusion.3), channel_id=1, source_target_pairs={{0,8},{8,0},{64,72},{72,64},{1,9},{9,1},{65,73},{73,65},{2,10},{10... | collective-permute-start | bytes 491528 | tf_op jit(solution)/shard_map/ppermute | solution.py:46
  129.7 4.6 %copy-start.6 = (f32[4,160,128]{2,1,0:T(8,128)}, f32[4,160,128]{2,1,0:T(8,128)S(1)}, u32[]{:S(2)}) copy-start(f32[4,160,128]{2,1,0:T(8,128)S(1)} %constant_dynamic-update-slice_fusion.mine) | copy-start | bytes 983044
  129.8 4.6 %collective-permute-start.26 = (f32[4,160,128]{2,1,0:T(8,128)S(1)}, f32[4,160,128]{2,1,0:T(8,128)S(1)}, u32[]{:S(2)}, u32[]{:S(2)}) collective-permute-start(f32[4,160,128]{2,1,0:T(8,128)S(1)} %constant_dynamic-update-slice_fusion.mine), channel_id=1, source_target_pairs={{0,1},{1,0},{2,3},{3,2},{4,5},{5,4},{6,7},{7,6},{8,9},{9,8},{10,11... | collective-permute-start | bytes 983048 | tf_op jit(solution)/shard_map/ppermute | solution.py:38
  131.3 11.9 %collective-permute-start.27 = (f32[192,512]{1,0:T(8,128)S(1)}, f32[192,512]{1,0:T(8,128)S(1)}, u32[]{:S(2)}, u32[]{:S(2)}) collective-permute-start(f32[192,512]{1,0:T(8,128)S(1)} %get-tuple-element.57), channel_id=1, source_target_pairs={{0,8},{8,0},{1,9},{9,1},{2,10},{10,2},{3,11},{11,3},{4,12},{12,4},... | collective-permute-start | bytes 1179656 | tf_op jit(solution)/shard_map/ppermute | solution.py:38
  134.4 0.7 copy-start.13
  143.2 0.7 copy-start.12

commit v5 on v4

--- a/solution.py
+++ b/solution.py
@@ -62,7 +62,12 @@
     return ref[i * BLK : (i + 1) * BLK, j * BLK : (j + 1) * BLK]
 
 
-def prep_kernel(l_ref, pg_ref, p_ref, inv_ref, g_ref):
+def split(a):
+    hi = a.astype(bf16)
+    return hi, (a - hi.astype(f32)).astype(bf16)
+
+
+def prep_kernel(l_ref, pg_ref, p_ref, step_n, step_t, low_t, g_ref):
     rows, cols = iotas(BLK)
     blocks = []
     inv = []
@@ -76,8 +81,13 @@
         right = [hi_dot(jnp.where(sel, blocks[b], 0.0), inv[b], ((1,), (0,))) for b in range(NB)]
         inv = [inv[b] - hi_dot(inv[b], right[b], ((1,), (0,))) for b in range(NB)]
         s *= 2
-    for b in range(NB):
-        inv_ref[b] = inv[b]
+    for i, j in LOWER:
+        m = blocks[i] if i == j else block(l_ref, i, j)
+        v = inv[i] if i == j else hi_dot(inv[i], m, ((1,), (0,)))
+        at_i, at_j = slice(i * BLK, (i + 1) * BLK), slice(j * BLK, (j + 1) * BLK)
+        step_n[0, at_i, at_j], step_n[1, at_i, at_j] = split(v)
+        step_t[0, at_j, at_i], step_t[1, at_j, at_i] = split(v.T)
+        low_t[0, at_j, at_i], low_t[1, at_j, at_i] = split(m.T)
     p = p_ref[...]
     g = pg_ref[...]
     total = None
@@ -93,11 +103,13 @@
     return pl.pallas_call(
         prep_kernel,
         out_shape=(
-            jax.ShapeDtypeStruct((NB, BLK, BLK), f32),
+            jax.ShapeDtypeStruct((2, B, B), bf16),
+            jax.ShapeDtypeStruct((2, B, B), bf16),
+            jax.ShapeDtypeStruct((2, B, B), bf16),
             jax.ShapeDtypeStruct((B, B), f32),
         ),
         in_specs=[whole()] * 3,
-        out_specs=(whole(), whole()),
+        out_specs=(whole(),) * 4,
         compiler_params=params(),
         cost_estimate=pl.CostEstimate(flops=4_000_000_000, bytes_accessed=3_000_000, transcendentals=0),
         name="prep",
@@ -292,15 +304,14 @@
     )(flip, z_all, p_all, x_two, *xr, g, *after)
 
 
-def split(a):
-    hi = a.astype(bf16)
-    return hi, (a - hi.astype(f32)).astype(bf16)
-
-
 def cat(parts, axis):
     return parts[0] if len(parts) == 1 else jnp.concatenate(parts, axis=axis)
 
 
+def halves(ref, *at):
+    return ref[(0, *at)], ref[(1, *at)]
+
+
 def cat2(pairs, axis):
     return cat([p[0] for p in pairs], axis), cat([p[1] for p in pairs], axis)
 
@@ -309,7 +320,7 @@
     return jnp.dot(cat([a[0], a[0], a[1]], 1), cat([b[0], b[1], b[0]], 0), preferred_element_type=f32)
 
 
-def tail_kernel(mine, other, l_ref, inv_ref, dg_ref, *refs):
+def tail_kernel(mine, other, step_n, step_t, low_t, dg_ref, *refs):
     out_ref, flat = refs[-2:]
     c, y = lax.axis_index("c"), lax.axis_index("yh") * 2 + lax.axis_index("yl")
     for k, q in enumerate(chunk_order(y)):
@@ -317,23 +328,14 @@
         flat[pl.ds(pl.multiple_of(((1 - c) * 4 + q) * CH, CH), CH), :] = other[k]
     rows, cols = iotas(BLK)
     tri = rows >= cols
-    low = {ij: block(l_ref, *ij) for ij in LOWER}
-    for i in range(NB):
-        low[i, i] = jnp.where(tri, low[i, i], 0.0)
-    low_t = {ij: split(v.T) for ij, v in low.items()}
-    low_n = {ij: split(v) for ij, v in low.items()}
-    inv_n = [split(inv_ref[i]) for i in range(NB)]
-    inv_t = [split(inv_ref[i].T) for i in range(NB)]
     q = {ij: flat[n * BLK : (n + 1) * BLK, :] for n, ij in enumerate(LOWER)}
     acc = {i: cat([q[i, j] for j in range(i + 1)], 1) for i in range(NB)}
     new = {}
     for i in reversed(range(NB)):
-        con = dot3(inv_t[i], split(acc[i]))
-        if i:
-            part = tuple(v[:, : i * BLK] for v in split(con))
-            upd = dot3(cat2([low_t[i, r] for r in range(i)], 0), part)
-            for r in range(i):
-                acc[r] = acc[r] - upd[r * BLK : (r + 1) * BLK, : (r + 1) * BLK]
+        both = dot3(halves(step_t, slice(0, (i + 1) * BLK), slice(i * BLK, (i + 1) * BLK)), split(acc[i]))
+        con = both[i * BLK :]
+        for r in range(i):
+            acc[r] = acc[r] - both[r * BLK : (r + 1) * BLK, : (r + 1) * BLK]
         n = dg_ref[i * BLK : (i + 1) * BLK, : (i + 1) * BLK] - con
         corner = jnp.where(tri, n[:, i * BLK :], 0.0)
         new[i] = split(corner if i == 0 else cat([n[:, : i * BLK], corner], 1))
@@ -342,7 +344,7 @@
     for i in range(NB):
         width = (i + 1) * BLK
         r = dot3(
-            cat2([low_t[k, i] for k in range(i, NB)], 1),
+            halves(low_t, slice(i * BLK, (i + 1) * BLK), slice(i * BLK, B)),
             cat2([tuple(v[:, :width] for v in new[k]) for k in range(i, NB)], 0),
         )
         parts = [] if i == 0 else [r[:, : i * BLK]]
@@ -352,18 +354,17 @@
         inner[i] = cat(parts, 1)
     left = {}
     for i in reversed(range(NB)):
-        left[i] = dot3(inv_t[i], split(inner[i]))
-        if i:
-            upd = dot3(cat2([low_t[i, r] for r in range(i)], 0), split(left[i]))
-            for r in range(i):
-                inner[r] = inner[r] - upd[r * BLK : (r + 1) * BLK]
+        both = dot3(halves(step_t, slice(0, (i + 1) * BLK), slice(i * BLK, (i + 1) * BLK)), split(inner[i]))
+        left[i] = both[i * BLK :]
+        for r in range(i):
+            inner[r] = inner[r] - both[r * BLK : (r + 1) * BLK]
     acc = cat([left[i] for i in range(NB)], 0)
     right = {}
     for j in reversed(range(NB)):
-        right[j] = dot3(split(acc[:, j * BLK : (j + 1) * BLK]), inv_n[j])
+        both = dot3(split(acc[:, j * BLK :]), halves(step_n, slice(j * BLK, (j + 1) * BLK), slice(0, (j + 1) * BLK)))
+        right[j] = both[:, j * BLK :]
         if j:
-            upd = dot3(split(right[j]), cat2([low_n[j, r] for r in range(j)], 1))
-            acc = acc[:, : j * BLK] - upd
+            acc = acc[:, : j * BLK] - both[:, : j * BLK]
     for i in range(NB):
         for j in range(i + 1):
             v = 0.5 * (right[j][i * BLK : (i + 1) * BLK] + right[i][j * BLK : (j + 1) * BLK].T)
@@ -372,38 +373,38 @@
                 out_ref[j * BLK : (j + 1) * BLK, i * BLK : (i + 1) * BLK] = v.T
 
 
-def tail(mine, other, lower, inv, diag_grad, *after):
+def tail(mine, other, factor, diag_grad, *after):
     return pl.pallas_call(
         tail_kernel,
         out_shape=jax.ShapeDtypeStruct((B, B), f32),
-        in_specs=[whole()] * 5 + [ANY] * len(after),
+        in_specs=[whole()] * 6 + [ANY] * len(after),
         out_specs=whole(),
         scratch_shapes=[pltpu.VMEM((8 * CH, BLK), f32)],
         compiler_params=params(),
         cost_estimate=pl.CostEstimate(flops=8_000_000_000, bytes_accessed=5_000_000, transcendentals=0),
         name="tail",
-    )(mine, other, lower, inv, diag_grad, *after)
-
-
-def solve_kernel(r_ref, d_ref, t_ref, l_ref, inv_ref, out_ref):
+    )(mine, other, *factor, diag_grad, *after)
+
+
+def solve_kernel(r_ref, d_ref, t_ref, step_n, out_ref):
     acc = r_ref[...] - d_ref[...] - t_ref[...]
     for j in reversed(range(NB)):
-        x = dot3(split(acc[:, j * BLK :]), split(inv_ref[j]))
-        out_ref[:, j * BLK : (j + 1) * BLK] = x
+        both = dot3(split(acc[:, j * BLK :]), halves(step_n, slice(j * BLK, (j + 1) * BLK), slice(0, (j + 1) * BLK)))
+        out_ref[:, j * BLK : (j + 1) * BLK] = both[:, j * BLK :]
         if j:
-            acc = acc[:, : j * BLK] - dot3(split(x), split(l_ref[j * BLK : (j + 1) * BLK, : j * BLK]))
-
-
-def solve(r, d, t, lower, inv):
+            acc = acc[:, : j * BLK] - both[:, : j * BLK]
+
+
+def solve(r, d, t, step_n):
     return pl.pallas_call(
         solve_kernel,
         out_shape=jax.ShapeDtypeStruct((U, B), f32),
-        in_specs=[whole()] * 5,
+        in_specs=[whole()] * 4,
         out_specs=whole(),
         compiler_params=params(),
         cost_estimate=pl.CostEstimate(flops=1_000_000_000, bytes_accessed=3_000_000, transcendentals=0),
         name="solve",
-    )(r, d, t, lower, inv)
+    )(r, d, t, step_n)
 
 
 def on_device(trailing_grad, panel, panel_grad, diag_factor, diag_grad):
@@ -411,9 +412,10 @@
 
     x_swp = shift(panel, "yh", 1, 2)
     z_swp = shift(panel, "yl", 1, 2)
-    inv, g = prep(diag_factor, panel_grad, panel)
-    x_swp, z_swp = after(x_swp, inv), after(z_swp, inv)
-    x_two, z_two = jnp.stack([panel, x_swp]), jnp.stack([panel, z_swp])
+    *factor, g = prep(diag_factor, panel_grad, panel)
+    x_swp, z_swp = after(x_swp, g), after(z_swp, g)
+    x_two = jnp.stack([panel, x_swp])
+    z_two = jnp.stack([panel, after(z_swp, x_two)])
     z_recv = [shift(z_two, "z", k) for k in NEAR]
     x_recv = [shift(x_two, "x", k) for k in NEAR]
     z_recv, x_recv = lax.optimization_barrier((z_recv, x_recv))
@@ -455,9 +457,9 @@
         - (d_own[0] + (full(d_in[2][0]) + full(d_in[3][0]) + full(d_in[1][0])))
     )
     q_pair = after(shift(q_all, "c", 1, 2), d_far)
-    diag_adj = tail(q_all, q_pair, diag_factor, inv, diag_grad)
+    diag_adj = tail(q_all, q_pair, factor, diag_grad)
     near = after(near, diag_adj)
-    return solve(near, d_last, t_last, diag_factor, inv), diag_adj
+    return solve(near, d_last, t_last, factor[0]), diag_adj
 
 
 def solution(mesh):

time: 149 us -> 146 us (0.980)
  starting transfers between devices: 47.3 us -> 38.3 us
  waiting for transfers between devices: 49.5 us -> 55.4 us
    ppermute x8, starting transfers between devices: 16.9 us -> 12 us  [swap(): lax.ppermute(x, axis, [(i, 3 - i if far else i ^ 1) for i in range(4)])]
    ppermute x20, waiting for transfers between devices: 28.9 us -> 33.2 us  [shift(): return lax.ppermute(x, axis, [(i, (i + k) % n) for i in range(n)])]
    ppermute x20, starting transfers between devices: 30.5 us -> 26.4 us  [shift(): return lax.ppermute(x, axis, [(i, (i + k) % n) for i in range(n)])]
    ppermute x8, waiting for transfers between devices: 20.6 us -> 22.3 us  [swap(): lax.ppermute(x, axis, [(i, 3 - i if far else i ^ 1) for i in range(4)])]
  transfers between devices with their start and end apart: 28 -> 28, of which waited for: 17 -> 18; matrix products, arithmetic and copies ran while one was open for 2% -> 2% of each run, Pallas kernels for 10% -> 11%
where the time goes in v5:
time: 146 us; the launch traced here: 144 us
  waiting for transfers between devices  55.4 us (38%)
  Pallas kernels  40.7 us (28%)
  starting transfers between devices  38.3 us (26%)
  other arithmetic  5.66 us (4%)
  local copies, waits for them, and re-layouts  2.73 us (2%)
    ppermute x20, waiting for transfers between devices, shift(): return lax.ppermute(x, axis, [(i, (i + k) % n) for i in range(n)])  33.2 us
    ppermute x20, starting transfers between devices, shift(): return lax.ppermute(x, axis, [(i, (i + k) % n) for i in range(n)])  26.4 us
    ppermute x8, waiting for transfers between devices, swap(): lax.ppermute(x, axis, [(i, 3 - i if far else i ^ 1) for i in range(4)])  22.3 us
    pallas_call x1, Pallas kernels, transposed(): pl.pallas_call(transposed_kernel, in_specs=[ANY] * (8 + len(after)), out_...  12 us
    ppermute x8, starting transfers between devices, swap(): lax.ppermute(x, axis, [(i, 3 - i if far else i ^ 1) for i in range(4)])  12 us
    pallas_call x1, Pallas kernels, direct(): pl.pallas_call(direct_kernel, in_specs=[ANY] * (5 + len(after)), out_spec...  10.3 us
    pallas_call x1, Pallas kernels, prep(): pl.pallas_call(prep_kernel, out_shape=(jax.ShapeDtypeStruct((2, B, B), bf...  7.74 us
    pallas_call x1, Pallas kernels, tail(): pl.pallas_call(tail_kernel, out_shape=jax.ShapeDtypeStruct((B, B), f32),...  7.42 us
  transfers between devices with their start and end apart: 28, of which 18 were waited for; matrix products, arithmetic and copies ran while one was open for 2% of the time, Pallas kernels for 11%

profile of v5, /device:TPU:8, one launch (start us, length us, event | category | flops | bytes accessed | tf_op | source)
XLA Modules:
  0.0 143.8 jit_solution(5826996773887905216)
XLA Ops:
  0.6 2.4 %collective-permute-start.1 = (bf16[192,512]{1,0:T(8,128)(2,1)}, bf16[192,512]{1,0:T(8,128)(2,1)S(1)}, u32[]{:S(2)}, u32[]{:S(2)}) collective-permute-start(bf16[192,512]{1,0:T(8,128)(2,1)} %p_ref.1), channel_id=1, source_target_pairs={{0,64},{64,0},{1,65},{65,1},{2,66},{66,2},{3,67},{67,3},{4,68},{68... | collective-permute-start | bytes 589832 | tf_op jit(solution)/shard_map/ppermute | solution.py:38
  3.0 7.7 %prep.1 = (bf16[2,512,512]{2,1,0:T(8,128)(2,1)}, bf16[2,512,512]{2,1,0:T(8,128)(2,1)}, bf16[2,512,512]{2,1,0:T(8,128)(2,1)}, f32[512,512]{1,0:T(8,128)}) custom-call(f32[512,512]{1,0:T(8,128)} %l_ref.1, f32[192,512]{1,0:T(8,128)} %pg_ref.1, bf16[192,512]{1,0:T(8,128)(2,1)} %p_ref.1), custom_call_target="tpu_custom_call" | custom-call | flops 4000000000 | bytes 3000000 | tf_op jit(solution)/shard_map/prep/pallas_call | solution.py:103
  10.8 1.6 %collective-permute-start.7 = (bf16[2,192,512]{2,1,0:T(8,128)(2,1)S(1)}, bf16[2,192,512]{2,1,0:T(8,128)(2,1)S(1)}, u32[]{:S(2)}, u32[]{:S(2)}) collective-permute-start(bf16[2,192,512]{2,1,0:T(8,128)(2,1)S(1)} %pad_maximum_fusion.1.x_two), channel_id=1, source_target_pairs={{0,16},{16,32},{32,48},{48,0},{1,17},{17,33},{33,49},{49,1},{2,18}... | collective-permute-start | bytes 1179656 | tf_op jit(solution)/shard_map/ppermute | solution.py:38
  12.4 1.3 collective-permute-start
  13.7 1.7 %collective-permute-start.6 = (bf16[2,192,512]{2,1,0:T(8,128)(2,1)S(1)}, bf16[2,192,512]{2,1,0:T(8,128)(2,1)S(1)}, u32[]{:S(2)}, u32[]{:S(2)}) collective-permute-start(bf16[2,192,512]{2,1,0:T(8,128)(2,1)S(1)} %pad_maximum_fusion.1.x_two), channel_id=1, source_target_pairs={{0,48},{16,0},{32,16},{48,32},{1,49},{17,1},{33,17},{49,33},{2,50}... | collective-permute-start | bytes 1179656 | tf_op jit(solution)/shard_map/ppermute | solution.py:38
  15.5 1.8 %collective-permute-start.5 = (bf16[2,192,512]{2,1,0:T(8,128)(2,1)S(1)}, bf16[2,192,512]{2,1,0:T(8,128)(2,1)S(1)}, u32[]{:S(2)}, u32[]{:S(2)}) collective-permute-start(bf16[2,192,512]{2,1,0:T(8,128)(2,1)S(1)} %pad_maximum_fusion.1.x_two), channel_id=1, source_target_pairs={{0,32},{16,48},{32,0},{48,16},{1,33},{17,49},{33,1},{49,17},{2,34}... | collective-permute-start | bytes 1179656 | tf_op jit(solution)/shard_map/ppermute | solution.py:38
  17.3 1.2 collective-permute-done
  18.5 4.1 %collective-permute-start.3 = (bf16[2,192,512]{2,1,0:T(8,128)(2,1)S(1)}, bf16[2,192,512]{2,1,0:T(8,128)(2,1)S(1)}, u32[]{:S(2)}, u32[]{:S(2)}) collective-permute-start(bf16[2,192,512]{2,1,0:T(8,128)(2,1)S(1)} %get-tuple-element.66), channel_id=1, source_target_pairs={{0,6},{2,0},{4,2},{6,4},{1,7},{3,1},{5,3},{7,5},{8,14},{10,8},{12,... | collective-permute-start | bytes 1179656 | tf_op jit(solution)/shard_map/ppermute | solution.py:38
  22.6 0.5 collective-permute-done.7.r1
  23.2 1.9 %collective-permute-start.4 = (bf16[2,192,512]{2,1,0:T(8,128)(2,1)S(1)}, bf16[2,192,512]{2,1,0:T(8,128)(2,1)S(1)}, u32[]{:S(2)}, u32[]{:S(2)}) collective-permute-start(bf16[2,192,512]{2,1,0:T(8,128)(2,1)S(1)} %get-tuple-element.66), channel_id=1, source_target_pairs={{0,2},{2,4},{4,6},{6,0},{1,3},{3,5},{5,7},{7,1},{8,10},{10,12},{12... | collective-permute-start | bytes 1179656 | tf_op jit(solution)/shard_map/ppermute | solution.py:38
  25.1 0.7 collective-permute-done.6.r3
  25.8 6.3 %collective-permute-done.5.r2 = bf16[2,192,512]{2,1,0:T(8,128)(2,1)S(1)} collective-permute-done((bf16[2,192,512]{2,1,0:T(8,128)(2,1)S(1)}, bf16[2,192,512]{2,1,0:T(8,128)(2,1)S(1)}, u32[]{:S(2)}, u32[]{:S(2)}) %collective-permute-start.5) | collective-permute-done | bytes 393248 | tf_op jit(solution)/shard_map/ppermute | solution.py:38
  32.1 5.9 %collective-permute-done.3 = bf16[2,192,512]{2,1,0:T(8,128)(2,1)S(1)} collective-permute-done((bf16[2,192,512]{2,1,0:T(8,128)(2,1)S(1)}, bf16[2,192,512]{2,1,0:T(8,128)(2,1)S(1)}, u32[]{:S(2)}, u32[]{:S(2)}) %collective-permute-start.3) | collective-permute-done | bytes 393248 | tf_op jit(solution)/shard_map/ppermute | solution.py:38
  37.9 3.7 %collective-permute-done.4 = bf16[2,192,512]{2,1,0:T(8,128)(2,1)S(1)} collective-permute-done((bf16[2,192,512]{2,1,0:T(8,128)(2,1)S(1)}, bf16[2,192,512]{2,1,0:T(8,128)(2,1)S(1)}, u32[]{:S(2)}, u32[]{:S(2)}) %collective-permute-start.4) | collective-permute-done | bytes 393248 | tf_op jit(solution)/shard_map/ppermute | solution.py:38
  42.0 3.4 %collective-permute-done.8.p_all = bf16[4,2,192,512]{3,2,1,0:T(8,128)(2,1)S(1)} collective-permute-done((bf16[4,2,192,512]{3,2,1,0:T(8,128)(2,1)S(1)}, bf16[4,2,192,512]{3,2,1,0:T(8,128)(2,1)S(1)}, u32[]{:S(2)}, u32[]{:S(2)}) %collective-permute-start.8) | collective-permute-done | bytes 1572896 | tf_op jit(solution)/shard_map/ppermute | solution.py:38
  45.4 1.2 copy-done.7
  46.5 12.0 %transposed.1 = (f32[4,2,192,512]{3,2,1,0:T(8,128)}, f32[4,160,128]{2,1,0:T(8,128)}, f32[4,160,128]{2,1,0:T(8,128)}) custom-call(bf16[1536,3072]{1,0:T(8,128)(2,1)} %bitcast.62, bf16[4,2,192,512]{3,2,1,0:T(8,128)(2,1)} %copy-done.1, bf16[4,2,192,512]{3,2,1,0:T(8,128)(2,1)} %copy-done.7, bf16[2,192,512]{2,1,0:T(8,128)(2,1)} %copy-done.4, ...), custom_call_target="tpu_custom_call" | custom-call | flops 15000000512 | bytes 17000000 | tf_op jit(solution)/shard_map/transposed/pallas_call | solution.py:280
  58.6 2.0 %fusion.2 = (f16[2,192,512]{2,1,0:T(8,128)(2,1)S(1)}, f16[2,192,512]{2,1,0:T(8,128)(2,1)S(1)}, f16[2,192,512]{2,1,0:T(8,128)(2,1)S(1)}) fusion(f32[4,2,192,512]{3,2,1,0:T(8,128)} %get-tuple-element.39), kind=kLoop, calls=%fused_computation.13 | loop fusion | flops 1179648 | bytes 3538944 | tf_op jit(solution)/shard_map/convert_element_type | solution.py:425
  60.8 1.5 %collective-permute-done.12 = f32[4,160,128]{2,1,0:T(8,128)S(1)} collective-permute-done((f32[4,160,128]{2,1,0:T(8,128)S(1)}, f32[4,160,128]{2,1,0:T(8,128)S(1)}, u32[]{:S(2)}, u32[]{:S(2)}) %collective-permute-start.12) | collective-permute-done | bytes 327712 | tf_op jit(solution)/shard_map/ppermute | solution.py:38
  62.3 1.4 collective-permute-start.13
  63.8 1.5 %collective-permute-start.11 = (f16[2,192,512]{2,1,0:T(8,128)(2,1)S(1)}, f16[2,192,512]{2,1,0:T(8,128)(2,1)S(1)}, u32[]{:S(2)}, u32[]{:S(2)}) collective-permute-start(f16[2,192,512]{2,1,0:T(8,128)(2,1)S(1)} %get-tuple-element.60), channel_id=1, source_target_pairs={{0,16},{16,32},{32,48},{48,0},{1,17},{17,33},{33,49},{49,1},{2,18}... | collective-permute-start | bytes 1179656 | tf_op jit(solution)/shard_map/ppermute | solution.py:38
  65.2 1.8 %collective-permute-start.10 = (f16[2,192,512]{2,1,0:T(8,128)(2,1)S(1)}, f16[2,192,512]{2,1,0:T(8,128)(2,1)S(1)}, u32[]{:S(2)}, u32[]{:S(2)}) collective-permute-start(f16[2,192,512]{2,1,0:T(8,128)(2,1)S(1)} %get-tuple-element.61), channel_id=1, source_target_pairs={{0,48},{16,0},{32,16},{48,32},{1,49},{17,1},{33,17},{49,33},{2,50}... | collective-permute-start | bytes 1179656 | tf_op jit(solution)/shard_map/ppermute | solution.py:38
  67.0 1.6 %collective-permute-done.13 = f32[2,160,128]{2,1,0:T(8,128)S(1)} collective-permute-done((f32[2,160,128]{2,1,0:T(8,128)S(1)}, f32[2,160,128]{2,1,0:T(8,128)S(1)}, u32[]{:S(2)}, u32[]{:S(2)}) %collective-permute-start.13) | collective-permute-done | bytes 163872 | tf_op jit(solution)/shard_map/ppermute | solution.py:46
  69.0 4.2 %collective-permute-done.14 = f32[160,128]{1,0:T(8,128)S(1)} collective-permute-done((f32[160,128]{1,0:T(8,128)S(1)}, f32[160,128]{1,0:T(8,128)S(1)}, u32[]{:S(2)}, u32[]{:S(2)}) %collective-permute-start.14) | collective-permute-done | bytes 81952 | tf_op jit(solution)/shard_map/ppermute | solution.py:46
  73.2 2.6 %collective-permute-done.11 = f16[2,192,512]{2,1,0:T(8,128)(2,1)S(1)} collective-permute-done((f16[2,192,512]{2,1,0:T(8,128)(2,1)S(1)}, f16[2,192,512]{2,1,0:T(8,128)(2,1)S(1)}, u32[]{:S(2)}, u32[]{:S(2)}) %collective-permute-start.11) | collective-permute-done | bytes 393248 | tf_op jit(solution)/shard_map/ppermute | solution.py:38
  75.9 10.3 %direct.1 = (f32[4,2,192,512]{3,2,1,0:T(8,128)}, f32[4,2,192,512]{3,2,1,0:T(8,128)}) custom-call(bf16[1536,3072]{1,0:T(8,128)(2,1)} %bitcast.63, bf16[2,192,512]{2,1,0:T(8,128)(2,1)} %copy-done.4, bf16[2,192,512]{2,1,0:T(8,128)(2,1)} %copy-done.10, bf16[2,192,512]{2,1,0:T(8,128)(2,1)} %copy-done.9, bf16[2,192,512]{2,1,0:T(8,128)(2,1)} %copy-done.8), custom_call_target="tpu_custom_call" | custom-call | flops 14000000000 | bytes 17000000 | tf_op jit(solution)/shard_map/direct/pallas_call | solution.py:182
  86.3 1.8 %collective-permute-start.9 = (f16[2,192,512]{2,1,0:T(8,128)(2,1)S(1)}, f16[2,192,512]{2,1,0:T(8,128)(2,1)S(1)}, u32[]{:S(2)}, u32[]{:S(2)}) collective-permute-start(f16[2,192,512]{2,1,0:T(8,128)(2,1)S(1)} %get-tuple-element.62), channel_id=1, source_target_pairs={{0,32},{16,48},{32,0},{48,16},{1,33},{17,49},{33,1},{49,17},{2,34}... | collective-permute-start | bytes 1179656 | tf_op jit(solution)/shard_map/ppermute | solution.py:38
  88.1 4.5 %collective-permute-done.16 = f32[160,128]{1,0:T(8,128)S(1)} collective-permute-done((f32[160,128]{1,0:T(8,128)S(1)}, f32[160,128]{1,0:T(8,128)S(1)}, u32[]{:S(2)}, u32[]{:S(2)}) %collective-permute-start.16) | collective-permute-done | bytes 81952 | tf_op jit(solution)/shard_map/ppermute | solution.py:46
  92.6 0.7 collective-permute-start.17
  93.3 6.0 %collective-permute-done.9 = f16[2,192,512]{2,1,0:T(8,128)(2,1)S(1)} collective-permute-done((f16[2,192,512]{2,1,0:T(8,128)(2,1)S(1)}, f16[2,192,512]{2,1,0:T(8,128)(2,1)S(1)}, u32[]{:S(2)}, u32[]{:S(2)}) %collective-permute-start.9) | collective-permute-done | bytes 393248 | tf_op jit(solution)/shard_map/ppermute | solution.py:38
  99.3 1.3 bitcast_add_fusion
  100.8 0.8 fusion.3
  101.7 3.2 %collective-permute-start.19 = (f16[2,192,512]{2,1,0:T(8,128)(2,1)S(1)}, f16[2,192,512]{2,1,0:T(8,128)(2,1)S(1)}, u32[]{:S(2)}, u32[]{:S(2)}) collective-permute-start(f16[2,192,512]{2,1,0:T(8,128)(2,1)S(1)} %get-tuple-element.58), channel_id=1, source_target_pairs={{0,6},{2,0},{4,2},{6,4},{1,7},{3,1},{5,3},{7,5},{8,14},{10,8},{12,... | collective-permute-start | bytes 1179656 | tf_op jit(solution)/shard_map/ppermute | solution.py:38
  105.3 1.1 collective-permute-start.21
  106.5 3.3 %collective-permute-done.21 = f32[160,128]{1,0:T(8,128)S(1)} collective-permute-done((f32[160,128]{1,0:T(8,128)S(1)}, f32[160,128]{1,0:T(8,128)S(1)}, u32[]{:S(2)}, u32[]{:S(2)}) %collective-permute-start.21) | collective-permute-done | bytes 81952 | tf_op jit(solution)/shard_map/ppermute | solution.py:46
  109.8 3.0 %collective-permute-start.22 = (f32[160,128]{1,0:T(8,128)S(1)}, f32[160,128]{1,0:T(8,128)S(1)}, u32[]{:S(2)}, u32[]{:S(2)}) collective-permute-start(f32[160,128]{1,0:T(8,128)S(1)} %add.98), channel_id=1, source_target_pairs={{0,48},{16,32},{32,16},{48,0},{1,49},{17,33},{33,17},{49,1},{2,50}... | collective-permute-start | bytes 245768 | tf_op jit(solution)/shard_map/ppermute | solution.py:46
  112.8 2.7 %collective-permute-done.22 = f32[160,128]{1,0:T(8,128)S(1)} collective-permute-done((f32[160,128]{1,0:T(8,128)S(1)}, f32[160,128]{1,0:T(8,128)S(1)}, u32[]{:S(2)}, u32[]{:S(2)}) %collective-permute-start.22) | collective-permute-done | bytes 81952 | tf_op jit(solution)/shard_map/ppermute | solution.py:46
  115.5 1.9 %collective-permute-start.23 = (f32[160,128]{1,0:T(8,128)S(1)}, f32[160,128]{1,0:T(8,128)S(1)}, u32[]{:S(2)}, u32[]{:S(2)}) collective-permute-start(f32[160,128]{1,0:T(8,128)S(1)} %add.99), channel_id=1, source_target_pairs={{0,72},{8,64},{64,8},{72,0},{1,73},{9,65},{65,9},{73,1},{2,74},{10... | collective-permute-start | bytes 245768 | tf_op jit(solution)/shard_map/ppermute | solution.py:46
  117.4 2.6 %collective-permute-done.23 = f32[160,128]{1,0:T(8,128)S(1)} collective-permute-done((f32[160,128]{1,0:T(8,128)S(1)}, f32[160,128]{1,0:T(8,128)S(1)}, u32[]{:S(2)}, u32[]{:S(2)}) %collective-permute-start.23) | collective-permute-done | bytes 81952 | tf_op jit(solution)/shard_map/ppermute | solution.py:46
  120.1 3.5 %collective-permute-start.25 = (f32[2,160,128]{2,1,0:T(8,128)S(1)}, f32[2,160,128]{2,1,0:T(8,128)S(1)}, u32[]{:S(2)}, u32[]{:S(2)}) collective-permute-start(f32[2,160,128]{2,1,0:T(8,128)S(1)} %pad_maximum_fusion.3), channel_id=1, source_target_pairs={{0,8},{8,0},{64,72},{72,64},{1,9},{9,1},{65,73},{73,65},{2,10},{10... | collective-permute-start | bytes 491528 | tf_op jit(solution)/shard_map/ppermute | solution.py:46
  123.6 3.3 %collective-permute-done.25 = f32[2,160,128]{2,1,0:T(8,128)S(1)} collective-permute-done((f32[2,160,128]{2,1,0:T(8,128)S(1)}, f32[2,160,128]{2,1,0:T(8,128)S(1)}, u32[]{:S(2)}, u32[]{:S(2)}) %collective-permute-start.25) | collective-permute-done | bytes 163872 | tf_op jit(solution)/shard_map/ppermute | solution.py:46
  127.0 1.1 fusion.6
  128.1 2.3 %collective-permute-start.27 = (f32[192,512]{1,0:T(8,128)S(1)}, f32[192,512]{1,0:T(8,128)S(1)}, u32[]{:S(2)}, u32[]{:S(2)}) collective-permute-start(f32[192,512]{1,0:T(8,128)S(1)} %get-tuple-element.63), channel_id=1, source_target_pairs={{0,8},{8,0},{1,9},{9,1},{2,10},{10,2},{3,11},{11,3},{4,12},{12,4},... | collective-permute-start | bytes 1179656 | tf_op jit(solution)/shard_map/ppermute | solution.py:38
  130.4 0.7 copy-done.13
  131.1 7.4 %tail.1 = f32[512,512]{1,0:T(8,128)} custom-call(f32[4,160,128]{2,1,0:T(8,128)} %copy-done.6, f32[4,160,128]{2,1,0:T(8,128)} %copy-done.13, bf16[2,512,512]{2,1,0:T(8,128)(2,1)} %get-tuple-element.52.step_n, bf16[2,512,512]{2,1,0:T(8,128)(2,1)} %get-tuple-element.53.step_t, bf16[2,512,512]{2,1,0:T(8,128)(2,1)} %get-tuple-element.54.low_t, f32[512,512]{1,0:T(8,128)} %dg_ref.1), custom_call_target="tpu_custom_call" | custom-call | flops 8000000000 | bytes 5000000 | tf_op jit(solution)/shard_map/tail/pallas_call | solution.py:377
  138.6 1.3 collective-permute-done.27.d_ref
  139.9 0.7 copy-done.12
  140.7 3.1 %solve.1 = f32[192,512]{1,0:T(8,128)} custom-call(f32[192,512]{1,0:T(8,128)} %get-tuple-element.55.r_ref, f32[192,512]{1,0:T(8,128)} %copy-done.12, f32[192,512]{1,0:T(8,128)} %copy-done.11, bf16[2,512,512]{2,1,0:T(8,128)(2,1)} %get-tuple-element.52.step_n), custom_call_target="tpu_custom_call" | custom-call | flops 1000000000 | bytes 3000000 | tf_op jit(solution)/shard_map/solve/pallas_call | solution.py:399
  (62 shorter events, 1.8 us)
Async XLA Ops:
  0.6 10.1 %copy-start.2 = (bf16[192,512]{1,0:T(8,128)(2,1)S(1)}, bf16[192,512]{1,0:T(8,128)(2,1)}, u32[]{:S(2)}) copy-start(bf16[192,512]{1,0:T(8,128)(2,1)} %p_ref.1) | copy-start | bytes 589828
  0.6 10.1 %collective-permute-start.1 = (bf16[192,512]{1,0:T(8,128)(2,1)}, bf16[192,512]{1,0:T(8,128)(2,1)S(1)}, u32[]{:S(2)}, u32[]{:S(2)}) collective-permute-start(bf16[192,512]{1,0:T(8,128)(2,1)} %p_ref.1), channel_id=1, source_target_pairs={{0,64},{64,0},{1,65},{65,1},{2,66},{66,2},{3,67},{67,3},{4,68},{68... | collective-permute-start | bytes 589832 | tf_op jit(solution)/shard_map/ppermute | solution.py:38
  10.8 34.5 %copy-start.4 = (bf16[2,192,512]{2,1,0:T(8,128)(2,1)}, bf16[2,192,512]{2,1,0:T(8,128)(2,1)S(1)}, u32[]{:S(2)}) copy-start(bf16[2,192,512]{2,1,0:T(8,128)(2,1)S(1)} %pad_maximum_fusion.1.x_two) | copy-start | bytes 1179652
  10.8 12.3 %collective-permute-start.7 = (bf16[2,192,512]{2,1,0:T(8,128)(2,1)S(1)}, bf16[2,192,512]{2,1,0:T(8,128)(2,1)S(1)}, u32[]{:S(2)}, u32[]{:S(2)}) collective-permute-start(bf16[2,192,512]{2,1,0:T(8,128)(2,1)S(1)} %pad_maximum_fusion.1.x_two), channel_id=1, source_target_pairs={{0,16},{16,32},{32,48},{48,0},{1,17},{17,33},{33,49},{49,1},{2,18}... | collective-permute-start | bytes 1179656 | tf_op jit(solution)/shard_map/ppermute | solution.py:38
  12.4 6.1 %collective-permute-start = (bf16[192,512]{1,0:T(8,128)(2,1)S(1)}, bf16[192,512]{1,0:T(8,128)(2,1)S(1)}, u32[]{:S(2)}, u32[]{:S(2)}) collective-permute-start(bf16[192,512]{1,0:T(8,128)(2,1)S(1)} %copy-done.2), channel_id=1, source_target_pairs={{0,8},{8,0},{1,9},{9,1},{2,10},{10,2},{3,11},{11,3},{4,12},{12,4},... | collective-permute-start | bytes 589832 | tf_op jit(solution)/shard_map/ppermute | solution.py:38
  13.7 12.1 %collective-permute-start.6 = (bf16[2,192,512]{2,1,0:T(8,128)(2,1)S(1)}, bf16[2,192,512]{2,1,0:T(8,128)(2,1)S(1)}, u32[]{:S(2)}, u32[]{:S(2)}) collective-permute-start(bf16[2,192,512]{2,1,0:T(8,128)(2,1)S(1)} %pad_maximum_fusion.1.x_two), channel_id=1, source_target_pairs={{0,48},{16,0},{32,16},{48,32},{1,49},{17,1},{33,17},{49,33},{2,50}... | collective-permute-start | bytes 1179656 | tf_op jit(solution)/shard_map/ppermute | solution.py:38
  15.5 16.6 %collective-permute-start.5 = (bf16[2,192,512]{2,1,0:T(8,128)(2,1)S(1)}, bf16[2,192,512]{2,1,0:T(8,128)(2,1)S(1)}, u32[]{:S(2)}, u32[]{:S(2)}) collective-permute-start(bf16[2,192,512]{2,1,0:T(8,128)(2,1)S(1)} %pad_maximum_fusion.1.x_two), channel_id=1, source_target_pairs={{0,32},{16,48},{32,0},{48,16},{1,33},{17,49},{33,1},{49,17},{2,34}... | collective-permute-start | bytes 1179656 | tf_op jit(solution)/shard_map/ppermute | solution.py:38
  18.5 19.4 %collective-permute-start.3 = (bf16[2,192,512]{2,1,0:T(8,128)(2,1)S(1)}, bf16[2,192,512]{2,1,0:T(8,128)(2,1)S(1)}, u32[]{:S(2)}, u32[]{:S(2)}) collective-permute-start(bf16[2,192,512]{2,1,0:T(8,128)(2,1)S(1)} %get-tuple-element.66), channel_id=1, source_target_pairs={{0,6},{2,0},{4,2},{6,4},{1,7},{3,1},{5,3},{7,5},{8,14},{10,8},{12,... | collective-permute-start | bytes 1179656 | tf_op jit(solution)/shard_map/ppermute | solution.py:38
  22.6 15.3 %collective-permute-start.2 = (bf16[2,192,512]{2,1,0:T(8,128)(2,1)S(1)}, bf16[2,192,512]{2,1,0:T(8,128)(2,1)S(1)}, u32[]{:S(2)}, u32[]{:S(2)}) collective-permute-start(bf16[2,192,512]{2,1,0:T(8,128)(2,1)S(1)} %get-tuple-element.66), channel_id=1, source_target_pairs={{0,4},{2,6},{4,0},{6,2},{1,5},{3,7},{5,1},{7,3},{8,12},{10,14},{12... | collective-permute-start | bytes 1179656 | tf_op jit(solution)/shard_map/ppermute | solution.py:38
  23.2 22.2 %copy-start.8 = (bf16[2,192,512]{2,1,0:T(8,128)(2,1)}, bf16[2,192,512]{2,1,0:T(8,128)(2,1)S(1)}, u32[]{:S(2)}) copy-start(bf16[2,192,512]{2,1,0:T(8,128)(2,1)S(1)} %collective-permute-done.7.r1) | copy-start | bytes 1179652
  23.2 18.5 %collective-permute-start.4 = (bf16[2,192,512]{2,1,0:T(8,128)(2,1)S(1)}, bf16[2,192,512]{2,1,0:T(8,128)(2,1)S(1)}, u32[]{:S(2)}, u32[]{:S(2)}) collective-permute-start(bf16[2,192,512]{2,1,0:T(8,128)(2,1)S(1)} %get-tuple-element.66), channel_id=1, source_target_pairs={{0,2},{2,4},{4,6},{6,0},{1,3},{3,5},{5,7},{7,1},{8,10},{10,12},{12... | collective-permute-start | bytes 1179656 | tf_op jit(solution)/shard_map/ppermute | solution.py:38
  25.8 15.9 %copy-start.9 = (bf16[2,192,512]{2,1,0:T(8,128)(2,1)}, bf16[2,192,512]{2,1,0:T(8,128)(2,1)S(1)}, u32[]{:S(2)}) copy-start(bf16[2,192,512]{2,1,0:T(8,128)(2,1)S(1)} %collective-permute-done.6.r3) | copy-start | bytes 1179652
  32.1 9.6 %copy-start.10 = (bf16[2,192,512]{2,1,0:T(8,128)(2,1)}, bf16[2,192,512]{2,1,0:T(8,128)(2,1)S(1)}, u32[]{:S(2)}) copy-start(bf16[2,192,512]{2,1,0:T(8,128)(2,1)S(1)} %collective-permute-done.5.r2) | copy-start | bytes 1179652
  41.8 3.5 %copy-start.1 = (bf16[4,2,192,512]{3,2,1,0:T(8,128)(2,1)}, bf16[4,2,192,512]{3,2,1,0:T(8,128)(2,1)S(1)}, u32[]{:S(2)}) copy-start(bf16[4,2,192,512]{3,2,1,0:T(8,128)(2,1)S(1)} %pad_maximum_fusion.z_all) | copy-start | bytes 4718596
  41.9 3.5 %collective-permute-start.8 = (bf16[4,2,192,512]{3,2,1,0:T(8,128)(2,1)S(1)}, bf16[4,2,192,512]{3,2,1,0:T(8,128)(2,1)S(1)}, u32[]{:S(2)}, u32[]{:S(2)}) collective-permute-start(bf16[4,2,192,512]{3,2,1,0:T(8,128)(2,1)S(1)} %pad_maximum_fusion.z_all), channel_id=1, source_target_pairs={{0,1},{1,0},{2,3},{3,2},{4,5},{5,4},{6,7},{7,6},{8,9},{9,8},{10,11... | collective-permute-start | bytes 4718600 | tf_op jit(solution)/shard_map/ppermute | solution.py:38
  45.3 1.2 copy-start.7
  58.6 2.0 %copy-start.14 = (f32[4,160,128]{2,1,0:T(8,128)S(1)}, f32[4,160,128]{2,1,0:T(8,128)}, u32[]{:S(2)}) copy-start(f32[4,160,128]{2,1,0:T(8,128)} %get-tuple-element.42) | copy-start | bytes 983044
  58.6 3.7 %copy-start.5 = (f32[4,160,128]{2,1,0:T(8,128)S(1)}, f32[4,160,128]{2,1,0:T(8,128)}, u32[]{:S(2)}) copy-start(f32[4,160,128]{2,1,0:T(8,128)} %get-tuple-element.40) | copy-start | bytes 983044
  60.6 1.7 %collective-permute-start.12 = (f32[4,160,128]{2,1,0:T(8,128)S(1)}, f32[4,160,128]{2,1,0:T(8,128)S(1)}, u32[]{:S(2)}, u32[]{:S(2)}) collective-permute-start(f32[4,160,128]{2,1,0:T(8,128)S(1)} %copy-done.14), channel_id=1, source_target_pairs={{0,1},{1,0},{2,3},{3,2},{4,5},{5,4},{6,7},{7,6},{8,9},{9,8},{10,11... | collective-permute-start | bytes 983048 | tf_op jit(solution)/shard_map/ppermute | solution.py:38
  62.3 6.3 %collective-permute-start.13 = (f32[2,160,128]{2,1,0:T(8,128)S(1)}, f32[2,160,128]{2,1,0:T(8,128)S(1)}, u32[]{:S(2)}, u32[]{:S(2)}) collective-permute-start(f32[2,160,128]{2,1,0:T(8,128)S(1)} %slice_add_fusion.1), channel_id=1, source_target_pairs={{0,8},{8,0},{64,72},{72,64},{1,9},{9,1},{65,73},{73,65},{2,10},{10... | collective-permute-start | bytes 491528 | tf_op jit(solution)/shard_map/ppermute | solution.py:46
  63.8 12.1 %collective-permute-start.11 = (f16[2,192,512]{2,1,0:T(8,128)(2,1)S(1)}, f16[2,192,512]{2,1,0:T(8,128)(2,1)S(1)}, u32[]{:S(2)}, u32[]{:S(2)}) collective-permute-start(f16[2,192,512]{2,1,0:T(8,128)(2,1)S(1)} %get-tuple-element.60), channel_id=1, source_target_pairs={{0,16},{16,32},{32,48},{48,0},{1,17},{17,33},{33,49},{49,1},{2,18}... | collective-permute-start | bytes 1179656 | tf_op jit(solution)/shard_map/ppermute | solution.py:38
  65.2 10.6 %collective-permute-start.10 = (f16[2,192,512]{2,1,0:T(8,128)(2,1)S(1)}, f16[2,192,512]{2,1,0:T(8,128)(2,1)S(1)}, u32[]{:S(2)}, u32[]{:S(2)}) collective-permute-start(f16[2,192,512]{2,1,0:T(8,128)(2,1)S(1)} %get-tuple-element.61), channel_id=1, source_target_pairs={{0,48},{16,0},{32,16},{48,32},{1,49},{17,1},{33,17},{49,33},{2,50}... | collective-permute-start | bytes 1179656 | tf_op jit(solution)/shard_map/ppermute | solution.py:38
  68.7 4.5 %collective-permute-start.14 = (f32[160,128]{1,0:T(8,128)S(1)}, f32[160,128]{1,0:T(8,128)S(1)}, u32[]{:S(2)}, u32[]{:S(2)}) collective-permute-start(f32[160,128]{1,0:T(8,128)S(1)} %slice_bitcast_fusion.4), channel_id=1, source_target_pairs={{0,72},{8,64},{64,8},{72,0},{1,73},{9,65},{65,9},{73,1},{2,74},{10... | collective-permute-start | bytes 245768 | tf_op jit(solution)/shard_map/ppermute | solution.py:46
  86.2 14.5 %copy-start = (f32[4,2,192,512]{3,2,1,0:T(8,128)S(1)}, f32[4,2,192,512]{3,2,1,0:T(8,128)}, u32[]{:S(2)}) copy-start(f32[4,2,192,512]{3,2,1,0:T(8,128)} %get-tuple-element.44) | copy-start | bytes 9437188
  86.2 14.5 %collective-permute-start.15 = (f32[4,2,192,512]{3,2,1,0:T(8,128)}, f32[4,2,192,512]{3,2,1,0:T(8,128)S(1)}, u32[]{:S(2)}, u32[]{:S(2)}) collective-permute-start(f32[4,2,192,512]{3,2,1,0:T(8,128)} %get-tuple-element.45), channel_id=1, source_target_pairs={{0,1},{1,0},{2,3},{3,2},{4,5},{5,4},{6,7},{7,6},{8,9},{9,8},{10,11... | collective-permute-start | bytes 9437192 | tf_op jit(solution)/shard_map/ppermute | solution.py:38
  86.3 13.0 %collective-permute-start.9 = (f16[2,192,512]{2,1,0:T(8,128)(2,1)S(1)}, f16[2,192,512]{2,1,0:T(8,128)(2,1)S(1)}, u32[]{:S(2)}, u32[]{:S(2)}) collective-permute-start(f16[2,192,512]{2,1,0:T(8,128)(2,1)S(1)} %get-tuple-element.62), channel_id=1, source_target_pairs={{0,32},{16,48},{32,0},{48,16},{1,33},{17,49},{33,1},{49,17},{2,34}... | collective-permute-start | bytes 1179656 | tf_op jit(solution)/shard_map/ppermute | solution.py:38
  88.1 4.5 %collective-permute-start.16 = (f32[160,128]{1,0:T(8,128)S(1)}, f32[160,128]{1,0:T(8,128)S(1)}, u32[]{:S(2)}, u32[]{:S(2)}) collective-permute-start(f32[160,128]{1,0:T(8,128)S(1)} %fusion.11), channel_id=1, source_target_pairs={{0,2},{2,0},{4,6},{6,4},{1,3},{3,1},{5,7},{7,5},{8,10},{10,8},{12,... | collective-permute-start | bytes 245768 | tf_op jit(solution)/shard_map/ppermute | solution.py:46
  92.6 8.1 %collective-permute-start.17 = (f32[160,128]{1,0:T(8,128)S(1)}, f32[160,128]{1,0:T(8,128)S(1)}, u32[]{:S(2)}, u32[]{:S(2)}) collective-permute-start(f32[160,128]{1,0:T(8,128)S(1)} %add.88), channel_id=1, source_target_pairs={{0,6},{2,4},{4,2},{6,0},{1,7},{3,5},{5,3},{7,1},{8,14},{10,12},{12... | collective-permute-start | bytes 245768 | tf_op jit(solution)/shard_map/ppermute | solution.py:46
  100.7 26.3 %copy-start.3 = (f32[192,512]{1,0:T(8,128)S(1)}, f32[192,512]{1,0:T(8,128)}, u32[]{:S(2)}) copy-start(f32[192,512]{1,0:T(8,128)} %pg_ref.1) | copy-start | bytes 1179652
  101.6 13.9 %collective-permute-start.20 = (f16[2,192,512]{2,1,0:T(8,128)(2,1)S(1)}, f16[2,192,512]{2,1,0:T(8,128)(2,1)S(1)}, u32[]{:S(2)}, u32[]{:S(2)}) collective-permute-start(f16[2,192,512]{2,1,0:T(8,128)(2,1)S(1)} %get-tuple-element.57), channel_id=1, source_target_pairs={{0,2},{2,4},{4,6},{6,0},{1,3},{3,5},{5,7},{7,1},{8,10},{10,12},{12... | collective-permute-start | bytes 1179656 | tf_op jit(solution)/shard_map/ppermute | solution.py:38
  101.7 13.9 %collective-permute-start.19 = (f16[2,192,512]{2,1,0:T(8,128)(2,1)S(1)}, f16[2,192,512]{2,1,0:T(8,128)(2,1)S(1)}, u32[]{:S(2)}, u32[]{:S(2)}) collective-permute-start(f16[2,192,512]{2,1,0:T(8,128)(2,1)S(1)} %get-tuple-element.58), channel_id=1, source_target_pairs={{0,6},{2,0},{4,2},{6,4},{1,7},{3,1},{5,3},{7,5},{8,14},{10,8},{12,... | collective-permute-start | bytes 1179656 | tf_op jit(solution)/shard_map/ppermute | solution.py:38
  104.9 15.2 %collective-permute-start.24 = (f32[192,512]{1,0:T(8,128)S(1)}, f32[192,512]{1,0:T(8,128)S(1)}, u32[]{:S(2)}, u32[]{:S(2)}) collective-permute-start(f32[192,512]{1,0:T(8,128)S(1)} %slice_bitcast_fusion.1), channel_id=1, source_target_pairs={{0,64},{64,0},{1,65},{65,1},{2,66},{66,2},{3,67},{67,3},{4,68},{68... | collective-permute-start | bytes 1179656 | tf_op jit(solution)/shard_map/ppermute | solution.py:38
  105.3 4.4 %collective-permute-start.21 = (f32[160,128]{1,0:T(8,128)S(1)}, f32[160,128]{1,0:T(8,128)S(1)}, u32[]{:S(2)}, u32[]{:S(2)}) collective-permute-start(f32[160,128]{1,0:T(8,128)S(1)} %add.89), channel_id=1, source_target_pairs={{0,16},{16,0},{32,48},{48,32},{1,17},{17,1},{33,49},{49,33},{2,18}... | collective-permute-start | bytes 245768 | tf_op jit(solution)/shard_map/ppermute | solution.py:46
  109.8 5.7 %collective-permute-start.22 = (f32[160,128]{1,0:T(8,128)S(1)}, f32[160,128]{1,0:T(8,128)S(1)}, u32[]{:S(2)}, u32[]{:S(2)}) collective-permute-start(f32[160,128]{1,0:T(8,128)S(1)} %add.98), channel_id=1, source_target_pairs={{0,48},{16,32},{32,16},{48,0},{1,49},{17,33},{33,17},{49,1},{2,50}... | collective-permute-start | bytes 245768 | tf_op jit(solution)/shard_map/ppermute | solution.py:46
  115.5 4.5 %collective-permute-start.23 = (f32[160,128]{1,0:T(8,128)S(1)}, f32[160,128]{1,0:T(8,128)S(1)}, u32[]{:S(2)}, u32[]{:S(2)}) collective-permute-start(f32[160,128]{1,0:T(8,128)S(1)} %add.99), channel_id=1, source_target_pairs={{0,72},{8,64},{64,8},{72,0},{1,73},{9,65},{65,9},{73,1},{2,74},{10... | collective-permute-start | bytes 245768 | tf_op jit(solution)/shard_map/ppermute | solution.py:46
  117.4 9.6 %collective-permute-start.18 = (f16[2,192,512]{2,1,0:T(8,128)(2,1)S(1)}, f16[2,192,512]{2,1,0:T(8,128)(2,1)S(1)}, u32[]{:S(2)}, u32[]{:S(2)}) collective-permute-start(f16[2,192,512]{2,1,0:T(8,128)(2,1)S(1)} %get-tuple-element.56), channel_id=1, source_target_pairs={{0,4},{2,6},{4,0},{6,2},{1,5},{3,7},{5,1},{7,3},{8,12},{10,14},{12... | collective-permute-start | bytes 1179656 | tf_op jit(solution)/shard_map/ppermute | solution.py:38
  120.1 18.5 %copy-start.11 = (f32[192,512]{1,0:T(8,128)}, f32[192,512]{1,0:T(8,128)S(1)}, u32[]{:S(2)}) copy-start(f32[192,512]{1,0:T(8,128)S(1)} %collective-permute-done.24.t_ref) | copy-start | bytes 1179652
  120.1 6.8 %collective-permute-start.25 = (f32[2,160,128]{2,1,0:T(8,128)S(1)}, f32[2,160,128]{2,1,0:T(8,128)S(1)}, u32[]{:S(2)}, u32[]{:S(2)}) collective-permute-start(f32[2,160,128]{2,1,0:T(8,128)S(1)} %pad_maximum_fusion.3), channel_id=1, source_target_pairs={{0,8},{8,0},{64,72},{72,64},{1,9},{9,1},{65,73},{73,65},{2,10},{10... | collective-permute-start | bytes 491528 | tf_op jit(solution)/shard_map/ppermute | solution.py:46
  126.9 3.5 %copy-start.6 = (f32[4,160,128]{2,1,0:T(8,128)}, f32[4,160,128]{2,1,0:T(8,128)S(1)}, u32[]{:S(2)}) copy-start(f32[4,160,128]{2,1,0:T(8,128)S(1)} %constant_dynamic-update-slice_fusion.mine) | copy-start | bytes 983044
  126.9 3.5 %collective-permute-start.26 = (f32[4,160,128]{2,1,0:T(8,128)S(1)}, f32[4,160,128]{2,1,0:T(8,128)S(1)}, u32[]{:S(2)}, u32[]{:S(2)}) collective-permute-start(f32[4,160,128]{2,1,0:T(8,128)S(1)} %constant_dynamic-update-slice_fusion.mine), channel_id=1, source_target_pairs={{0,1},{1,0},{2,3},{3,2},{4,5},{5,4},{6,7},{7,6},{8,9},{9,8},{10,11... | collective-permute-start | bytes 983048 | tf_op jit(solution)/shard_map/ppermute | solution.py:38
  128.1 11.8 %collective-permute-start.27 = (f32[192,512]{1,0:T(8,128)S(1)}, f32[192,512]{1,0:T(8,128)S(1)}, u32[]{:S(2)}, u32[]{:S(2)}) collective-permute-start(f32[192,512]{1,0:T(8,128)S(1)} %get-tuple-element.63), channel_id=1, source_target_pairs={{0,8},{8,0},{1,9},{9,1},{2,10},{10,2},{3,11},{11,3},{4,12},{12,4},... | collective-permute-start | bytes 1179656 | tf_op jit(solution)/shard_map/ppermute | solution.py:38
  130.4 0.7 copy-start.13
  139.9 0.7 copy-start.12
